TPU v7x, 32 devices: a whole 2x2x4 slice. The times are simulated.
32 devices in a mesh: seg: 2 (over y), rows: 8 (over z, x), cam: 2 (over core).
Axes of the slice: x: 2, y: 2, z: 4, core: 2. Of those that a mesh axis runs over, the one named last changes fastest.
Arguments:
- features: bfloat16 [4, 128, 32, 128], P(('seg', 'cam'), None, 'rows'), parts along dimension 0, may hold values from -6 to 6
- partner: int32 [2], replicated, may hold values from 0 to 1, as said below
- pattern: int32 [64, 6], P(('seg', 'rows')), parts along dimension 0, may hold values from 0 to 1, as said below
- valid: int32 [4, 32, 4], P(('seg', 'cam'), 'rows'), parts along dimension 0, may hold values 0 or 1
- carried: bfloat16 [4, 16, 96, 32, 128], P(('seg', 'cam'), None, None, 'rows'), parts along dimension 0, may hold values from -6 to 6
- w_first: bfloat16 [27, 16], replicated, may hold values from -1.25 to 1.25
- w_second: bfloat16 [27, 16, 16], replicated, may hold values from -0.3125 to 0.3125
- w_third: bfloat16 [27, 16, 16], replicated, may hold values from -0.3125 to 0.3125
- w_last: bfloat16 [27, 16], replicated, may hold values from -0.3125 to 0.3125
Outputs:
- aggregated: float32 [4, 96, 32, 128], P(('seg', 'cam'), None, 'rows'), parts along dimension 0
There are 2 independent parts, one for each index of `seg`. A program takes and returns all parts, laid end to end along the dimension named above; an argument that names none is the same for every part. Nothing has to cross between parts.
Inputs may be any that keep to these rules, and one draw needn't show every extreme that they name: partner is its own inverse; cameras 0 to 0 pair with cameras 1 to 1. `pattern`: in every row the live tiles (ones) form one run of consecutive tiles, at least one.
All inputs are finite; a program needn't handle non-finite values. No bound on the sum of `valid` on one device may be relied on, other than what follows from the above.
Results may differ from a plain program's by a relative error of at most 0.0037.
Values may be sent and summed in bfloat16 or wider, within the bound.
No kernel may reach another device: no remote copies, remote signals or barrier semaphores. Data moves between devices by JAX's collectives and lax.ppermute only.
A program may use at most 128 MiB of HBM per device.

v0:
```python
import jax
import jax.numpy as jnp
from jax import lax
from jax.sharding import PartitionSpec as P

DTILE = 16
BLOCK_COLS = 32


def from_partner(value, axis, bit):
    mask = 2**bit
    pairs = [(source, source ^ mask) for source in range(lax.axis_size(axis))]
    return lax.ppermute(value, axis, pairs)


def padded(block, sides, width):
    for axis, dim in sides:
        count = lax.axis_size(axis)
        forward = [(i, i + 1) for i in range(count - 1)]
        backward = [(target, source) for source, target in forward]
        low = lax.ppermute(
            lax.slice_in_dim(block, block.shape[dim] - width, None, axis=dim), axis, forward
        )
        high = lax.ppermute(lax.slice_in_dim(block, 0, width, axis=dim), axis, backward)
        block = jnp.concatenate([low, block, high], axis=dim)
    return block


def conv_taps(volume, kernel):
    outs, ins = (kernel.shape[1], kernel.shape[2])
    weights = kernel.reshape(3, 3, 3, outs, ins).transpose(3, 4, 0, 1, 2)
    return lax.conv_general_dilated(
        volume,
        weights,
        (1, 1, 1),
        ((1, 1), (0, 0), (1, 1)),
        dimension_numbers=("NCDHW", "OIDHW", "NCDHW"),
        preferred_element_type=jnp.float32,
    )


def correlate(own_raw, mate_raw, right, pattern_rows, valid_rows, disp):
    cam_dev, channels, rows_here, width = own_raw.shape
    own = jnp.where(right, own_raw[..., ::-1], own_raw)
    mate_feat = jnp.where(right, mate_raw[..., ::-1], mate_raw)
    scores = jnp.einsum("icrw,icrv->irwv", own, mate_feat, preferred_element_type=jnp.float32)
    shifted = jnp.pad(scores, ((0, 0), (0, 0), (0, 0), (disp, 0)))
    flat = shifted.reshape(cam_dev, rows_here, width * (width + disp))
    flat = jnp.pad(flat, ((0, 0), (0, 0), (0, width)))
    skewed = flat.reshape(cam_dev, rows_here, width, width + disp + 1)
    band = skewed[..., 1 : disp + 1][..., ::-1]
    corr = band.transpose(0, 3, 1, 2) / jnp.sqrt(jnp.float32(channels))
    corr = jnp.where(right, corr[..., ::-1], corr)
    tiles = jnp.repeat(pattern_rows, DTILE, axis=1).T.astype(jnp.float32)
    pixels = jnp.repeat(valid_rows, BLOCK_COLS, axis=2).astype(jnp.float32)
    return (corr * tiles[None, :, :, None] * pixels[:, None, :, :]).astype(jnp.bfloat16)


def local(features, partner, pattern, valid, carried, w_first, w_second, w_third, w_last):
    cam_dev, channels, rows_dev, width = features.shape
    disp = carried.shape[2]
    mine = lax.axis_index("cam") * cam_dev + jnp.arange(cam_dev, dtype=jnp.int32)
    others = from_partner(features, "cam", 0)
    cameras = partner.shape[0]
    picked = jnp.arange(cameras, dtype=jnp.int32)[None, :] == mine[:, None]
    mates = jnp.sum(jnp.where(picked, partner[None, :], 0), axis=1)
    slots = mates - (1 - lax.axis_index("cam")) * cam_dev
    chosen = slots[:, None] == jnp.arange(cam_dev, dtype=jnp.int32)[None, :]
    right = (mates < mine)[:, None, None, None]
    first_kernel = w_first[:, :, None]
    last_kernel = w_last[:, None, :]
    corr = correlate(
        features,
        jnp.sum(
            jnp.where(chosen[:, :, None, None, None], others[None], jnp.zeros((), jnp.bfloat16)),
            axis=1,
        ),
        right,
        pattern,
        valid,
        disp,
    )
    volume = corr[:, None]

    def one_layer(source, kernel):
        extended = padded(source, (("rows", 3),), 1)
        return conv_taps(extended, kernel)

    h1 = jax.nn.relu(one_layer(volume, first_kernel)).astype(jnp.bfloat16)
    h2 = jax.nn.relu(one_layer(h1, w_second) + carried.astype(jnp.float32)).astype(jnp.bfloat16)
    h3 = jax.nn.relu(one_layer(h2, w_third)).astype(jnp.bfloat16)
    final = one_layer(h3, last_kernel)
    return corr.astype(jnp.float32) + final[:, 0]


def solution(mesh):
    return jax.shard_map(
        local,
        mesh=mesh,
        in_specs=(
            P(("seg", "cam"), None, "rows", None),
            P(),
            P(("seg", "rows"), None),
            P(("seg", "cam"), "rows", None),
            P(("seg", "cam"), None, None, "rows", None),
            P(),
            P(),
            P(),
            P(),
        ),
        out_specs=P(("seg", "cam"), None, "rows", None),
        check_vma=False,
    )
```

profile of v0, /device:TPU:0, one launch (start us, length us, event | category | flops | bytes accessed | tf_op | source)
XLA Modules:
  0.0 402.4 jit_solution(9291901865620313710)
XLA Ops:
  0.0 0.5 collective-permute-start
  0.5 1.2 rev.12
  1.6 1.3 fusion.44
  4.2 0.7 convert_element_type.56
  5.1 0.7 convert_bitcast_fusion
  5.9 1.0 select_bitcast_fusion.1
  7.0 0.3 rev.13
  7.4 0.2 convolution_bitcast_fusion
  7.6 0.2 pad.8.clone
  7.8 0.5 reshape.76
  8.4 0.6 reshape.77
  9.1 0.4 rev.14
  9.8 4.4 %collective-permute-start.1 = (bf16[1,1,96,1,128]{2,4,3,1,0:T(8,128)(2,1)S(1)}, bf16[1,1,96,1,128]{2,4,3,1,0:T(8,128)(2,1)S(1)}, u32[]{:S(2)}, u32[]{:S(2)}) collective-permute-start(bf16[1,1,96,1,128]{2,4,3,1,0:T(8,128)(2,1)S(1)} %get-tuple-element.11), channel_id=1, source_target_pairs={{0,2},{2,4},{4,6},{6,8},{8,10},{10,12},{12,14},{1,3},{3,5},{5,7},{... | collective-permute-start | bytes 73736 | tf_op jit(solution)/shard_map/ppermute | solution.py:21
  14.2 1.3 collective-permute-start.2
  15.6 0.1 collective-permute-done.1
  15.8 4.2 %collective-permute-done.2 = bf16[1,1,96,1,128]{2,4,3,1,0:T(8,128)(2,1)S(1)} collective-permute-done((bf16[1,1,96,1,128]{2,4,3,1,0:T(8,128)(2,1)S(1)}, bf16[1,1,96,1,128]{2,4,3,1,0:T(8,128)(2,1)S(1)}, u32[]{:S(2)}, u32[]{:S(2)}) %collective-permute-start.2) | collective-permute-done | bytes 24608 | tf_op jit(solution)/shard_map/ppermute | solution.py:24
  20.4 10.2 %copy.109 = bf16[1,96,6,8,19]{3,0,4,2,1:T(2,128)(2,1)} copy(bf16[1,96,6,8,19]{1,4,3,2,0:T(8,128)(2,1)S(1)} %fusion.40) | data formatting | bytes 350208 | tf_op jit(solution)/shard_map/conv_general_dilated | solution.py:32
  30.6 44.4 %maximum_convert_fusion.1 = bf16[96,4,8,17,16]{4,2,3,1,0:T(8,128)(2,1)S(1)} fusion(bf16[1,96,6,8,19]{3,0,4,2,1:T(2,128)(2,1)} %copy.109, bf16[3,3,3,16,1]{3,4,2,1,0:T(2,128)(2,1)S(1)} %reshape_broadcast_in_dim.8, pred[8,17]{0,1:T(8,128)(4,1)S(1)} %copy-done.8), kind=kOutput, calls=%fused_computation.5 | convolution fusion | flops 47314944 | bytes 1847272 | tf_op jit(solution)/shard_map/conv_general_dilated | solution.py:32
  75.0 4.8 %copy-done.1 = bf16[96,4,8,17,16]{4,2,3,1,0:T(8,128)(2,1)} copy-done((bf16[96,4,8,17,16]{4,2,3,1,0:T(8,128)(2,1)}, bf16[96,4,8,17,16]{4,2,3,1,0:T(8,128)(2,1)S(1)}, u32[]{:S(2)}) %copy-start.1) | copy-done | bytes 1671192
  79.8 2.8 fusion.55
  82.6 5.3 %copy.111 = bf16[96,1,8,17,16]{0,4,3,2,1:T(8,128)(2,1)} copy(bf16[96,1,8,17,16]{4,2,3,1,0:T(8,128)(2,1)} %get-tuple-element.7) | data formatting | bytes 835584 | tf_op jit(solution)/shard_map/convert_element_type | solution.py:89
  88.0 1.9 slice_bitcast_fusion.6
  89.8 5.2 %collective-permute-start.3 = (bf16[1,16,96,1,128]{2,1,4,0,3:T(8,128)(2,1)}, bf16[1,16,96,1,128]{2,1,4,0,3:T(8,128)(2,1)}, u32[]{:S(2)}, u32[]{:S(2)}) collective-permute-start(bf16[1,16,96,1,128]{2,1,4,0,3:T(8,128)(2,1)} %slice_bitcast_fusion.6), channel_id=1, source_target_pairs={{0,2},{2,4},{4,6},{6,8},{8,10},{10,12},{12,14},{1,3},{3,5},{5,7},{... | collective-permute-start | bytes 1179656 | tf_op jit(solution)/shard_map/ppermute | solution.py:21
  95.0 3.9 copy.113
  98.9 1.1 slice_bitcast_fusion.5
  100.0 1.3 collective-permute-start.4
  101.3 0.2 copy.116
  101.5 3.6 copy.118
  105.1 14.3 %copy.112 = bf16[96,4,8,17,16]{0,4,3,2,1:T(8,128)(2,1)S(1)} copy(bf16[96,4,8,17,16]{4,2,3,1,0:T(8,128)(2,1)} %copy-done.1) | data formatting | bytes 3342336 | tf_op jit(solution)/shard_map/convert_element_type | solution.py:89
  119.4 0.4 slice_bitcast_fusion.2
  119.8 1.8 maximum_bitcast_fusion
  121.6 0.6 pad.12
  122.2 17.2 %copy.115 = bf16[16,96,6,1,8,17]{0,4,5,2,1,3:T(8,128)(2,1)} copy(bf16[16,96,6,1,8,17]{1,0,5,4,2,3:T(8,128)(2,1)S(1)} %bitcast.97) | data formatting | bytes 5013504 | tf_op jit(solution)/shard_map/conv_general_dilated | solution.py:32
  139.4 2.3 slice.61
  141.7 37.6 %fusion.27 = f32[96,4,8,17,16]{4,2,3,1,0:T(8,128)} fusion(bf16[3,3,3,16,16]{4,3,2,1,0:T(8,128)(2,1)S(1)} %bitcast.109, bf16[16,96,6,1,7,2]{0,4,5,2,1,3:T(8,128)(2,1)S(1)} %slice.61, bf16[16,96,6,1,8,17]{0,4,5,2,1,3:T(8,128)(2,1)} %copy.115, pred[8,17]{0,1:T(8,128)(4,1)S(1)} %copy-done.8), kind=kOutput, calls=%fused_computation.25 | convolution fusion | flops 726171648 | bytes 6121096 | tf_op jit(solution)/shard_map/conv_general_dilated | solution.py:32
  179.3 17.9 %copy.117 = f32[96,4,8,17,16]{0,4,3,2,1:T(8,128)} copy(f32[96,4,8,17,16]{4,2,3,1,0:T(8,128)} %fusion.27) | data formatting | bytes 6684672 | tf_op jit(solution)/shard_map/conv_general_dilated | solution.py:32
  197.2 3.4 fusion.37
  200.6 1.2 fusion.56
  201.8 4.6 %collective-permute-start.5 = (bf16[1,16,96,1,128]{2,1,4,0,3:T(8,128)(2,1)}, bf16[1,16,96,1,128]{2,1,4,0,3:T(8,128)(2,1)S(1)}, u32[]{:S(2)}, u32[]{:S(2)}) collective-permute-start(bf16[1,16,96,1,128]{2,1,4,0,3:T(8,128)(2,1)} %get-tuple-element.9), channel_id=1, source_target_pairs={{0,2},{2,4},{4,6},{6,8},{8,10},{10,12},{12,14},{1,3},{3,5},{5,7},{... | collective-permute-start | bytes 1179656 | tf_op jit(solution)/shard_map/ppermute | solution.py:21
  206.3 1.3 collective-permute-start.6
  207.7 0.2 copy.121
  207.8 19.0 %collective-permute-done.5 = bf16[1,16,96,1,128]{2,1,4,0,3:T(8,128)(2,1)S(1)} collective-permute-done((bf16[1,16,96,1,128]{2,1,4,0,3:T(8,128)(2,1)}, bf16[1,16,96,1,128]{2,1,4,0,3:T(8,128)(2,1)S(1)}, u32[]{:S(2)}, u32[]{:S(2)}) %collective-permute-start.5) | collective-permute-done | bytes 393248 | tf_op jit(solution)/shard_map/ppermute | solution.py:21
  226.8 0.7 maximum_bitcast_fusion.1
  227.5 0.6 pad.14
  228.2 17.3 %copy.120 = bf16[16,96,6,1,8,17]{0,4,5,2,1,3:T(8,128)(2,1)} copy(bf16[16,96,6,1,8,17]{1,0,5,4,2,3:T(8,128)(2,1)S(1)} %bitcast.98) | data formatting | bytes 5013504 | tf_op jit(solution)/shard_map/conv_general_dilated | solution.py:32
  245.5 2.3 slice.65
  247.8 34.6 %maximum_convert_fusion = bf16[96,4,8,17,16]{4,2,3,1,0:T(8,128)(2,1)S(1)} fusion(bf16[3,3,3,16,16]{4,3,2,1,0:T(8,128)(2,1)S(1)} %bitcast.110, bf16[16,96,6,1,7,2]{0,4,5,2,1,3:T(8,128)(2,1)S(1)} %slice.65, bf16[16,96,6,1,8,17]{0,4,5,2,1,3:T(8,128)(2,1)} %copy.120, pred[8,17]{0,1:T(8,128)(4,1)S(1)} %copy-done.8), kind=kOutput, calls=%fused_computation.4 | convolution fusion | flops 727842816 | bytes 4449928 | tf_op jit(solution)/shard_map/conv_general_dilated | solution.py:32
  282.4 3.3 fusion.54
  285.7 2.5 copy-done
  288.2 4.9 %copy.122 = bf16[96,1,8,17,16]{0,4,3,2,1:T(8,128)(2,1)} copy(bf16[96,1,8,17,16]{4,2,3,1,0:T(8,128)(2,1)} %get-tuple-element.5) | data formatting | bytes 835584 | tf_op jit(solution)/shard_map/convert_element_type | solution.py:91
  293.1 1.9 slice_bitcast_fusion.4
  295.0 5.1 %collective-permute-start.7 = (bf16[1,16,96,1,128]{2,1,4,0,3:T(8,128)(2,1)}, bf16[1,16,96,1,128]{2,1,4,0,3:T(8,128)(2,1)}, u32[]{:S(2)}, u32[]{:S(2)}) collective-permute-start(bf16[1,16,96,1,128]{2,1,4,0,3:T(8,128)(2,1)} %slice_bitcast_fusion.4), channel_id=1, source_target_pairs={{0,2},{2,4},{4,6},{6,8},{8,10},{10,12},{12,14},{1,3},{3,5},{5,7},{... | collective-permute-start | bytes 1179656 | tf_op jit(solution)/shard_map/ppermute | solution.py:21
  300.1 4.1 %copy.124 = bf16[96,1,8,17,16]{0,4,3,2,1:T(8,128)(2,1)} copy(bf16[96,1,8,17,16]{4,2,3,1,0:T(8,128)(2,1)S(1)} %get-tuple-element.6) | data formatting | bytes 835584 | tf_op jit(solution)/shard_map/convert_element_type | solution.py:91
  304.2 1.1 slice_bitcast_fusion.3
  305.3 1.3 collective-permute-start.8
  306.7 14.3 %copy.123 = bf16[96,4,8,17,16]{0,4,3,2,1:T(8,128)(2,1)S(1)} copy(bf16[96,4,8,17,16]{4,2,3,1,0:T(8,128)(2,1)} %copy-done) | data formatting | bytes 3342336 | tf_op jit(solution)/shard_map/convert_element_type | solution.py:91
  321.0 0.4 slice_bitcast_fusion.1
  321.4 1.8 maximum_bitcast_fusion.2
  323.2 0.6 pad.16
  323.8 17.2 %copy.126 = bf16[16,96,6,1,8,17]{0,4,5,2,1,3:T(8,128)(2,1)} copy(bf16[16,96,6,1,8,17]{1,0,5,4,2,3:T(8,128)(2,1)S(1)} %bitcast.96) | data formatting | bytes 5013504 | tf_op jit(solution)/shard_map/conv_general_dilated | solution.py:32
  341.0 2.3 slice.71
  343.3 37.5 %fusion.24 = f32[96,4,8,17,1]{4,2,3,1,0:T(8,128)} fusion(bf16[3,3,3,1,16]{4,3,2,1,0:T(2,128)(2,1)S(1)} %reshape_broadcast_in_dim.9, bf16[16,96,6,1,7,2]{0,4,5,2,1,3:T(8,128)(2,1)S(1)} %slice.71, bf16[16,96,6,1,8,17]{0,4,5,2,1,3:T(8,128)(2,1)} %copy.126, pred[8,17]{0,1:T(8,128)(4,1)S(1)} %copy-done.8), kind=kOutput, calls=%fused_computation.24 | convolution fusion | flops 53265408 | bytes 2974696 | tf_op jit(solution)/shard_map/conv_general_dilated | solution.py:32
  380.9 20.4 %copy.129 = f32[96,4,8,17,1]{0,1,3,2,4:T(4,128)S(1)} copy(f32[96,4,8,17,1]{4,2,3,1,0:T(8,128)} %fusion.24) | data formatting | bytes 417792 | tf_op jit(solution)/shard_map/conv_general_dilated | solution.py:32
  401.4 0.8 copy.131
  (44 shorter events, 1.6 us)
Async XLA Ops:
  0.0 15.5 %copy-start.6 = (bf16[27,16]{0,1:T(8,128)(2,1)S(1)}, bf16[27,16]{0,1:T(8,128)(2,1)}, u32[]{:S(2)}) copy-start(bf16[27,16]{0,1:T(8,128)(2,1)} %param.14) | copy-start | bytes 2596
  0.0 6.9 %collective-permute-start = (bf16[1,128,4,128]{3,2,1,0:T(4,128)(2,1)}, bf16[1,128,4,128]{3,2,1,0:T(4,128)(2,1)S(1)}, u32[]{:S(2)}, u32[]{:S(2)}) collective-permute-start(bf16[1,128,4,128]{3,2,1,0:T(4,128)(2,1)} %param.9), channel_id=1, source_target_pairs={{0,1},{1,0},{2,3},{3,2},{4,5},{5,4},{6,7},{7,6},{8,9},{9,8},{10,11... | collective-permute-start | bytes 393224 | tf_op jit(solution)/shard_map/ppermute | solution.py:13
  7.8 22.8 %copy-start.8 = (pred[8,17]{0,1:T(8,128)(4,1)S(1)}, pred[8,17]{0,1:T(8,128)(4,1)}, u32[]{:S(2)}) copy-start(pred[8,17]{0,1:T(8,128)(4,1)} %constant.47) | copy-start | bytes 412
  9.8 20.8 %copy-start.2 = (bf16[1,96,4,128]{1,3,2,0:T(8,128)(2,1)}, bf16[1,96,4,128]{1,3,2,0:T(8,128)(2,1)S(1)}, u32[]{:S(2)}) copy-start(bf16[1,96,4,128]{1,3,2,0:T(8,128)(2,1)S(1)} %multiply_convert_fusion) | copy-start | bytes 294916
  9.8 6.0 %collective-permute-start.1 = (bf16[1,1,96,1,128]{2,4,3,1,0:T(8,128)(2,1)S(1)}, bf16[1,1,96,1,128]{2,4,3,1,0:T(8,128)(2,1)S(1)}, u32[]{:S(2)}, u32[]{:S(2)}) collective-permute-start(bf16[1,1,96,1,128]{2,4,3,1,0:T(8,128)(2,1)S(1)} %get-tuple-element.11), channel_id=1, source_target_pairs={{0,2},{2,4},{4,6},{6,8},{8,10},{10,12},{12,14},{1,3},{3,5},{5,7},{... | collective-permute-start | bytes 73736 | tf_op jit(solution)/shard_map/ppermute | solution.py:21
  14.2 5.8 %collective-permute-start.2 = (bf16[1,1,96,1,128]{2,4,3,1,0:T(8,128)(2,1)S(1)}, bf16[1,1,96,1,128]{2,4,3,1,0:T(8,128)(2,1)S(1)}, u32[]{:S(2)}, u32[]{:S(2)}) collective-permute-start(bf16[1,1,96,1,128]{2,4,3,1,0:T(8,128)(2,1)S(1)} %get-tuple-element.12), channel_id=1, source_target_pairs={{2,0},{4,2},{6,4},{8,6},{10,8},{12,10},{14,12},{3,1},{5,3},{7,5},{... | collective-permute-start | bytes 73736 | tf_op jit(solution)/shard_map/ppermute | solution.py:24
  75.0 4.8 %copy-start.1 = (bf16[96,4,8,17,16]{4,2,3,1,0:T(8,128)(2,1)}, bf16[96,4,8,17,16]{4,2,3,1,0:T(8,128)(2,1)S(1)}, u32[]{:S(2)}) copy-start(bf16[96,4,8,17,16]{4,2,3,1,0:T(8,128)(2,1)S(1)} %maximum_convert_fusion.1) | copy-start | bytes 5013508
  82.6 18.7 %copy-start.4 = (bf16[27,16,16]{0,2,1:T(8,128)(2,1)S(1)}, bf16[27,16,16]{0,2,1:T(8,128)(2,1)}, u32[]{:S(2)}) copy-start(bf16[27,16,16]{0,2,1:T(8,128)(2,1)} %param.15) | copy-start | bytes 41476
  89.8 29.9 %collective-permute-start.3 = (bf16[1,16,96,1,128]{2,1,4,0,3:T(8,128)(2,1)}, bf16[1,16,96,1,128]{2,1,4,0,3:T(8,128)(2,1)}, u32[]{:S(2)}, u32[]{:S(2)}) collective-permute-start(bf16[1,16,96,1,128]{2,1,4,0,3:T(8,128)(2,1)} %slice_bitcast_fusion.6), channel_id=1, source_target_pairs={{0,2},{2,4},{4,6},{6,8},{8,10},{10,12},{12,14},{1,3},{3,5},{5,7},{... | collective-permute-start | bytes 1179656 | tf_op jit(solution)/shard_map/ppermute | solution.py:21
  100.0 19.8 %collective-permute-start.4 = (bf16[1,16,96,1,128]{2,1,4,0,3:T(8,128)(2,1)S(1)}, bf16[1,16,96,1,128]{2,1,4,0,3:T(8,128)(2,1)S(1)}, u32[]{:S(2)}, u32[]{:S(2)}) collective-permute-start(bf16[1,16,96,1,128]{2,1,4,0,3:T(8,128)(2,1)S(1)} %slice_bitcast_fusion.5), channel_id=1, source_target_pairs={{2,0},{4,2},{6,4},{8,6},{10,8},{12,10},{14,12},{3,1},{5,3},{7,5},{... | collective-permute-start | bytes 1179656 | tf_op jit(solution)/shard_map/ppermute | solution.py:24
  197.2 10.5 %copy-start.5 = (bf16[27,16,16]{0,2,1:T(8,128)(2,1)S(1)}, bf16[27,16,16]{0,2,1:T(8,128)(2,1)}, u32[]{:S(2)}) copy-start(bf16[27,16,16]{0,2,1:T(8,128)(2,1)} %param.16) | copy-start | bytes 41476
  201.8 25.0 %collective-permute-start.5 = (bf16[1,16,96,1,128]{2,1,4,0,3:T(8,128)(2,1)}, bf16[1,16,96,1,128]{2,1,4,0,3:T(8,128)(2,1)S(1)}, u32[]{:S(2)}, u32[]{:S(2)}) collective-permute-start(bf16[1,16,96,1,128]{2,1,4,0,3:T(8,128)(2,1)} %get-tuple-element.9), channel_id=1, source_target_pairs={{0,2},{2,4},{4,6},{6,8},{8,10},{10,12},{12,14},{1,3},{3,5},{5,7},{... | collective-permute-start | bytes 1179656 | tf_op jit(solution)/shard_map/ppermute | solution.py:21
  206.3 20.5 %collective-permute-start.6 = (bf16[1,16,96,1,128]{2,1,4,0,3:T(8,128)(2,1)}, bf16[1,16,96,1,128]{2,1,4,0,3:T(8,128)(2,1)S(1)}, u32[]{:S(2)}, u32[]{:S(2)}) collective-permute-start(bf16[1,16,96,1,128]{2,1,4,0,3:T(8,128)(2,1)} %get-tuple-element.10), channel_id=1, source_target_pairs={{2,0},{4,2},{6,4},{8,6},{10,8},{12,10},{14,12},{3,1},{5,3},{7,5},{... | collective-permute-start | bytes 1179656 | tf_op jit(solution)/shard_map/ppermute | solution.py:24
  282.4 5.8 %copy-start = (bf16[96,4,8,17,16]{4,2,3,1,0:T(8,128)(2,1)}, bf16[96,4,8,17,16]{4,2,3,1,0:T(8,128)(2,1)S(1)}, u32[]{:S(2)}) copy-start(bf16[96,4,8,17,16]{4,2,3,1,0:T(8,128)(2,1)S(1)} %maximum_convert_fusion) | copy-start | bytes 5013508
  288.2 18.4 %copy-start.7 = (bf16[27,16]{0,1:T(8,128)(2,1)S(1)}, bf16[27,16]{0,1:T(8,128)(2,1)}, u32[]{:S(2)}) copy-start(bf16[27,16]{0,1:T(8,128)(2,1)} %param.17) | copy-start | bytes 2596
  295.0 26.4 %collective-permute-start.7 = (bf16[1,16,96,1,128]{2,1,4,0,3:T(8,128)(2,1)}, bf16[1,16,96,1,128]{2,1,4,0,3:T(8,128)(2,1)}, u32[]{:S(2)}, u32[]{:S(2)}) collective-permute-start(bf16[1,16,96,1,128]{2,1,4,0,3:T(8,128)(2,1)} %slice_bitcast_fusion.4), channel_id=1, source_target_pairs={{0,2},{2,4},{4,6},{6,8},{8,10},{10,12},{12,14},{1,3},{3,5},{5,7},{... | collective-permute-start | bytes 1179656 | tf_op jit(solution)/shard_map/ppermute | solution.py:21
  305.3 16.1 %collective-permute-start.8 = (bf16[1,16,96,1,128]{2,1,4,0,3:T(8,128)(2,1)S(1)}, bf16[1,16,96,1,128]{2,1,4,0,3:T(8,128)(2,1)S(1)}, u32[]{:S(2)}, u32[]{:S(2)}) collective-permute-start(bf16[1,16,96,1,128]{2,1,4,0,3:T(8,128)(2,1)S(1)} %slice_bitcast_fusion.3), channel_id=1, source_target_pairs={{2,0},{4,2},{6,4},{8,6},{10,8},{12,10},{14,12},{3,1},{5,3},{7,5},{... | collective-permute-start | bytes 1179656 | tf_op jit(solution)/shard_map/ppermute | solution.py:24
  380.9 20.5 %copy-start.3 = (bf16[1,96,4,128]{1,3,2,0:T(8,128)(2,1)S(1)}, bf16[1,96,4,128]{1,3,2,0:T(8,128)(2,1)}, u32[]{:S(2)}) copy-start(bf16[1,96,4,128]{1,3,2,0:T(8,128)(2,1)} %copy-done.2) | copy-start | bytes 294916
where the time goes:
time: 408 us; the launch traced here: 402 us
  local copies, waits for them, and re-layouts  186 us (46%)
  matrix products  154 us (38%)
  starting transfers between devices  24.8 us (6%)
  waiting for transfers between devices  23.3 us (6%)
  other arithmetic  11.8 us (3%)
    conv_general_dilated x4, matrix products, conv_taps(): lax.conv_general_dilated(volume, weights, (1, 1, 1), ((1, 1), (0, 0), (1,...  154 us
    conv_general_dilated x12, local copies, waits for them, and re-layouts, conv_taps(): lax.conv_general_dilated(volume, weights, (1, 1, 1), ((1, 1), (0, 0), (1,...  107 us
    convert_element_type x5, local copies, waits for them, and re-layouts, local(): h3 = jax.nn.relu(one_layer(h2, w_third)).astype(jnp.bfloat16)  27.1 us
    convert_element_type x5, local copies, waits for them, and re-layouts, local(): h1 = jax.nn.relu(one_layer(volume, first_kernel)).astype(jnp.bfloat16)  26.7 us
    ppermute x4, starting transfers between devices, padded(): lax.ppermute(lax.slice_in_dim(block, block.shape[dim] - width, None, axis...  19.2 us
    ppermute x4, waiting for transfers between devices, padded(): lax.ppermute(lax.slice_in_dim(block, block.shape[dim] - width, None, axis...  19.1 us
    unnamed x23, local copies, waits for them, and re-layouts  11.5 us
  transfers between devices with their start and end apart: 9, of which 3 were waited for; matrix products, arithmetic and copies ran while one was open for 12% of the time, Pallas kernels for 0%

commit v1 on v0

v1 whole, which is shorter than its diff:
```python
import numpy as np
import jax
import jax.numpy as jnp
from jax import lax
from jax.experimental import pallas as pl
from jax.experimental.pallas import tpu as pltpu
from jax.sharding import PartitionSpec as P

DTILE = 16
BLOCK_COLS = 32
BF = jnp.bfloat16
F32 = jnp.float32
VM = pl.BlockSpec(memory_space=pltpu.VMEM)
SM = pl.BlockSpec(memory_space=pltpu.SMEM)
MIB = 2**20

R, W, A = 4, 128, 16
T1 = 14


def window_starts(disp):
    count = -(-disp // T1)
    return [min(T1 * k, disp - T1) for k in range(count)]


def place_first():
    m = np.zeros((32, T1 * 3, 256), np.float32)
    for d in range(T1):
        for r in range(3):
            for a in range(3):
                for b in range(3):
                    for e in range(3):
                        col = (r + b) * 48 + e * 16 + d + a
                        m[9 * a + 3 * b + e, d * 3 + r, col] = 1
    return m.reshape(32, -1)


def place_second():
    m = np.zeros((3, 3, A, 2, 2, 4, 4, A), np.float32)
    c = np.arange(A)
    for d in range(2):
        for r in range(2):
            for a in range(3):
                for b in range(3):
                    m[a, b, c, d, r, d + a, r + b, c] = 1
    return m.reshape(9 * A, 4 * 256)


def place_third():
    m = np.zeros((3, 3, A, 2, R, 4, R, A), np.float32)
    c = np.arange(A)
    for d in range(2):
        for r in range(R):
            for a in range(3):
                for b in range(3):
                    if 0 <= r + b - 1 < R:
                        m[a, b, c, d, r, d + a, r + b - 1, c] = 1
    return m.reshape(9 * A, 2 * R * 256)


def place_halo():
    m = np.zeros((3, A, T1, 16, A), np.float32)
    c = np.arange(A)
    for d in range(T1):
        for a in range(3):
            m[a, c, d, d + a, c] = 1
    return m.reshape(3 * A, T1 * 256)


def place_last(rows, depth):
    n = len(rows)
    m = np.zeros((depth + 2, 3, 8, depth, n, 27), np.float32)
    for d in range(depth):
        for k, r in enumerate(rows):
            for a in range(3):
                for b in range(3):
                    for e in range(3):
                        m[d - (a - 1) + 1, e, r - (b - 1) + 1, d, k, 9 * a + 3 * b + e] = 1
    return m.reshape((depth + 2) * 24, depth * n * 27)


def pick_carried():
    m = np.zeros((4, R, A, A, 4, R), np.float32)
    for d in range(4):
        for r in range(R):
            for o in range(A):
                m[d, r, o, o, d, r] = 1
    return m


def bf(x):
    return jnp.asarray(x, BF)


def dot(a, b):
    return jnp.dot(a, b, preferred_element_type=F32)


def lanes(shape):
    return lax.broadcasted_iota(jnp.int32, shape, len(shape) - 1)


def shifted_sum(low, mid, high):
    lane = lanes(mid.shape)
    low = jnp.where(lane == 0, 0.0, pltpu.roll(low, 1, low.ndim - 1))
    high = jnp.where(lane == W - 1, 0.0, pltpu.roll(high, W - 1, high.ndim - 1))
    return mid + low + high


def combine(p):
    return shifted_sum(p[0:A], p[A : 2 * A], p[2 * A : 3 * A])


def parity():
    return lax.rem(lax.axis_index("rows"), 2)


def edges_kernel(carried, pick, even, odd):
    even_side = 1 - parity()
    pe = pick[even_side]
    po = pick[1 - even_side]
    both = jnp.concatenate([pe, po], axis=0)

    def step(q, _):
        c = carried[:, pl.ds(q * 16, 16), :].reshape(256, W)
        v = dot(both, c).astype(BF)
        even[pl.ds(4 * q, 4)] = v[:64].reshape(4, A, W)
        odd[pl.ds(4 * q, 4)] = v[64:].reshape(4, A, W)
        return 0

    lax.fori_loop(0, carried.shape[1] // 16, step, 0, unroll=4)


def prep_kernel(w1, w2, w3, w4, p1, p2, p3, ph, im, ie, tile, rep, bd, a1, a2, a3, ah, am, ae):
    v = dot(w1[...], p1[...]).astype(BF)
    for k in range(3 * T1):
        a1[pl.ds(k * A, A), :] = v[:, k * 256 : (k + 1) * 256]
    v = dot(w2[...], p2[...]).astype(BF)
    for k in range(4):
        a2[pl.ds(k * 48, 48), :] = v[:, k * 256 : (k + 1) * 256]
    v = dot(w3[...], p3[...]).astype(BF)
    for k in range(2 * R):
        a3[pl.ds(k * 48, 48), :] = v[:, k * 256 : (k + 1) * 256]
    for side in range(2):
        v = dot(ah_source(w3, side), ph[...]).astype(BF)
        for k in range(T1):
            ah[side, pl.ds(k * 48, 48), :] = v[:, k * 256 : (k + 1) * 256]
    t = dot(w4[...], tile[...]).astype(BF)
    blocks = dot(rep[...], t).astype(BF) * bd[...]
    am[...] = dot(im[...], blocks).astype(BF)
    for side in range(2):
        ae[side] = dot(ie[side], blocks).astype(BF)


def ah_source(w3, side):
    b = 2 * side
    v = w3[...]
    return jnp.concatenate([v[:, (3 * a + b) * A : (3 * a + b + 1) * A] for a in range(3)], axis=1)


def corr_kernel(own, mate, partner, pattern, valid, corr, even, odd):
    cam = lax.axis_index("cam")
    right = partner[cam] < cam
    disp = corr.shape[1]
    channels = own.shape[0] // R
    x, y = own[...], mate[...]
    left_side = jnp.where(right, x, y)
    right_side = jnp.where(right, y, x)
    lane = lanes((W, W))
    sub = lax.broadcasted_iota(jnp.int32, (W, W), 0)
    flip = jnp.where(lane + sub == W - 1, 1.0, 0.0).astype(BF)
    lt = dot(left_side, flip).astype(BF).T
    row = lax.rem(lax.broadcasted_iota(jnp.int32, right_side.shape, 0), R)
    zero = jnp.zeros((), BF)
    rs = jnp.concatenate([jnp.where(row == r, right_side, zero) for r in range(R)], axis=1)
    s = dot(lt, rs)
    scale = 1.0 / np.sqrt(channels).astype(np.float32)
    line = lanes((1, W)) // BLOCK_COLS
    for r in range(R):
        v = pltpu.roll(s[:, r * W : (r + 1) * W], 1, 1, stride=1, stride_axis=0)
        v = jnp.where(lane <= sub, v, 0.0).T[:disp] * scale
        v = jnp.concatenate(
            [v[t * DTILE : (t + 1) * DTILE] * pattern[r, t].astype(F32) for t in range(disp // DTILE)], axis=0
        )
        v = dot(v.astype(BF), flip)
        v = jnp.where(right, v, pltpu.roll(v, 0, 1, stride=1, stride_axis=0))
        pixels = jnp.zeros((1, W), F32)
        for k in range(W // BLOCK_COLS):
            pixels = jnp.where(line == k, valid[r, k].astype(F32), pixels)
        corr[r] = (v * pixels).astype(BF)
    side = 1 - parity()
    even[...] = corr[pl.ds(side, 3)]
    odd[...] = corr[pl.ds(1 - side, 3)]


def volume_kernel(
    corr, even, odd, carried, a1, a2, a3, am, pick,
    pre2, pre3, acc,
    ext, cs, h1, h2, h3,
):
    disp = corr.shape[1]
    bands = lax.axis_size("rows")
    me = lax.axis_index("rows")
    side = 1 - parity()
    top_live = (me > 0).astype(F32)
    bottom_live = (me < bands - 1).astype(F32)

    ext[:, 0:8, :] = jnp.zeros((10, 8, W), F32)
    ext[:, pl.ds(8 + disp, 8), :] = jnp.zeros((10, 8, W), F32)
    ext[3:7, pl.ds(8, disp), :] = corr[...].astype(F32)
    ext[pl.ds(7 * side, 3), pl.ds(8, disp), :] = even[...].astype(F32)
    ext[pl.ds(7 * (1 - side), 3), pl.ds(8, disp), :] = odd[...].astype(F32)
    starts = window_starts(disp)
    lane = lanes((16, W))
    for k, d0 in enumerate(starts):
        cs[k, 480:512, :] = jnp.zeros((32, W), BF)
        for r in range(10):
            v = ext[r, d0 + 7 : d0 + 23, :]
            low = jnp.where(lane == 0, 0.0, pltpu.roll(v, 1, 1))
            high = jnp.where(lane == W - 1, 0.0, pltpu.roll(v, W - 1, 1))
            cs[k, r * 48 : r * 48 + 16, :] = low.astype(BF)
            cs[k, r * 48 + 16 : r * 48 + 32, :] = v.astype(BF)
            cs[k, r * 48 + 32 : r * 48 + 48, :] = high.astype(BF)

    zero_row = jnp.zeros((8, A, W), BF)
    h1[0] = zero_row
    h1[disp + 1] = zero_row
    h2[0] = zero_row[:R]
    h2[disp + 1] = zero_row[:R]

    w1 = a1[...]
    for k, d0 in enumerate(starts):
        x = jnp.concatenate([cs[k, pl.ds(j * 48, 256), :] for j in (0, 3, 5)], axis=1)
        p = jnp.maximum(dot(w1, x), 0.0)
        for g, j0 in enumerate((0, 3, 5)):
            q = p[:, g * W : (g + 1) * W].reshape(T1, 3, A, W)
            for t in range(3):
                j = j0 + t
                if g == 2 and t == 0:
                    continue
                v = q[:, t]
                if j < 2:
                    v = v * top_live
                if j > 5:
                    v = v * bottom_live
                h1[pl.ds(1 + d0, T1), j] = v.astype(BF)

    w2 = a2[...]
    sel = pick[...]

    def second(i, _):
        c = carried[:, pl.ds(i * 16, 16), :].reshape(256, W)
        own = dot(sel, c)
        for g in range(3):
            x = jnp.concatenate(
                [h1[pl.ds(4 * i + 2 * h, 4), 2 * g : 2 * g + 4].reshape(256, W) for h in range(2)], axis=1
            )
            p = dot(w2, x)
            for h in range(2):
                for d in range(2):
                    for r in range(2):
                        n = (d * 2 + r) * 48
                        v = combine(p[n : n + 48, h * W : (h + 1) * W])
                        j = 2 * g + r
                        dd = 2 * h + d
                        if j == 0:
                            pre2[0, 4 * i + dd] = v
                        elif j == 5:
                            pre2[1, 4 * i + dd] = v
                        else:
                            m = (dd * R + j - 1) * A
                            v = jnp.maximum(v + own[m : m + A], 0.0)
                            h2[4 * i + dd + 1, j - 1] = v.astype(BF)
        return 0

    lax.fori_loop(0, disp // 4, second, 0)

    w3 = a3[...]

    def third(i, _):
        x = jnp.concatenate([h2[pl.ds(4 * i + 2 * h, 4)].reshape(256, W) for h in range(2)], axis=1)
        p = dot(w3, x)
        for h in range(2):
            for d in range(2):
                for r in range(R):
                    n = (d * R + r) * 48
                    v = combine(p[n : n + 48, h * W : (h + 1) * W])
                    dd = 4 * i + 2 * h + d
                    if r == 0:
                        pre3[0, dd] = v
                    elif r == R - 1:
                        pre3[1, dd] = v
                    else:
                        h3[dd, r - 1] = jnp.maximum(v, 0.0).astype(BF)
        return 0

    lax.fori_loop(0, disp // 4, third, 0)

    acc[0:2] = jnp.zeros((2, 24, W), F32)
    w4 = am[...]
    for k in range(disp // 8):
        p = dot(w4, h3[8 * k : 8 * k + 8].reshape(256, W)).reshape(10, 24, W)
        acc[8 * k : 8 * k + 2] += p[:2]
        acc[8 * k + 2 : 8 * k + 10] = p[2:]


def edge_kernel(
    even, odd, corr, pre2, pre3, acc_in, ah, ae,
    main, part_even, part_odd,
    acc, h2, h3, comb,
):
    disp = corr.shape[1]
    bands = lax.axis_size("rows")
    me = lax.axis_index("rows")
    acc[...] = acc_in[...]
    zero_row = jnp.zeros((A, W), BF)
    starts = window_starts(disp)
    for kind, carried in enumerate((even, odd)):
        side = (1 - parity()) if kind == 0 else parity()
        live = jnp.where(side == 0, me > 0, me < bands - 1).astype(F32)
        h2[0] = zero_row
        h2[disp + 1] = zero_row
        v = jnp.maximum(pre2[side] + carried[...].astype(F32), 0.0) * live
        h2[1 : disp + 1] = v.astype(BF)
        w3 = ah[side]
        for d0 in starts:
            p = dot(w3, h2[d0 : d0 + 16].reshape(256, W))
            for d in range(T1):
                v = combine(p[d * 48 : d * 48 + 48]) + pre3[side, d0 + d]
                h3[d0 + d] = jnp.maximum(v, 0.0).astype(BF)
        w4 = ae[side]
        for k in range(disp // 16):
            p = dot(w4, h3[16 * k : 16 * k + 16].reshape(256, W)).reshape(18, 24, W)
            acc[16 * k : 16 * k + 18] += p

    for d in range(disp):
        comb[d * 8 : d * 8 + 8, :] = shifted_sum(acc[d + 1, 0:8], acc[d + 1, 8:16], acc[d + 1, 16:24])
    side = 1 - parity()
    for r in range(R):
        v = comb[pl.ds(r + 1, disp, stride=8), :] + corr[r].astype(F32)
        main[pl.ds(r, disp, stride=R), :] = v
    top = comb[pl.ds(0, disp, stride=8), :]
    bottom = comb[pl.ds(5, disp, stride=8), :]
    part_even[...] = jnp.where(side == 0, top, bottom)
    part_odd[...] = jnp.where(side == 0, bottom, top)


def call(kernel, outs, args, specs=None, scratch=(), us=2.0):
    return pl.pallas_call(
        kernel,
        out_shape=tuple(jax.ShapeDtypeStruct(s, d) for s, d in outs),
        in_specs=specs or [VM] * len(args),
        out_specs=tuple(VM for _ in outs),
        scratch_shapes=[pltpu.VMEM(s, d) for s, d in scratch],
        compiler_params=pltpu.CompilerParams(vmem_limit_bytes=40 * MIB),
        cost_estimate=pl.CostEstimate(flops=int(us * 1.1e9), bytes_accessed=1000, transcendentals=0),
    )(*args)


def local(features, partner, pattern, valid, carried, w_first, w_second, w_third, w_last):
    channels = features.shape[1]
    disp = carried.shape[2]
    bands = lax.axis_size("rows")
    cams = lax.axis_size("cam")
    even_pairs = [p for k in range(0, bands - 1, 2) for p in ((k, k + 1), (k + 1, k))]
    odd_pairs = [p for k in range(1, bands - 1, 2) for p in ((k, k + 1), (k + 1, k))]

    def swap(x, pairs):
        return lax.ppermute(x, "rows", pairs)

    own = features.reshape(channels * R, W)
    mate = lax.ppermute(own, "cam", [(i, i ^ 1) for i in range(cams)])
    flat = carried.reshape(A, disp * R, W)
    pick = pick_carried()
    ends = np.stack([pick[:, 0], pick[:, R - 1]]).reshape(2, 4 * A, 256)
    edge = ((disp, A, W), BF)
    even_c, odd_c = call(edges_kernel, [edge, edge], [flat, bf(ends)], us=1.5)
    even_c = swap(even_c, even_pairs)
    odd_c = swap(odd_c, odd_pairs)

    w1 = jnp.pad(w_first.T, ((0, 0), (0, 5)))
    rows_of = lambda w: w.reshape(3, 3, 3, A, A).transpose(2, 3, 0, 1, 4).reshape(48, 9 * A)
    w4 = jnp.pad(w_last, ((0, 5), (0, 0)))
    tile = np.tile(np.eye(A), (1, 16))
    rep = np.pad(np.tile(np.eye(27), (16, 1)), ((0, 0), (0, 5)))
    mask = np.kron(np.eye(16), np.ones((27, A)))
    ie = np.stack([place_last([0], 16), place_last([R - 1], 16)])
    consts = [place_first(), place_second(), place_third(), place_halo(), place_last([1, 2], 8), ie, tile, rep, mask]
    mats = [
        ((T1 * 48, 256), BF),
        ((192, 256), BF),
        ((384, 256), BF),
        ((2, T1 * 48, 256), BF),
        ((240, 256), BF),
        ((2, 432, 256), BF),
    ]
    a1, a2, a3, ah, am, ae = call(
        prep_kernel, mats, [w1, rows_of(w_second), rows_of(w_third), w4] + [bf(c) for c in consts], us=1.5
    )

    rows3 = ((3, disp, W), BF)
    corr, even_r, odd_r = call(
        corr_kernel,
        [((R, disp, W), BF), rows3, rows3],
        [own, mate, partner, pattern, valid[0]],
        specs=[VM, VM, SM, SM, SM],
        us=2.0,
    )
    even_r = swap(even_r, even_pairs)
    odd_r = swap(odd_r, odd_pairs)
    pre = ((2, disp, A, W), F32)
    pre2, pre3, acc = call(
        volume_kernel,
        [pre, pre, ((disp + 2, 24, W), F32)],
        [corr, even_r, odd_r, flat, a1, a2, a3, am, bf(pick.reshape(256, 256))],
        scratch=[
            ((10, disp + 16, W), F32),
            ((len(window_starts(disp)), 512, W), BF),
            ((disp + 2, 8, A, W), BF),
            ((disp + 2, R, A, W), BF),
            ((disp, 2, A, W), BF),
        ],
        us=10.0,
    )
    main, part_even, part_odd = call(
        edge_kernel,
        [((disp * R, W), F32), ((disp, W), F32), ((disp, W), F32)],
        [even_c, odd_c, corr, pre2, pre3, acc, ah, ae],
        scratch=[
            ((disp + 2, 24, W), F32),
            ((disp + 2, A, W), BF),
            ((disp, A, W), BF),
            ((disp * 8, W), F32),
        ],
        us=4.0,
    )
    part_even = swap(part_even, even_pairs)
    part_odd = swap(part_odd, odd_pairs)
    is_odd = lax.rem(lax.axis_index("rows"), 2) == 1
    top = jnp.where(is_odd, part_even, part_odd)[:, None]
    bottom = jnp.where(is_odd, part_odd, part_even)[:, None]
    none = jnp.zeros((disp, R - 2, W), F32)
    out = main.reshape(disp, R, W) + jnp.concatenate([top, none, bottom], axis=1)
    return out[None]


def solution(mesh):
    return jax.shard_map(
        local,
        mesh=mesh,
        in_specs=(
            P(("seg", "cam"), None, "rows", None),
            P(),
            P(("seg", "rows"), None),
            P(("seg", "cam"), "rows", None),
            P(("seg", "cam"), None, None, "rows", None),
            P(),
            P(),
            P(),
            P(),
        ),
        out_specs=P(("seg", "cam"), None, "rows", None),
        check_vma=False,
    )
```

time: 408 us -> 57.2 us (0.14)
  the two profiles are of different devices: /device:TPU:0 before, /device:TPU:16 now
where the time goes in v1:
time: 57.2 us; the launch traced here: 57 us
  Pallas kernels  24.9 us (44%)
  waiting for transfers between devices  15.1 us (26%)
  starting transfers between devices  12.5 us (22%)
  local copies, waits for them, and re-layouts  3.31 us (6%)
  other arithmetic  0.83 us (1%)
    pallas_call x5, Pallas kernels, call(): pl.pallas_call(kernel, out_shape=tuple((jax.ShapeDtypeStruct(s, d) for s,...  24.9 us
    ppermute x6, waiting for transfers between devices, swap(): return lax.ppermute(x, 'rows', pairs)  15.1 us
    ppermute x6, starting transfers between devices, swap(): return lax.ppermute(x, 'rows', pairs)  12.5 us
    unnamed x45, local copies, waits for them, and re-layouts  2.83 us
  transfers between devices with their start and end apart: 7, of which 3 were waited for; matrix products, arithmetic and copies ran while one was open for 2% of the time, Pallas kernels for 39%

profile of v1, /device:TPU:16, one launch (start us, length us, event | category | flops | bytes accessed | tf_op | source)
XLA Modules:
  0.0 57.0 jit_solution(657789176322570381)
XLA Ops:
  0.0 0.0 collective-permute-start.2
  0.0 0.0 copy-start
  0.0 1.4 %copy-done = bf16[1,16,96,4,128]{4,3,2,1,0:T(4,128)(2,1)S(1)} copy-done((bf16[1,16,96,4,128]{4,3,2,1,0:T(4,128)(2,1)S(1)}, bf16[1,16,96,4,128]{4,3,2,1,0:T(4,128)(2,1)}, u32[]{:S(2)}) %copy-start) | copy-done | bytes 1572888
  1.4 0.0 copy-start.15
  1.4 0.8 %copy-done.15 = bf16[2,64,256]{2,1,0:T(8,128)(2,1)S(1)} copy-done((bf16[2,64,256]{2,1,0:T(8,128)(2,1)S(1)}, bf16[2,64,256]{2,1,0:T(8,128)(2,1)}, u32[]{:S(2)}) %copy-start.15) | copy-done | bytes 65560
  2.3 0.0 copy-start.2
  2.3 0.0 copy-start.3
  2.3 0.0 copy-start.4
  2.3 0.0 copy-start.5
  2.3 1.3 %shard_map.190 = (bf16[96,16,128]{2,1,0:T(8,128)(2,1)S(1)}, bf16[96,16,128]{2,1,0:T(8,128)(2,1)S(1)}) custom-call(bf16[16,384,128]{2,1,0:T(8,128)(2,1)S(1)} %bitcast.18, bf16[2,64,256]{2,1,0:T(8,128)(2,1)S(1)} %copy-done.15), custom_call_target="tpu_custom_call" | custom-call | flops 1650000000 | bytes 1000 | tf_op jit(solution)/shard_map/pallas_call | solution.py:349
  3.6 1.6 %collective-permute-start = (bf16[96,16,128]{2,1,0:T(8,128)(2,1)S(1)}, bf16[96,16,128]{2,1,0:T(8,128)(2,1)S(1)}, u32[]{:S(2)}, u32[]{:S(2)}) collective-permute-start(bf16[96,16,128]{2,1,0:T(8,128)(2,1)S(1)} %get-tuple-element.22), channel_id=1, source_target_pairs={{0,2},{2,0},{4,6},{6,4},{8,10},{10,8},{12,14},{14,12},{1,3},{3,1},... | collective-permute-start | bytes 1179656 | tf_op jit(solution)/shard_map/ppermute | solution.py:369
  5.2 2.3 %collective-permute-start.1 = (bf16[96,16,128]{2,1,0:T(8,128)(2,1)S(1)}, bf16[96,16,128]{2,1,0:T(8,128)(2,1)S(1)}, u32[]{:S(2)}, u32[]{:S(2)}) collective-permute-start(bf16[96,16,128]{2,1,0:T(8,128)(2,1)S(1)} %get-tuple-element.23), channel_id=1, source_target_pairs={{2,4},{4,2},{6,8},{8,6},{10,12},{12,10},{3,5},{5,3},{7,9},{9,7},{1... | collective-permute-start | bytes 1179656 | tf_op jit(solution)/shard_map/ppermute | solution.py:369
  7.5 0.0 copy-done.17
  7.5 0.2 copy.26
  7.7 0.1 copy.27
  7.8 0.1 reshape.69.w2
  7.9 0.0 copy-done.18
  7.9 0.2 copy.28
  8.1 0.1 copy.29
  8.2 0.1 reshape.71.w3
  8.3 0.0 copy-done.19
  8.3 0.1 copy.30
  8.4 0.0 copy-done.20
  8.5 0.0 collective-permute-done.2.mate
  8.5 0.0 copy-done.2
  8.5 0.0 copy-done.3
  8.5 0.0 copy-done.4
  8.5 0.0 copy-done.5
  8.5 0.0 copy-start.6
  8.5 0.0 copy-start.7
  8.5 0.0 copy-start.8
  8.5 0.0 copy-start.9
  8.6 0.0 copy-start.10
  8.6 0.0 copy-start.11
  8.6 0.0 copy-start.12
  8.6 0.0 copy-start.14
  8.6 0.0 copy-start.16
  8.6 1.5 %shard_map.191 = (bf16[4,96,128]{2,1,0:T(8,128)(2,1)S(1)}, bf16[3,96,128]{2,1,0:T(8,128)(2,1)S(1)}, bf16[3,96,128]{2,1,0:T(8,128)(2,1)S(1)}) custom-call(bf16[512,128]{1,0:T(8,128)(2,1)S(1)} %bitcast.21, bf16[512,128]{1,0:T(8,128)(2,1)S(1)} %collective-permute-done.2.mate, s32[2]{0:T(128)S(1)} %copy-done.5, s32[4,6]{1,0:T(4,128)S(1)} %copy-done.3, ...), custom_call_target="tpu_custom_call" | custom-call | flops 2200000000 | bytes 1000 | tf_op jit(solution)/shard_map/pallas_call | solution.py:349
  10.1 2.7 %collective-permute-start.3 = (bf16[3,96,128]{2,1,0:T(8,128)(2,1)S(1)}, bf16[3,96,128]{2,1,0:T(8,128)(2,1)S(1)}, u32[]{:S(2)}, u32[]{:S(2)}) collective-permute-start(bf16[3,96,128]{2,1,0:T(8,128)(2,1)S(1)} %get-tuple-element.25), channel_id=1, source_target_pairs={{0,2},{2,0},{4,6},{6,4},{8,10},{10,8},{12,14},{14,12},{1,3},{3,1},... | collective-permute-start | bytes 221192 | tf_op jit(solution)/shard_map/ppermute | solution.py:369
  12.8 2.0 %collective-permute-start.4 = (bf16[3,96,128]{2,1,0:T(8,128)(2,1)S(1)}, bf16[3,96,128]{2,1,0:T(8,128)(2,1)S(1)}, u32[]{:S(2)}, u32[]{:S(2)}) collective-permute-start(bf16[3,96,128]{2,1,0:T(8,128)(2,1)S(1)} %get-tuple-element.26), channel_id=1, source_target_pairs={{2,4},{4,2},{6,8},{8,6},{10,12},{12,10},{3,5},{5,3},{7,9},{9,7},{1... | collective-permute-start | bytes 221192 | tf_op jit(solution)/shard_map/ppermute | solution.py:369
  14.8 0.0 copy-done.6
  14.9 0.0 copy-done.7
  14.9 0.0 copy-done.8
  14.9 0.0 copy-done.9
  14.9 0.0 copy-done.10
  14.9 0.0 copy-done.11
  14.9 0.0 copy-done.12
  14.9 0.0 copy-done.14
  14.9 0.0 copy-done.16
  14.9 1.2 %shard_map.192 = (bf16[672,256]{1,0:T(8,128)(2,1)S(1)}, bf16[192,256]{1,0:T(8,128)(2,1)S(1)}, bf16[384,256]{1,0:T(8,128)(2,1)S(1)}, bf16[2,672,256]{2,1,0:T(8,12...) custom-call(bf16[16,32]{1,0:T(8,128)(2,1)S(1)} %pad.8.w1, bf16[48,144]{1,0:T(8,128)(2,1)S(1)} %reshape.69.w2, ...), custom_call_target="tpu_custom_call" | custom-call | flops 1650000000 | bytes 1000 | tf_op jit(solution)/shard_map/pallas_call | solution.py:349
  16.2 10.6 %collective-permute-done.3.even = bf16[3,96,128]{2,1,0:T(8,128)(2,1)S(1)} collective-permute-done((bf16[3,96,128]{2,1,0:T(8,128)(2,1)S(1)}, bf16[3,96,128]{2,1,0:T(8,128)(2,1)S(1)}, u32[]{:S(2)}, u32[]{:S(2)}) %collective-permute-start.3) | collective-permute-done | bytes 73760 | tf_op jit(solution)/shard_map/ppermute | solution.py:369
  26.8 0.0 collective-permute-done.4.odd
  26.8 0.0 copy-done.1
  26.8 0.0 copy-done.13
  26.8 18.0 %shard_map.193 = (f32[2,96,16,128]{3,2,1,0:T(8,128)S(1)}, f32[2,96,16,128]{3,2,1,0:T(8,128)S(1)}, f32[98,24,128]{2,1,0:T(8,128)S(1)}) custom-call(bf16[4,96,128]{2,1,0:T(8,128)(2,1)S(1)} %get-tuple-element.24.corr, bf16[3,96,128]{2,1,0:T(8,128)(2,1)S(1)} %collective-permute-done.3.even, bf16[3,96,128]{2,1,0:T(8,128)(2,1)S(1)} %collective-permute-done.4.odd, ...), custom_call_target="tpu_custom_call" | custom-call | flops 11000000512 | bytes 1000 | tf_op jit(solution)/shard_map/pallas_call | solution.py:349
  44.8 0.0 collective-permute-done.even
  44.8 0.0 collective-permute-done.1.odd
  44.8 2.9 %shard_map.194 = (f32[384,128]{1,0:T(8,128)S(1)}, f32[96,128]{1,0:T(8,128)S(1)}, f32[96,128]{1,0:T(8,128)S(1)}) custom-call(bf16[96,16,128]{2,1,0:T(8,128)(2,1)S(1)} %collective-permute-done.even, bf16[96,16,128]{2,1,0:T(8,128)(2,1)S(1)} %collective-permute-done.1.odd, bf16[4,96,128]{2,1,0:T(8,128)(2,1)S(1)} %get-tuple-element.24.corr, ...), custom_call_target="tpu_custom_call" | custom-call | flops 4400000000 | bytes 1000 | tf_op jit(solution)/shard_map/pallas_call | solution.py:349
  47.7 1.6 %collective-permute-start.5 = (f32[96,128]{1,0:T(8,128)S(1)}, f32[96,128]{1,0:T(8,128)S(1)}, u32[]{:S(2)}, u32[]{:S(2)}) collective-permute-start(f32[96,128]{1,0:T(8,128)S(1)} %get-tuple-element.37), channel_id=1, source_target_pairs={{0,2},{2,0},{4,6},{6,4},{8,10},{10,8},{12,14},{14,12},{1,3},{3,1},... | collective-permute-start | bytes 147464 | tf_op jit(solution)/shard_map/ppermute | solution.py:369
  49.3 2.3 %collective-permute-start.6 = (f32[96,128]{1,0:T(8,128)S(1)}, f32[96,128]{1,0:T(8,128)S(1)}, u32[]{:S(2)}, u32[]{:S(2)}) collective-permute-start(f32[96,128]{1,0:T(8,128)S(1)} %get-tuple-element.38), channel_id=1, source_target_pairs={{2,4},{4,2},{6,8},{8,6},{10,12},{12,10},{3,5},{5,3},{7,9},{9,7},{1... | collective-permute-start | bytes 147464 | tf_op jit(solution)/shard_map/ppermute | solution.py:369
  51.6 0.1 pad.11.clone
  51.7 0.2 collective-permute-done.5
  51.9 4.3 %collective-permute-done.6 = f32[96,128]{1,0:T(8,128)S(1)} collective-permute-done((f32[96,128]{1,0:T(8,128)S(1)}, f32[96,128]{1,0:T(8,128)S(1)}, u32[]{:S(2)}, u32[]{:S(2)}) %collective-permute-start.6) | collective-permute-done | bytes 49184 | tf_op jit(solution)/shard_map/ppermute | solution.py:369
  56.1 0.8 %maximum_add_fusion = f32[1,96,4,128]{3,2,1,0:T(4,128)} fusion(f32[1,96,4,128]{3,2,1,0:T(4,128)S(1)} %bitcast.17, f32[1,96,1,128]{3,2,1,0:T(1,128)S(1)} %bitcast.26, f32[1,96,1,128]{3,2,1,0:T(1,128)S(1)} %bitcast.25, f32[4]{0:T(128)S(1)} %pad.11.clone), kind=kLoop, calls=%fused_computation | loop fusion | flops 147456 | bytes 491536 | tf_op jit(solution)/shard_map/add | solution.py:443
  (10 shorter events, 0.0 us)
Async XLA Ops:
  0.0 8.5 %collective-permute-start.2 = (bf16[512,128]{1,0:T(8,128)(2,1)}, bf16[512,128]{1,0:T(8,128)(2,1)S(1)}, u32[]{:S(2)}, u32[]{:S(2)}) collective-permute-start(bf16[512,128]{1,0:T(8,128)(2,1)} %bitcast.20), channel_id=1, source_target_pairs={{0,1},{1,0},{2,3},{3,2},{4,5},{5,4},{6,7},{7,6},{8,9},{9,8},{10,11... | collective-permute-start | bytes 393224 | tf_op jit(solution)/shard_map/ppermute | solution.py:372
  0.0 1.4 %copy-start = (bf16[1,16,96,4,128]{4,3,2,1,0:T(4,128)(2,1)S(1)}, bf16[1,16,96,4,128]{4,3,2,1,0:T(4,128)(2,1)}, u32[]{:S(2)}) copy-start(bf16[1,16,96,4,128]{4,3,2,1,0:T(4,128)(2,1)} %param.24) | copy-start | bytes 4718596
  1.4 0.8 %copy-start.15 = (bf16[2,64,256]{2,1,0:T(8,128)(2,1)S(1)}, bf16[2,64,256]{2,1,0:T(8,128)(2,1)}, u32[]{:S(2)}) copy-start(bf16[2,64,256]{2,1,0:T(8,128)(2,1)} %constant.39.clone.pick) | copy-start | bytes 196612
  2.3 5.3 %copy-start.17 = (bf16[27,16,16]{0,2,1:T(8,128)(2,1)S(1)}, bf16[27,16,16]{0,2,1:T(8,128)(2,1)}, u32[]{:S(2)}) copy-start(bf16[27,16,16]{0,2,1:T(8,128)(2,1)} %param.26) | copy-start | bytes 41476
  2.3 5.7 %copy-start.18 = (bf16[27,16,16]{0,2,1:T(8,128)(2,1)S(1)}, bf16[27,16,16]{0,2,1:T(8,128)(2,1)}, u32[]{:S(2)}) copy-start(bf16[27,16,16]{0,2,1:T(8,128)(2,1)} %param.27) | copy-start | bytes 41476
  2.3 6.1 %copy-start.19 = (bf16[27,16]{0,1:T(8,128)(2,1)S(1)}, bf16[27,16]{0,1:T(8,128)(2,1)}, u32[]{:S(2)}) copy-start(bf16[27,16]{0,1:T(8,128)(2,1)} %param.28) | copy-start | bytes 2596
  2.3 6.2 %copy-start.20 = (bf16[27,16]{0,1:T(8,128)(2,1)S(1)}, bf16[27,16]{0,1:T(8,128)(2,1)}, u32[]{:S(2)}) copy-start(bf16[27,16]{0,1:T(8,128)(2,1)} %param.25) | copy-start | bytes 2596
  2.3 6.2 %copy-start.2 = (bf16[1,128,4,128]{3,2,1,0:T(4,128)(2,1)S(1)}, bf16[1,128,4,128]{3,2,1,0:T(4,128)(2,1)}, u32[]{:S(2)}) copy-start(bf16[1,128,4,128]{3,2,1,0:T(4,128)(2,1)} %param.20) | copy-start | bytes 393220
  2.3 6.2 %copy-start.3 = (s32[4,6]{1,0:T(4,128)S(1)}, s32[4,6]{1,0:T(4,128)}, u32[]{:S(2)}) copy-start(s32[4,6]{1,0:T(4,128)} %pattern.1) | copy-start | bytes 292
  2.3 6.2 %copy-start.4 = (s32[1,4,4]{2,1,0:T(4,128)S(1)}, s32[1,4,4]{2,1,0:T(4,128)}, u32[]{:S(2)}) copy-start(s32[1,4,4]{2,1,0:T(4,128)} %param.23) | copy-start | bytes 196
  2.3 6.2 %copy-start.5 = (s32[2]{0:T(128)S(1)}, s32[2]{0:T(128)}, u32[]{:S(2)}) copy-start(s32[2]{0:T(128)} %partner.1) | copy-start | bytes 28
  3.6 41.2 %collective-permute-start = (bf16[96,16,128]{2,1,0:T(8,128)(2,1)S(1)}, bf16[96,16,128]{2,1,0:T(8,128)(2,1)S(1)}, u32[]{:S(2)}, u32[]{:S(2)}) collective-permute-start(bf16[96,16,128]{2,1,0:T(8,128)(2,1)S(1)} %get-tuple-element.22), channel_id=1, source_target_pairs={{0,2},{2,0},{4,6},{6,4},{8,10},{10,8},{12,14},{14,12},{1,3},{3,1},... | collective-permute-start | bytes 1179656 | tf_op jit(solution)/shard_map/ppermute | solution.py:369
  5.2 39.6 %collective-permute-start.1 = (bf16[96,16,128]{2,1,0:T(8,128)(2,1)S(1)}, bf16[96,16,128]{2,1,0:T(8,128)(2,1)S(1)}, u32[]{:S(2)}, u32[]{:S(2)}) collective-permute-start(bf16[96,16,128]{2,1,0:T(8,128)(2,1)S(1)} %get-tuple-element.23), channel_id=1, source_target_pairs={{2,4},{4,2},{6,8},{8,6},{10,12},{12,10},{3,5},{5,3},{7,9},{9,7},{1... | collective-permute-start | bytes 1179656 | tf_op jit(solution)/shard_map/ppermute | solution.py:369
  8.5 6.3 %copy-start.6 = (bf16[2,432,432]{2,1,0:T(8,128)(2,1)S(1)}, bf16[2,432,432]{2,1,0:T(8,128)(2,1)}, u32[]{:S(2)}) copy-start(bf16[2,432,432]{2,1,0:T(8,128)(2,1)} %constant.45.clone.ie) | copy-start | bytes 2239492
  8.5 6.3 %copy-start.7 = (bf16[32,10752]{1,0:T(8,128)(2,1)S(1)}, bf16[32,10752]{1,0:T(8,128)(2,1)}, u32[]{:S(2)}) copy-start(bf16[32,10752]{1,0:T(8,128)(2,1)} %constant.40.clone.p1) | copy-start | bytes 2064388
  8.5 6.3 %copy-start.8 = (bf16[144,2048]{1,0:T(8,128)(2,1)S(1)}, bf16[144,2048]{1,0:T(8,128)(2,1)}, u32[]{:S(2)}) copy-start(bf16[144,2048]{1,0:T(8,128)(2,1)} %constant.42.clone.p3) | copy-start | bytes 1769476
  8.5 6.3 %copy-start.9 = (bf16[48,3584]{1,0:T(8,128)(2,1)S(1)}, bf16[48,3584]{1,0:T(8,128)(2,1)}, u32[]{:S(2)}) copy-start(bf16[48,3584]{1,0:T(8,128)(2,1)} %constant.43.clone.ph) | copy-start | bytes 1032196
  8.6 6.3 %copy-start.10 = (bf16[144,1024]{1,0:T(8,128)(2,1)S(1)}, bf16[144,1024]{1,0:T(8,128)(2,1)}, u32[]{:S(2)}) copy-start(bf16[144,1024]{1,0:T(8,128)(2,1)} %constant.41.clone.p2) | copy-start | bytes 884740
  8.6 6.3 %copy-start.11 = (bf16[240,432]{1,0:T(8,128)(2,1)S(1)}, bf16[240,432]{1,0:T(8,128)(2,1)}, u32[]{:S(2)}) copy-start(bf16[240,432]{1,0:T(8,128)(2,1)} %constant.44.clone.im) | copy-start | bytes 622084
  8.6 6.3 %copy-start.12 = (bf16[432,256]{1,0:T(8,128)(2,1)S(1)}, bf16[432,256]{1,0:T(8,128)(2,1)}, u32[]{:S(2)}) copy-start(bf16[432,256]{1,0:T(8,128)(2,1)} %constant.48.clone.bd) | copy-start | bytes 663556
  8.6 6.3 %copy-start.14 = (bf16[432,32]{1,0:T(8,128)(2,1)S(1)}, bf16[432,32]{1,0:T(8,128)(2,1)}, u32[]{:S(2)}) copy-start(bf16[432,32]{1,0:T(8,128)(2,1)} %constant.47.clone.rep) | copy-start | bytes 82948
  8.6 6.3 %copy-start.16 = (bf16[16,256]{1,0:T(8,128)(2,1)S(1)}, bf16[16,256]{1,0:T(8,128)(2,1)}, u32[]{:S(2)}) copy-start(bf16[16,256]{1,0:T(8,128)(2,1)} %constant.46.clone.tile) | copy-start | bytes 24580
  10.1 16.7 %collective-permute-start.3 = (bf16[3,96,128]{2,1,0:T(8,128)(2,1)S(1)}, bf16[3,96,128]{2,1,0:T(8,128)(2,1)S(1)}, u32[]{:S(2)}, u32[]{:S(2)}) collective-permute-start(bf16[3,96,128]{2,1,0:T(8,128)(2,1)S(1)} %get-tuple-element.25), channel_id=1, source_target_pairs={{0,2},{2,0},{4,6},{6,4},{8,10},{10,8},{12,14},{14,12},{1,3},{3,1},... | collective-permute-start | bytes 221192 | tf_op jit(solution)/shard_map/ppermute | solution.py:369
  12.8 14.0 %copy-start.1 = (bf16[1,16,96,4,128]{4,3,2,1,0:T(4,128)(2,1)S(1)}, bf16[1,16,96,4,128]{4,3,2,1,0:T(4,128)(2,1)}, u32[]{:S(2)}) copy-start(bf16[1,16,96,4,128]{4,3,2,1,0:T(4,128)(2,1)} %param.24) | copy-start | bytes 4718596
  12.8 14.0 %copy-start.13 = (bf16[256,256]{1,0:T(8,128)(2,1)S(1)}, bf16[256,256]{1,0:T(8,128)(2,1)}, u32[]{:S(2)}) copy-start(bf16[256,256]{1,0:T(8,128)(2,1)} %constant.49.clone.pick) | copy-start | bytes 393220
  12.8 14.0 %collective-permute-start.4 = (bf16[3,96,128]{2,1,0:T(8,128)(2,1)S(1)}, bf16[3,96,128]{2,1,0:T(8,128)(2,1)S(1)}, u32[]{:S(2)}, u32[]{:S(2)}) collective-permute-start(bf16[3,96,128]{2,1,0:T(8,128)(2,1)S(1)} %get-tuple-element.26), channel_id=1, source_target_pairs={{2,4},{4,2},{6,8},{8,6},{10,12},{12,10},{3,5},{5,3},{7,9},{9,7},{1... | collective-permute-start | bytes 221192 | tf_op jit(solution)/shard_map/ppermute | solution.py:369
  47.7 4.2 %collective-permute-start.5 = (f32[96,128]{1,0:T(8,128)S(1)}, f32[96,128]{1,0:T(8,128)S(1)}, u32[]{:S(2)}, u32[]{:S(2)}) collective-permute-start(f32[96,128]{1,0:T(8,128)S(1)} %get-tuple-element.37), channel_id=1, source_target_pairs={{0,2},{2,0},{4,6},{6,4},{8,10},{10,8},{12,14},{14,12},{1,3},{3,1},... | collective-permute-start | bytes 147464 | tf_op jit(solution)/shard_map/ppermute | solution.py:369
  49.3 6.9 %collective-permute-start.6 = (f32[96,128]{1,0:T(8,128)S(1)}, f32[96,128]{1,0:T(8,128)S(1)}, u32[]{:S(2)}, u32[]{:S(2)}) collective-permute-start(f32[96,128]{1,0:T(8,128)S(1)} %get-tuple-element.38), channel_id=1, source_target_pairs={{2,4},{4,2},{6,8},{8,6},{10,12},{12,10},{3,5},{5,3},{7,9},{9,7},{1... | collective-permute-start | bytes 147464 | tf_op jit(solution)/shard_map/ppermute | solution.py:369

commit v2 on v1

--- a/solution.py
+++ b/solution.py
@@ -12,6 +12,7 @@
 F32 = jnp.float32
 VM = pl.BlockSpec(memory_space=pltpu.VMEM)
 SM = pl.BlockSpec(memory_space=pltpu.SMEM)
+HB = pl.BlockSpec(memory_space=pltpu.HBM)
 MIB = 2**20
 
 R, W, A = 4, 128, 16
@@ -24,7 +25,7 @@
 
 
 def place_first():
-    m = np.zeros((32, T1 * 3, 256), np.float32)
+    m = np.zeros((27, T1 * 3, 256), np.float32)
     for d in range(T1):
         for r in range(3):
             for a in range(3):
@@ -32,7 +33,7 @@
                     for e in range(3):
                         col = (r + b) * 48 + e * 16 + d + a
                         m[9 * a + 3 * b + e, d * 3 + r, col] = 1
-    return m.reshape(32, -1)
+    return m.reshape(27, -1)
 
 
 def place_second():
@@ -115,38 +116,101 @@
     return lax.rem(lax.axis_index("rows"), 2)
 
 
-def edges_kernel(carried, pick, even, odd):
-    even_side = 1 - parity()
-    pe = pick[even_side]
-    po = pick[1 - even_side]
-    both = jnp.concatenate([pe, po], axis=0)
-
-    def step(q, _):
-        c = carried[:, pl.ds(q * 16, 16), :].reshape(256, W)
-        v = dot(both, c).astype(BF)
-        even[pl.ds(4 * q, 4)] = v[:64].reshape(4, A, W)
-        odd[pl.ds(4 * q, 4)] = v[64:].reshape(4, A, W)
-        return 0
-
-    lax.fori_loop(0, carried.shape[1] // 16, step, 0, unroll=4)
-
-
-def prep_kernel(w1, w2, w3, w4, p1, p2, p3, ph, im, ie, tile, rep, bd, a1, a2, a3, ah, am, ae):
+def edge_pick(row):
+    m = lax.broadcasted_iota(jnp.int32, (4 * A, 256), 0)
+    n = lax.broadcasted_iota(jnp.int32, (4 * A, 256), 1)
+    want = (m % A) * 16 + (m // A) * R + row
+    return jnp.where(n == want, 1.0, 0.0).astype(BF)
+
+
+def edges_kernel(
+    carried, features, partner, pattern, valid,
+    even, odd, own, masks, right,
+    buf, sems, partner_s, pattern_s, valid_s, own_sem, small_sems,
+):
+    parts = sems.shape[0]
+    size = carried.shape[1] // parts
+    copies = []
+    for k in range(parts):
+        at = pl.ds(k * size, size)
+        copies.append(pltpu.make_async_copy(carried.at[:, at, :], buf.at[:, at, :], sems.at[k]))
+        copies[-1].start()
+    load_own = pltpu.make_async_copy(features, own, own_sem)
+    load_own.start()
+    small = [
+        pltpu.make_async_copy(a, b, small_sems.at[k])
+        for k, (a, b) in enumerate(((partner, partner_s), (pattern, pattern_s), (valid, valid_s)))
+    ]
+    for c in small:
+        c.start()
+    last = R - 1
+    even_row = jnp.where(parity() == 0, last, 0)
+    both = jnp.concatenate([edge_pick(even_row), edge_pick(last - even_row)], axis=0)
+    for q in range(carried.shape[1] // 16):
+        if q % (size // 16) == 0:
+            copies[q // (size // 16)].wait()
+        v = dot(both, buf[:, q * 16 : q * 16 + 16, :].reshape(256, W)).astype(BF)
+        even[4 * q : 4 * q + 4] = v[:64].reshape(4, A, W)
+        odd[4 * q : 4 * q + 4] = v[64:].reshape(4, A, W)
+    for c in small:
+        c.wait()
+    cam = lax.axis_index("cam")
+    flag = jnp.where(partner_s[cam] < cam, 1.0, 0.0)
+    right[...] = jnp.full((8, W), flag, F32)
+    line = lanes((DTILE, W)) // BLOCK_COLS
+    for r in range(R):
+        pixels = jnp.zeros((DTILE, W), F32)
+        for k in range(W // BLOCK_COLS):
+            pixels = jnp.where(line == k, valid_s[0, r, k].astype(F32), pixels)
+        for t in range(masks.shape[1] // DTILE):
+            masks[r, t * DTILE : (t + 1) * DTILE, :] = pixels * pattern_s[r, t].astype(F32)
+    load_own.wait()
+
+
+def ordered(w):
+    outs = []
+    v = w[...]
+    for e in range(3):
+        t = lax.broadcasted_iota(jnp.int32, (27, 9 * A), 0)
+        n = lax.broadcasted_iota(jnp.int32, (27, 9 * A), 1)
+        take = jnp.where(t == (n // A) * 3 + e, 1.0, 0.0).astype(BF)
+        spread = dot(v, take)
+        m = lax.broadcasted_iota(jnp.int32, spread.shape, 0)
+        n = lax.broadcasted_iota(jnp.int32, spread.shape, 1)
+        spread = jnp.where(m % A == n % A, spread, 0.0).astype(BF)
+        o = lax.broadcasted_iota(jnp.int32, (A, A * A), 0)
+        m = lax.broadcasted_iota(jnp.int32, (A, A * A), 1)
+        gather = jnp.where(m // A == o, 1.0, 0.0).astype(BF)
+        outs.append(dot(gather, spread).astype(BF))
+    return jnp.concatenate(outs, axis=0)
+
+
+def place_weights(w1, w2, w3, w4, p1, p2, p3, ph, im, ie, a1, a2, a3, ah, am, ae):
     v = dot(w1[...], p1[...]).astype(BF)
     for k in range(3 * T1):
         a1[pl.ds(k * A, A), :] = v[:, k * 256 : (k + 1) * 256]
-    v = dot(w2[...], p2[...]).astype(BF)
+    v = dot(ordered(w2), p2[...]).astype(BF)
     for k in range(4):
         a2[pl.ds(k * 48, 48), :] = v[:, k * 256 : (k + 1) * 256]
-    v = dot(w3[...], p3[...]).astype(BF)
+    third = ordered(w3)
+    v = dot(third, p3[...]).astype(BF)
     for k in range(2 * R):
         a3[pl.ds(k * 48, 48), :] = v[:, k * 256 : (k + 1) * 256]
     for side in range(2):
-        v = dot(ah_source(w3, side), ph[...]).astype(BF)
+        v = dot(ah_source(third, side), ph[...]).astype(BF)
         for k in range(T1):
             ah[side, pl.ds(k * 48, 48), :] = v[:, k * 256 : (k + 1) * 256]
-    t = dot(w4[...], tile[...]).astype(BF)
-    blocks = dot(rep[...], t).astype(BF) * bd[...]
+    m = lax.broadcasted_iota(jnp.int32, (432, 27), 0)
+    n = lax.broadcasted_iota(jnp.int32, (432, 27), 1)
+    tall = jnp.where(m % 27 == n, 1.0, 0.0).astype(BF)
+    tall = lax.dot_general(tall, w4[...], (((1,), (1,)), ((), ())), preferred_element_type=F32).astype(BF)
+    m = lax.broadcasted_iota(jnp.int32, (A, 256), 0)
+    n = lax.broadcasted_iota(jnp.int32, (A, 256), 1)
+    wide = jnp.where(n % A == m, 1.0, 0.0).astype(BF)
+    blocks = dot(tall, wide)
+    m = lax.broadcasted_iota(jnp.int32, (432, 256), 0)
+    n = lax.broadcasted_iota(jnp.int32, (432, 256), 1)
+    blocks = jnp.where(m // 27 == n // A, blocks, 0.0).astype(BF)
     am[...] = dot(im[...], blocks).astype(BF)
     for side in range(2):
         ae[side] = dot(ie[side], blocks).astype(BF)
@@ -154,13 +218,11 @@
 
 def ah_source(w3, side):
     b = 2 * side
-    v = w3[...]
-    return jnp.concatenate([v[:, (3 * a + b) * A : (3 * a + b + 1) * A] for a in range(3)], axis=1)
-
-
-def corr_kernel(own, mate, partner, pattern, valid, corr, even, odd):
-    cam = lax.axis_index("cam")
-    right = partner[cam] < cam
+    return jnp.concatenate([w3[:, (3 * a + b) * A : (3 * a + b + 1) * A] for a in range(3)], axis=1)
+
+
+def corr_kernel(own, mate, masks, right_ref, even_c, odd_c, corr, even, odd, even_out, odd_out):
+    right = right_ref[0:1, :] > 0.5
     disp = corr.shape[1]
     channels = own.shape[0] // R
     x, y = own[...], mate[...]
@@ -175,29 +237,36 @@
     rs = jnp.concatenate([jnp.where(row == r, right_side, zero) for r in range(R)], axis=1)
     s = dot(lt, rs)
     scale = 1.0 / np.sqrt(channels).astype(np.float32)
-    line = lanes((1, W)) // BLOCK_COLS
     for r in range(R):
         v = pltpu.roll(s[:, r * W : (r + 1) * W], 1, 1, stride=1, stride_axis=0)
         v = jnp.where(lane <= sub, v, 0.0).T[:disp] * scale
-        v = jnp.concatenate(
-            [v[t * DTILE : (t + 1) * DTILE] * pattern[r, t].astype(F32) for t in range(disp // DTILE)], axis=0
-        )
         v = dot(v.astype(BF), flip)
         v = jnp.where(right, v, pltpu.roll(v, 0, 1, stride=1, stride_axis=0))
-        pixels = jnp.zeros((1, W), F32)
-        for k in range(W // BLOCK_COLS):
-            pixels = jnp.where(line == k, valid[r, k].astype(F32), pixels)
-        corr[r] = (v * pixels).astype(BF)
+        corr[r] = (v * masks[r]).astype(BF)
     side = 1 - parity()
     even[...] = corr[pl.ds(side, 3)]
     odd[...] = corr[pl.ds(1 - side, 3)]
+    even_out[...] = even_c[...]
+    odd_out[...] = odd_c[...]
 
 
 def volume_kernel(
-    corr, even, odd, carried, a1, a2, a3, am, pick,
-    pre2, pre3, acc,
-    ext, cs, h1, h2, h3,
+    corr, even, odd, carried_hbm, pick_hbm,
+    w1_hbm, w2_hbm, w3_hbm, w4_hbm, p1_hbm, p2_hbm, p3_hbm, ph_hbm, im_hbm, ie_hbm,
+    pre2, pre3, main, ah, ae,
+    ext, cs, h1, h2, h3, acc, comb, a1, a2, a3, am,
+    carried, pick, w1, w2, w3, w4, p1, p2, p3, ph, im, ie, sems,
 ):
+    far = (w1_hbm, w2_hbm, w3_hbm, w4_hbm, p1_hbm, p2_hbm, p3_hbm, ph_hbm, im_hbm, ie_hbm, pick_hbm, carried_hbm)
+    near = (w1, w2, w3, w4, p1, p2, p3, ph, im, ie, pick, carried)
+    copies = [pltpu.make_async_copy(a, b, sems.at[k]) for k, (a, b) in enumerate(zip(far, near))]
+    for c in copies:
+        c.start()
+    for c in copies[:10]:
+        c.wait()
+    place_weights(w1, w2, w3, w4, p1, p2, p3, ph, im, ie, a1, a2, a3, ah, am, ae)
+    for c in copies[10:]:
+        c.wait()
     disp = corr.shape[1]
     bands = lax.axis_size("rows")
     me = lax.axis_index("rows")
@@ -248,7 +317,7 @@
     w2 = a2[...]
     sel = pick[...]
 
-    def second(i, _):
+    for i in range(disp // 4):
         c = carried[:, pl.ds(i * 16, 16), :].reshape(256, W)
         own = dot(sel, c)
         for g in range(3):
@@ -271,13 +340,10 @@
                             m = (dd * R + j - 1) * A
                             v = jnp.maximum(v + own[m : m + A], 0.0)
                             h2[4 * i + dd + 1, j - 1] = v.astype(BF)
-        return 0
-
-    lax.fori_loop(0, disp // 4, second, 0)
 
     w3 = a3[...]
 
-    def third(i, _):
+    for i in range(disp // 4):
         x = jnp.concatenate([h2[pl.ds(4 * i + 2 * h, 4)].reshape(256, W) for h in range(2)], axis=1)
         p = dot(w3, x)
         for h in range(2):
@@ -292,9 +358,6 @@
                         pre3[1, dd] = v
                     else:
                         h3[dd, r - 1] = jnp.maximum(v, 0.0).astype(BF)
-        return 0
-
-    lax.fori_loop(0, disp // 4, third, 0)
 
     acc[0:2] = jnp.zeros((2, 24, W), F32)
     w4 = am[...]
@@ -302,57 +365,82 @@
         p = dot(w4, h3[8 * k : 8 * k + 8].reshape(256, W)).reshape(10, 24, W)
         acc[8 * k : 8 * k + 2] += p[:2]
         acc[8 * k + 2 : 8 * k + 10] = p[2:]
-
-
-def edge_kernel(
-    even, odd, corr, pre2, pre3, acc_in, ah, ae,
-    main, part_even, part_odd,
-    acc, h2, h3, comb,
-):
-    disp = corr.shape[1]
-    bands = lax.axis_size("rows")
-    me = lax.axis_index("rows")
-    acc[...] = acc_in[...]
-    zero_row = jnp.zeros((A, W), BF)
-    starts = window_starts(disp)
-    for kind, carried in enumerate((even, odd)):
-        side = (1 - parity()) if kind == 0 else parity()
-        live = jnp.where(side == 0, me > 0, me < bands - 1).astype(F32)
-        h2[0] = zero_row
-        h2[disp + 1] = zero_row
-        v = jnp.maximum(pre2[side] + carried[...].astype(F32), 0.0) * live
-        h2[1 : disp + 1] = v.astype(BF)
-        w3 = ah[side]
-        for d0 in starts:
-            p = dot(w3, h2[d0 : d0 + 16].reshape(256, W))
-            for d in range(T1):
-                v = combine(p[d * 48 : d * 48 + 48]) + pre3[side, d0 + d]
-                h3[d0 + d] = jnp.maximum(v, 0.0).astype(BF)
-        w4 = ae[side]
-        for k in range(disp // 16):
-            p = dot(w4, h3[16 * k : 16 * k + 16].reshape(256, W)).reshape(18, 24, W)
-            acc[16 * k : 16 * k + 18] += p
-
+    sum_columns(acc, comb, disp)
+    for r in range(R):
+        main[r] = comb[pl.ds(r + 1, disp, stride=8), :] + corr[r].astype(F32)
+
+
+def sum_columns(acc, comb, disp):
     for d in range(disp):
         comb[d * 8 : d * 8 + 8, :] = shifted_sum(acc[d + 1, 0:8], acc[d + 1, 8:16], acc[d + 1, 16:24])
+
+
+def edge_rows(side, carried, pre2, pre3, ah, ae, acc, h2, h3, comb):
+    disp = carried.shape[0]
+    me = lax.axis_index("rows")
+    live = jnp.where(side == 0, me > 0, me < lax.axis_size("rows") - 1).astype(F32)
+    zero_row = jnp.zeros((A, W), BF)
+    h2[0] = zero_row
+    h2[disp + 1] = zero_row
+    v = jnp.maximum(pre2[...] + carried[...].astype(F32), 0.0) * live
+    h2[1 : disp + 1] = v.astype(BF)
+    w3 = ah[side]
+    for d0 in window_starts(disp):
+        p = dot(w3, h2[d0 : d0 + 16].reshape(256, W))
+        for d in range(T1):
+            v = combine(p[d * 48 : d * 48 + 48]) + pre3[d0 + d]
+            h3[d0 + d] = jnp.maximum(v, 0.0).astype(BF)
+    w4 = ae[side]
+    acc[0:2] = jnp.zeros((2, 24, W), F32)
+    for k in range(disp // 16):
+        p = dot(w4, h3[16 * k : 16 * k + 16].reshape(256, W)).reshape(18, 24, W)
+        acc[16 * k : 16 * k + 2] += p[:2]
+        acc[16 * k + 2 : 16 * k + 18] = p[2:]
+    sum_columns(acc, comb, disp)
+
+
+def first_kernel(carried, main_in, pre2, pre3, ah, ae, main, part, pre2_rest, pre3_rest, acc, h2, h3, comb):
+    disp = carried.shape[0]
+    side = parity()
+    edge_rows(side, carried, pre2.at[side], pre3.at[side], ah, ae, acc, h2, h3, comb)
+    main[...] = main_in[...]
+    for k in range(2):
+        main[2 * side + k] += comb[pl.ds(2 * side + 1 + k, disp, stride=8), :]
+    part[...] = comb[pl.ds(5 * side, disp, stride=8), :]
+    pre2_rest[...] = pre2[1 - side]
+    pre3_rest[...] = pre3[1 - side]
+
+
+def last_kernel(carried, main_in, received, pre2, pre3, ah, ae, main, part, acc, h2, h3, comb):
+    disp = carried.shape[0]
     side = 1 - parity()
+    edge_rows(side, carried, pre2, pre3, ah, ae, acc, h2, h3, comb)
     for r in range(R):
-        v = comb[pl.ds(r + 1, disp, stride=8), :] + corr[r].astype(F32)
+        v = main_in[r] + jnp.where(side == r // 2, comb[pl.ds(r + 1, disp, stride=8), :], 0.0)
+        if r in (0, R - 1):
+            v += jnp.where(side == r // 2, 0.0, received[...])
         main[pl.ds(r, disp, stride=R), :] = v
-    top = comb[pl.ds(0, disp, stride=8), :]
-    bottom = comb[pl.ds(5, disp, stride=8), :]
-    part_even[...] = jnp.where(side == 0, top, bottom)
-    part_odd[...] = jnp.where(side == 0, bottom, top)
-
-
-def call(kernel, outs, args, specs=None, scratch=(), us=2.0):
+    part[...] = comb[pl.ds(5 * side, disp, stride=8), :]
+
+
+def add_kernel(main, part, out):
+    disp = part.shape[0]
+    out[...] = main[...]
+    odd_band = parity() == 1
+    for r in (0, R - 1):
+        at = pl.ds(r, disp, stride=R)
+        mine = odd_band if r == 0 else jnp.logical_not(odd_band)
+        out[at, :] += jnp.where(mine, part[...], 0.0)
+
+
+def call(kernel, outs, args, specs=None, scratch=(), sems=0, us=2.0):
     return pl.pallas_call(
         kernel,
         out_shape=tuple(jax.ShapeDtypeStruct(s, d) for s, d in outs),
         in_specs=specs or [VM] * len(args),
         out_specs=tuple(VM for _ in outs),
-        scratch_shapes=[pltpu.VMEM(s, d) for s, d in scratch],
-        compiler_params=pltpu.CompilerParams(vmem_limit_bytes=40 * MIB),
+        scratch_shapes=[pltpu.VMEM(s, d) for s, d in scratch] + [pltpu.SemaphoreType.DMA((sems,))] * (sems > 0),
+        compiler_params=pltpu.CompilerParams(vmem_limit_bytes=24 * MIB),
         cost_estimate=pl.CostEstimate(flops=int(us * 1.1e9), bytes_accessed=1000, transcendentals=0),
     )(*args)
 
@@ -371,77 +459,89 @@
     own = features.reshape(channels * R, W)
     mate = lax.ppermute(own, "cam", [(i, i ^ 1) for i in range(cams)])
     flat = carried.reshape(A, disp * R, W)
-    pick = pick_carried()
-    ends = np.stack([pick[:, 0], pick[:, R - 1]]).reshape(2, 4 * A, 256)
     edge = ((disp, A, W), BF)
-    even_c, odd_c = call(edges_kernel, [edge, edge], [flat, bf(ends)], us=1.5)
-    even_c = swap(even_c, even_pairs)
-    odd_c = swap(odd_c, odd_pairs)
-
-    w1 = jnp.pad(w_first.T, ((0, 0), (0, 5)))
-    rows_of = lambda w: w.reshape(3, 3, 3, A, A).transpose(2, 3, 0, 1, 4).reshape(48, 9 * A)
-    w4 = jnp.pad(w_last, ((0, 5), (0, 0)))
-    tile = np.tile(np.eye(A), (1, 16))
-    rep = np.pad(np.tile(np.eye(27), (16, 1)), ((0, 0), (0, 5)))
-    mask = np.kron(np.eye(16), np.ones((27, A)))
-    ie = np.stack([place_last([0], 16), place_last([R - 1], 16)])
-    consts = [place_first(), place_second(), place_third(), place_halo(), place_last([1, 2], 8), ie, tile, rep, mask]
-    mats = [
-        ((T1 * 48, 256), BF),
-        ((192, 256), BF),
-        ((384, 256), BF),
-        ((2, T1 * 48, 256), BF),
-        ((240, 256), BF),
-        ((2, 432, 256), BF),
-    ]
-    a1, a2, a3, ah, am, ae = call(
-        prep_kernel, mats, [w1, rows_of(w_second), rows_of(w_third), w4] + [bf(c) for c in consts], us=1.5
-    )
+    parts = 4
+    even_c, odd_c, own, masks, right = pl.pallas_call(
+        edges_kernel,
+        out_shape=tuple(
+            jax.ShapeDtypeStruct(s, d)
+            for s, d in (edge, edge, (own.shape, BF), ((R, disp, W), F32), ((8, W), F32))
+        ),
+        in_specs=[HB] * 5,
+        out_specs=(VM,) * 5,
+        scratch_shapes=[
+            pltpu.VMEM(flat.shape, BF),
+            pltpu.SemaphoreType.DMA((parts,)),
+            pltpu.SMEM(partner.shape, jnp.int32),
+            pltpu.SMEM(pattern.shape, jnp.int32),
+            pltpu.SMEM(valid.shape, jnp.int32),
+            pltpu.SemaphoreType.DMA,
+            pltpu.SemaphoreType.DMA((3,)),
+        ],
+        compiler_params=pltpu.CompilerParams(vmem_limit_bytes=24 * MIB),
+        cost_estimate=pl.CostEstimate(flops=2 * 10**9, bytes_accessed=1000, transcendentals=0),
+    )(flat, own, partner, pattern, valid)
 
     rows3 = ((3, disp, W), BF)
-    corr, even_r, odd_r = call(
+    corr, even_r, odd_r, even_c, odd_c = call(
         corr_kernel,
-        [((R, disp, W), BF), rows3, rows3],
-        [own, mate, partner, pattern, valid[0]],
-        specs=[VM, VM, SM, SM, SM],
+        [((R, disp, W), BF), rows3, rows3, edge, edge],
+        [own, mate, masks, right, even_c, odd_c],
         us=2.0,
     )
+    odd_r = swap(odd_r, odd_pairs)
     even_r = swap(even_r, even_pairs)
-    odd_r = swap(odd_r, odd_pairs)
+    odd_c = swap(odd_c, odd_pairs)
+    even_c = swap(even_c, even_pairs)
+
+    by_tap = lambda w: w.transpose(1, 2, 0).reshape(A * A, 27)
+    ie = np.stack([place_last([0], 16), place_last([R - 1], 16)])
+    consts = [place_first(), place_second(), place_third(), place_halo(), place_last([1, 2], 8), ie]
+    far = [flat, bf(pick_carried().reshape(256, 256)), w_first.T, by_tap(w_second), by_tap(w_third), w_last.T]
+    far += [bf(c) for c in consts]
     pre = ((2, disp, A, W), F32)
-    pre2, pre3, acc = call(
+    rows = ((R, disp, W), F32)
+    line = ((disp, W), F32)
+    pre2, pre3, main, ah, ae = call(
         volume_kernel,
-        [pre, pre, ((disp + 2, 24, W), F32)],
-        [corr, even_r, odd_r, flat, a1, a2, a3, am, bf(pick.reshape(256, 256))],
+        [pre, pre, rows, ((2, T1 * 48, 256), BF), ((2, 432, 256), BF)],
+        [corr, even_r, odd_r] + far,
+        specs=[VM] * 3 + [HB] * len(far),
         scratch=[
             ((10, disp + 16, W), F32),
             ((len(window_starts(disp)), 512, W), BF),
             ((disp + 2, 8, A, W), BF),
             ((disp + 2, R, A, W), BF),
             ((disp, 2, A, W), BF),
-        ],
-        us=10.0,
+            ((disp + 2, 24, W), F32),
+            ((disp * 8, W), F32),
+            ((T1 * 48, 256), BF),
+            ((192, 256), BF),
+            ((384, 256), BF),
+            ((240, 256), BF),
+        ]
+        + [(x.shape, BF) for x in far],
+        sems=len(far),
+        us=8.0,
     )
-    main, part_even, part_odd = call(
-        edge_kernel,
-        [((disp * R, W), F32), ((disp, W), F32), ((disp, W), F32)],
-        [even_c, odd_c, corr, pre2, pre3, acc, ah, ae],
-        scratch=[
-            ((disp + 2, 24, W), F32),
-            ((disp + 2, A, W), BF),
-            ((disp, A, W), BF),
-            ((disp * 8, W), F32),
-        ],
-        us=4.0,
+    scratch = [
+        ((disp + 2, 24, W), F32),
+        ((disp + 2, A, W), BF),
+        ((disp, A, W), BF),
+        ((disp * 8, W), F32),
+    ]
+    half = ((disp, A, W), F32)
+    main, part, pre2, pre3 = call(
+        first_kernel, [rows, line, half, half], [odd_c, main, pre2, pre3, ah, ae], scratch=scratch, us=2.0
     )
-    part_even = swap(part_even, even_pairs)
-    part_odd = swap(part_odd, odd_pairs)
-    is_odd = lax.rem(lax.axis_index("rows"), 2) == 1
-    top = jnp.where(is_odd, part_even, part_odd)[:, None]
-    bottom = jnp.where(is_odd, part_odd, part_even)[:, None]
-    none = jnp.zeros((disp, R - 2, W), F32)
-    out = main.reshape(disp, R, W) + jnp.concatenate([top, none, bottom], axis=1)
-    return out[None]
+    part = swap(part, odd_pairs)
+    flat_rows = ((disp * R, W), F32)
+    main, part = call(
+        last_kernel, [flat_rows, line], [even_c, main, part, pre2, pre3, ah, ae], scratch=scratch, us=2.0
+    )
+    part = swap(part, even_pairs)
+    (out,) = call(add_kernel, [flat_rows], [main, part], us=0.3)
+    return out.reshape(1, disp, R, W)
 
 
 def solution(mesh):

time: 57.2 us -> 44.1 us (0.77)
  the two profiles are of different devices: /device:TPU:16 before, /device:TPU:0 now
where the time goes in v2:
time: 44.1 us; the launch traced here: 43.8 us
  Pallas kernels  17.2 us (39%)
  starting transfers between devices  16.8 us (38%)
  waiting for transfers between devices  5.18 us (12%)
  local copies, waits for them, and re-layouts  4.41 us (10%)
    ppermute x6, starting transfers between devices, swap(): return lax.ppermute(x, 'rows', pairs)  16.3 us
    pallas_call x5, Pallas kernels, call(): pl.pallas_call(kernel, out_shape=tuple((jax.ShapeDtypeStruct(s, d) for s,...  15.7 us
    ppermute x6, waiting for transfers between devices, swap(): return lax.ppermute(x, 'rows', pairs)  5.18 us
    unnamed x34, local copies, waits for them, and re-layouts  4.41 us
    pallas_call x1, Pallas kernels, local(): pl.pallas_call(edges_kernel, out_shape=tuple((jax.ShapeDtypeStruct(s, d)...  1.49 us
  transfers between devices with their start and end apart: 7, of which 2 were waited for; matrix products, arithmetic and copies ran while one was open for 0% of the time, Pallas kernels for 32%

profile of v2, /device:TPU:0, one launch (start us, length us, event | category | flops | bytes accessed | tf_op | source)
XLA Modules:
  0.0 43.8 jit_solution(7492038002233847875)
XLA Ops:
  0.0 0.5 %collective-permute-start = (bf16[512,128]{1,0:T(8,128)(2,1)}, bf16[512,128]{1,0:T(8,128)(2,1)S(1)}, u32[]{:S(2)}, u32[]{:S(2)}) collective-permute-start(bf16[512,128]{1,0:T(8,128)(2,1)} %bitcast.13), channel_id=1, source_target_pairs={{0,1},{1,0},{2,3},{3,2},{4,5},{5,4},{6,7},{7,6},{8,9},{9,8},{10,11... | collective-permute-start | bytes 393224 | tf_op jit(solution)/shard_map/ppermute | solution.py:460
  0.5 0.0 copy-start
  0.5 1.4 %copy-done = bf16[1,16,96,4,128]{4,3,2,1,0:T(4,128)(2,1)S(1)} copy-done((bf16[1,16,96,4,128]{4,3,2,1,0:T(4,128)(2,1)S(1)}, bf16[1,16,96,4,128]{4,3,2,1,0:T(4,128)(2,1)}, u32[]{:S(2)}) %copy-start) | copy-done | bytes 1572888
  1.9 0.0 copy-start.2
  1.9 0.9 %copy-done.2 = bf16[1,128,4,128]{3,2,1,0:T(4,128)(2,1)S(1)} copy-done((bf16[1,128,4,128]{3,2,1,0:T(4,128)(2,1)S(1)}, bf16[1,128,4,128]{3,2,1,0:T(4,128)(2,1)}, u32[]{:S(2)}) %copy-start.2) | copy-done | bytes 131096
  2.8 0.0 copy-start.7
  2.8 0.7 %copy-done.7 = s32[4,6]{1,0:T(4,128)S(1)} copy-done((s32[4,6]{1,0:T(4,128)S(1)}, s32[4,6]{1,0:T(4,128)}, u32[]{:S(2)}) %copy-start.7) | copy-done | bytes 120
  3.4 0.0 copy-start.8
  3.5 0.7 %copy-done.8 = s32[1,4,4]{2,1,0:T(4,128)S(1)} copy-done((s32[1,4,4]{2,1,0:T(4,128)S(1)}, s32[1,4,4]{2,1,0:T(4,128)}, u32[]{:S(2)}) %copy-start.8) | copy-done | bytes 88
  4.1 0.0 copy-start.9
  4.1 0.7 %copy-done.9 = s32[2]{0:T(128)S(1)} copy-done((s32[2]{0:T(128)S(1)}, s32[2]{0:T(128)}, u32[]{:S(2)}) %copy-start.9) | copy-done | bytes 32
  4.8 1.5 %shard_map.154 = (bf16[96,16,128]{2,1,0:T(8,128)(2,1)S(1)}, bf16[96,16,128]{2,1,0:T(8,128)(2,1)S(1)}, bf16[512,128]{1,0:T(8,128)(2,1)S(1)}, f32[4,96,128]{2,1,0:T(8,128)S(1)}, f32[8,128]{1,0:T(8,128)S(1)}) custom-call(bf16[16,384,128]{2,1,0:T(8,128)(2,1)S(1)} %bitcast.11, bf16[512,128]{1,0:T(8,128)(2,1)S(1)} %bitcast.14, s32[2]{0:T(128)S(1)} %copy-done.9, ...), custom_call_target="tpu_custom_call" | custom-call | flops 2000000000 | bytes 1000 | tf_op jit(solution)/shard_map/pallas_call | solution.py:464
  6.3 0.0 collective-permute-done.mate
  6.3 0.0 copy-start.1
  6.3 0.0 copy-start.3
  6.3 0.0 copy-start.4
  6.3 0.0 copy-start.5
  6.3 0.0 copy-start.6
  6.4 0.0 copy-start.10
  6.4 0.0 copy-start.11
  6.4 0.0 copy-start.12
  6.4 0.0 copy-start.13
  6.4 0.0 copy-start.14
  6.4 0.0 copy-start.15
  6.4 0.0 copy-start.16
  6.4 0.9 %shard_map.155 = (bf16[4,96,128]{2,1,0:T(8,128)(2,1)S(1)}, bf16[3,96,128]{2,1,0:T(8,128)(2,1)S(1)}, bf16[3,96,128]{2,1,0:T(8,128)(2,1)S(1)}, bf16[96,16,128]{2,1,0:T(8,128)(2,1)S(1)}, bf16[96,16,128]{2,1,0:T(8,128)(2,1)S(1)}) custom-call(bf16[512,128]{1,0:T(8,128)(2,1)S(1)} %get-tuple-element.26.own, bf16[512,128]{1,0:T(8,128)(2,1)S(1)} %collective-permute-done.mate, ...), custom_call_target="tpu_custom_call" | custom-call | flops 2200000000 | bytes 1000 | tf_op jit(solution)/shard_map/pallas_call | solution.py:437
  7.3 2.6 %collective-permute-start.3 = (bf16[3,96,128]{2,1,0:T(8,128)(2,1)S(1)}, bf16[3,96,128]{2,1,0:T(8,128)(2,1)S(1)}, u32[]{:S(2)}, u32[]{:S(2)}) collective-permute-start(bf16[3,96,128]{2,1,0:T(8,128)(2,1)S(1)} %get-tuple-element.34), channel_id=1, source_target_pairs={{0,2},{2,0},{4,6},{6,4},{8,10},{10,8},{12,14},{14,12},{1,3},{3,1},... | collective-permute-start | bytes 221192 | tf_op jit(solution)/shard_map/ppermute | solution.py:457
  9.9 0.7 %collective-permute-start.4 = (bf16[3,96,128]{2,1,0:T(8,128)(2,1)S(1)}, bf16[3,96,128]{2,1,0:T(8,128)(2,1)S(1)}, u32[]{:S(2)}, u32[]{:S(2)}) collective-permute-start(bf16[3,96,128]{2,1,0:T(8,128)(2,1)S(1)} %get-tuple-element.35), channel_id=1, source_target_pairs={{2,4},{4,2},{6,8},{8,6},{10,12},{12,10},{3,5},{5,3},{7,9},{9,7},{1... | collective-permute-start | bytes 221192 | tf_op jit(solution)/shard_map/ppermute | solution.py:457
  10.6 4.3 %collective-permute-start.1 = (bf16[96,16,128]{2,1,0:T(8,128)(2,1)S(1)}, bf16[96,16,128]{2,1,0:T(8,128)(2,1)S(1)}, u32[]{:S(2)}, u32[]{:S(2)}) collective-permute-start(bf16[96,16,128]{2,1,0:T(8,128)(2,1)S(1)} %get-tuple-element.31), channel_id=1, source_target_pairs={{0,2},{2,0},{4,6},{6,4},{8,10},{10,8},{12,14},{14,12},{1,3},{3,1},... | collective-permute-start | bytes 1179656 | tf_op jit(solution)/shard_map/ppermute | solution.py:457
  14.9 0.7 %collective-permute-start.2 = (bf16[96,16,128]{2,1,0:T(8,128)(2,1)S(1)}, bf16[96,16,128]{2,1,0:T(8,128)(2,1)S(1)}, u32[]{:S(2)}, u32[]{:S(2)}) collective-permute-start(bf16[96,16,128]{2,1,0:T(8,128)(2,1)S(1)} %get-tuple-element.32), channel_id=1, source_target_pairs={{2,4},{4,2},{6,8},{8,6},{10,12},{12,10},{3,5},{5,3},{7,9},{9,7},{1... | collective-permute-start | bytes 1179656 | tf_op jit(solution)/shard_map/ppermute | solution.py:457
  15.6 0.0 collective-permute-done.3.even
  15.6 0.0 collective-permute-done.4.odd
  15.6 0.0 copy-done.1
  15.6 0.0 copy-done.3
  15.6 0.0 copy-done.4
  15.6 0.0 copy-done.5
  15.6 0.0 copy-done.6
  15.7 0.0 copy-done.10
  15.7 0.0 copy-done.11
  15.7 0.0 copy-done.12
  15.7 0.0 copy-done.13
  15.7 0.0 copy-done.14
  15.7 0.0 copy-done.15
  15.7 0.0 copy-done.16
  15.7 10.6 %shard_map.156 = (f32[2,96,16,128]{3,2,1,0:T(8,128)S(1)}, f32[2,96,16,128]{3,2,1,0:T(8,128)S(1)}, f32[4,96,128]{2,1,0:T(8,128)S(1)}, bf16[2,672,256]{2,1,0:T(8,128)(2,1)S(1)}, bf16[2,432,256]{2,1,0:T(8,128)(2,1)S(1)}) custom-call(bf16[4,96,128]{2,1,0:T(8,128)(2,1)S(1)} %get-tuple-element.33.corr, bf16[3,96,128]{2,1,0:T(8,128)(2,1)S(1)} %collective-permute-done.3.even, ...), custom_call_target="tpu_custom_call" | custom-call | flops 8800000000 | bytes 1000 | tf_op jit(solution)/shard_map/pallas_call | solution.py:437
  26.3 0.0 collective-permute-done.2.carried
  26.3 1.8 %shard_map.157 = (f32[4,96,128]{2,1,0:T(8,128)S(1)}, f32[96,128]{1,0:T(8,128)S(1)}, f32[96,16,128]{2,1,0:T(8,128)S(1)}, f32[96,16,128]{2,1,0:T(8,128)S(1)}) custom-call(bf16[96,16,128]{2,1,0:T(8,128)(2,1)S(1)} %collective-permute-done.2.carried, f32[4,96,128]{2,1,0:T(8,128)S(1)} %get-tuple-element.36.main_in, f32[2,96,16,128]{3,2,1,0:T(8,128)S(1)} %get-tuple-element.37.pre2, ...), custom_call_target="tpu_custom_call" | custom-call | flops 2200000000 | bytes 1000 | tf_op jit(solution)/shard_map/pallas_call | solution.py:437
  28.1 0.7 %collective-permute-start.5 = (f32[96,128]{1,0:T(8,128)S(1)}, f32[96,128]{1,0:T(8,128)S(1)}, u32[]{:S(2)}, u32[]{:S(2)}) collective-permute-start(f32[96,128]{1,0:T(8,128)S(1)} %get-tuple-element.42), channel_id=1, source_target_pairs={{2,4},{4,2},{6,8},{8,6},{10,12},{12,10},{3,5},{5,3},{7,9},{9,7},{1... | collective-permute-start | bytes 147464 | tf_op jit(solution)/shard_map/ppermute | solution.py:457
  28.8 3.1 %collective-permute-done.1.carried = bf16[96,16,128]{2,1,0:T(8,128)(2,1)S(1)} collective-permute-done((bf16[96,16,128]{2,1,0:T(8,128)(2,1)S(1)}, bf16[96,16,128]{2,1,0:T(8,128)(2,1)S(1)}, u32[]{:S(2)}, u32[]{:S(2)}) %collective-permute-start.1) | collective-permute-done | bytes 393248 | tf_op jit(solution)/shard_map/ppermute | solution.py:457
  31.9 0.0 collective-permute-done.5.received
  31.9 1.7 %shard_map.158 = (f32[384,128]{1,0:T(8,128)S(1)}, f32[96,128]{1,0:T(8,128)S(1)}) custom-call(bf16[96,16,128]{2,1,0:T(8,128)(2,1)S(1)} %collective-permute-done.1.carried, f32[4,96,128]{2,1,0:T(8,128)S(1)} %get-tuple-element.41.main_in, f32[96,128]{1,0:T(8,128)S(1)} %collective-permute-done.5.received, f32[96,16,128]{2,1,0:T(8,128)S(1)} %get-tuple-element.43.pre2, ...), custom_call_target="tpu_custom_call" | custom-call | flops 2200000000 | bytes 1000 | tf_op jit(solution)/shard_map/pallas_call | solution.py:437
  33.6 7.4 %collective-permute-start.6 = (f32[96,128]{1,0:T(8,128)S(1)}, f32[96,128]{1,0:T(8,128)S(1)}, u32[]{:S(2)}, u32[]{:S(2)}) collective-permute-start(f32[96,128]{1,0:T(8,128)S(1)} %get-tuple-element.46), channel_id=1, source_target_pairs={{0,2},{2,0},{4,6},{6,4},{8,10},{10,8},{12,14},{14,12},{1,3},{3,1},... | collective-permute-start | bytes 147464 | tf_op jit(solution)/shard_map/ppermute | solution.py:457
  41.0 2.1 %collective-permute-done.6.part = f32[96,128]{1,0:T(8,128)S(1)} collective-permute-done((f32[96,128]{1,0:T(8,128)S(1)}, f32[96,128]{1,0:T(8,128)S(1)}, u32[]{:S(2)}, u32[]{:S(2)}) %collective-permute-start.6) | collective-permute-done | bytes 49184 | tf_op jit(solution)/shard_map/ppermute | solution.py:457
  43.1 0.7 %shard_map.159 = f32[384,128]{1,0:T(8,128)} custom-call(f32[384,128]{1,0:T(8,128)S(1)} %get-tuple-element.45.main, f32[96,128]{1,0:T(8,128)S(1)} %collective-permute-done.6.part), custom_call_target="tpu_custom_call" | custom-call | flops 330000000 | bytes 1000 | tf_op jit(solution)/shard_map/pallas_call | solution.py:437
Async XLA Ops:
  0.0 6.3 %collective-permute-start = (bf16[512,128]{1,0:T(8,128)(2,1)}, bf16[512,128]{1,0:T(8,128)(2,1)S(1)}, u32[]{:S(2)}, u32[]{:S(2)}) collective-permute-start(bf16[512,128]{1,0:T(8,128)(2,1)} %bitcast.13), channel_id=1, source_target_pairs={{0,1},{1,0},{2,3},{3,2},{4,5},{5,4},{6,7},{7,6},{8,9},{9,8},{10,11... | collective-permute-start | bytes 393224 | tf_op jit(solution)/shard_map/ppermute | solution.py:460
  0.5 1.4 %copy-start = (bf16[1,16,96,4,128]{4,3,2,1,0:T(4,128)(2,1)S(1)}, bf16[1,16,96,4,128]{4,3,2,1,0:T(4,128)(2,1)}, u32[]{:S(2)}) copy-start(bf16[1,16,96,4,128]{4,3,2,1,0:T(4,128)(2,1)} %param.20) | copy-start | bytes 4718596
  1.9 0.9 %copy-start.2 = (bf16[1,128,4,128]{3,2,1,0:T(4,128)(2,1)S(1)}, bf16[1,128,4,128]{3,2,1,0:T(4,128)(2,1)}, u32[]{:S(2)}) copy-start(bf16[1,128,4,128]{3,2,1,0:T(4,128)(2,1)} %param.16) | copy-start | bytes 393220
  2.8 0.7 %copy-start.7 = (s32[4,6]{1,0:T(4,128)S(1)}, s32[4,6]{1,0:T(4,128)}, u32[]{:S(2)}) copy-start(s32[4,6]{1,0:T(4,128)} %pattern.1) | copy-start | bytes 292
  3.4 0.7 %copy-start.8 = (s32[1,4,4]{2,1,0:T(4,128)S(1)}, s32[1,4,4]{2,1,0:T(4,128)}, u32[]{:S(2)}) copy-start(s32[1,4,4]{2,1,0:T(4,128)} %valid.1) | copy-start | bytes 196
  4.1 0.7 %copy-start.9 = (s32[2]{0:T(128)S(1)}, s32[2]{0:T(128)}, u32[]{:S(2)}) copy-start(s32[2]{0:T(128)} %partner.1) | copy-start | bytes 28
  6.3 9.3 %copy-start.1 = (bf16[1,16,96,4,128]{4,3,2,1,0:T(4,128)(2,1)S(1)}, bf16[1,16,96,4,128]{4,3,2,1,0:T(4,128)(2,1)}, u32[]{:S(2)}) copy-start(bf16[1,16,96,4,128]{4,3,2,1,0:T(4,128)(2,1)} %param.20) | copy-start | bytes 4718596
  6.3 9.3 %copy-start.3 = (bf16[27,16,16]{0,2,1:T(8,128)(2,1)S(1)}, bf16[27,16,16]{0,2,1:T(8,128)(2,1)}, u32[]{:S(2)}) copy-start(bf16[27,16,16]{0,2,1:T(8,128)(2,1)} %param.22) | copy-start | bytes 41476
  6.3 9.3 %copy-start.4 = (bf16[27,16,16]{0,2,1:T(8,128)(2,1)S(1)}, bf16[27,16,16]{0,2,1:T(8,128)(2,1)}, u32[]{:S(2)}) copy-start(bf16[27,16,16]{0,2,1:T(8,128)(2,1)} %param.23) | copy-start | bytes 41476
  6.3 9.3 %copy-start.5 = (bf16[27,16]{0,1:T(8,128)(2,1)S(1)}, bf16[27,16]{0,1:T(8,128)(2,1)}, u32[]{:S(2)}) copy-start(bf16[27,16]{0,1:T(8,128)(2,1)} %param.21) | copy-start | bytes 2596
  6.3 9.3 %copy-start.6 = (bf16[27,16]{0,1:T(8,128)(2,1)S(1)}, bf16[27,16]{0,1:T(8,128)(2,1)}, u32[]{:S(2)}) copy-start(bf16[27,16]{0,1:T(8,128)(2,1)} %param.24) | copy-start | bytes 2596
  6.4 9.3 %copy-start.10 = (bf16[2,432,432]{2,1,0:T(8,128)(2,1)S(1)}, bf16[2,432,432]{2,1,0:T(8,128)(2,1)}, u32[]{:S(2)}) copy-start(bf16[2,432,432]{2,1,0:T(8,128)(2,1)} %constant.20.clone.ie_hbm) | copy-start | bytes 2239492
  6.4 9.3 %copy-start.11 = (bf16[27,10752]{1,0:T(8,128)(2,1)S(1)}, bf16[27,10752]{1,0:T(8,128)(2,1)}, u32[]{:S(2)}) copy-start(bf16[27,10752]{1,0:T(8,128)(2,1)} %constant.15.clone.p1_hbm) | copy-start | bytes 1741828
  6.4 9.3 %copy-start.12 = (bf16[144,2048]{1,0:T(8,128)(2,1)S(1)}, bf16[144,2048]{1,0:T(8,128)(2,1)}, u32[]{:S(2)}) copy-start(bf16[144,2048]{1,0:T(8,128)(2,1)} %constant.17.clone.p3_hbm) | copy-start | bytes 1769476
  6.4 9.3 %copy-start.13 = (bf16[48,3584]{1,0:T(8,128)(2,1)S(1)}, bf16[48,3584]{1,0:T(8,128)(2,1)}, u32[]{:S(2)}) copy-start(bf16[48,3584]{1,0:T(8,128)(2,1)} %constant.18.clone.ph_hbm) | copy-start | bytes 1032196
  6.4 9.3 %copy-start.14 = (bf16[144,1024]{1,0:T(8,128)(2,1)S(1)}, bf16[144,1024]{1,0:T(8,128)(2,1)}, u32[]{:S(2)}) copy-start(bf16[144,1024]{1,0:T(8,128)(2,1)} %constant.16.clone.p2_hbm) | copy-start | bytes 884740
  6.4 9.3 %copy-start.15 = (bf16[240,432]{1,0:T(8,128)(2,1)S(1)}, bf16[240,432]{1,0:T(8,128)(2,1)}, u32[]{:S(2)}) copy-start(bf16[240,432]{1,0:T(8,128)(2,1)} %constant.19.clone.im_hbm) | copy-start | bytes 622084
  6.4 9.3 %copy-start.16 = (bf16[256,256]{1,0:T(8,128)(2,1)S(1)}, bf16[256,256]{1,0:T(8,128)(2,1)}, u32[]{:S(2)}) copy-start(bf16[256,256]{1,0:T(8,128)(2,1)} %constant.14.clone.pick_hbm) | copy-start | bytes 393220
  7.3 8.2 %collective-permute-start.3 = (bf16[3,96,128]{2,1,0:T(8,128)(2,1)S(1)}, bf16[3,96,128]{2,1,0:T(8,128)(2,1)S(1)}, u32[]{:S(2)}, u32[]{:S(2)}) collective-permute-start(bf16[3,96,128]{2,1,0:T(8,128)(2,1)S(1)} %get-tuple-element.34), channel_id=1, source_target_pairs={{0,2},{2,0},{4,6},{6,4},{8,10},{10,8},{12,14},{14,12},{1,3},{3,1},... | collective-permute-start | bytes 221192 | tf_op jit(solution)/shard_map/ppermute | solution.py:457
  9.9 5.7 %collective-permute-start.4 = (bf16[3,96,128]{2,1,0:T(8,128)(2,1)S(1)}, bf16[3,96,128]{2,1,0:T(8,128)(2,1)S(1)}, u32[]{:S(2)}, u32[]{:S(2)}) collective-permute-start(bf16[3,96,128]{2,1,0:T(8,128)(2,1)S(1)} %get-tuple-element.35), channel_id=1, source_target_pairs={{2,4},{4,2},{6,8},{8,6},{10,12},{12,10},{3,5},{5,3},{7,9},{9,7},{1... | collective-permute-start | bytes 221192 | tf_op jit(solution)/shard_map/ppermute | solution.py:457
  10.6 21.3 %collective-permute-start.1 = (bf16[96,16,128]{2,1,0:T(8,128)(2,1)S(1)}, bf16[96,16,128]{2,1,0:T(8,128)(2,1)S(1)}, u32[]{:S(2)}, u32[]{:S(2)}) collective-permute-start(bf16[96,16,128]{2,1,0:T(8,128)(2,1)S(1)} %get-tuple-element.31), channel_id=1, source_target_pairs={{0,2},{2,0},{4,6},{6,4},{8,10},{10,8},{12,14},{14,12},{1,3},{3,1},... | collective-permute-start | bytes 1179656 | tf_op jit(solution)/shard_map/ppermute | solution.py:457
  14.9 11.4 %collective-permute-start.2 = (bf16[96,16,128]{2,1,0:T(8,128)(2,1)S(1)}, bf16[96,16,128]{2,1,0:T(8,128)(2,1)S(1)}, u32[]{:S(2)}, u32[]{:S(2)}) collective-permute-start(bf16[96,16,128]{2,1,0:T(8,128)(2,1)S(1)} %get-tuple-element.32), channel_id=1, source_target_pairs={{2,4},{4,2},{6,8},{8,6},{10,12},{12,10},{3,5},{5,3},{7,9},{9,7},{1... | collective-permute-start | bytes 1179656 | tf_op jit(solution)/shard_map/ppermute | solution.py:457
  28.1 3.8 %collective-permute-start.5 = (f32[96,128]{1,0:T(8,128)S(1)}, f32[96,128]{1,0:T(8,128)S(1)}, u32[]{:S(2)}, u32[]{:S(2)}) collective-permute-start(f32[96,128]{1,0:T(8,128)S(1)} %get-tuple-element.42), channel_id=1, source_target_pairs={{2,4},{4,2},{6,8},{8,6},{10,12},{12,10},{3,5},{5,3},{7,9},{9,7},{1... | collective-permute-start | bytes 147464 | tf_op jit(solution)/shard_map/ppermute | solution.py:457
  33.6 9.5 %collective-permute-start.6 = (f32[96,128]{1,0:T(8,128)S(1)}, f32[96,128]{1,0:T(8,128)S(1)}, u32[]{:S(2)}, u32[]{:S(2)}) collective-permute-start(f32[96,128]{1,0:T(8,128)S(1)} %get-tuple-element.46), channel_id=1, source_target_pairs={{0,2},{2,0},{4,6},{6,4},{8,10},{10,8},{12,14},{14,12},{1,3},{3,1},... | collective-permute-start | bytes 147464 | tf_op jit(solution)/shard_map/ppermute | solution.py:457

commit v3 on v2

--- a/solution.py
+++ b/solution.py
@@ -14,6 +14,7 @@
 SM = pl.BlockSpec(memory_space=pltpu.SMEM)
 HB = pl.BlockSpec(memory_space=pltpu.HBM)
 MIB = 2**20
+EDGES, CORR, VOL, EDGE = 1.5, 1.5, 8.0, 2.0
 
 R, W, A = 4, 128, 16
 T1 = 14
@@ -123,48 +124,14 @@
     return jnp.where(n == want, 1.0, 0.0).astype(BF)
 
 
-def edges_kernel(
-    carried, features, partner, pattern, valid,
-    even, odd, own, masks, right,
-    buf, sems, partner_s, pattern_s, valid_s, own_sem, small_sems,
-):
-    parts = sems.shape[0]
-    size = carried.shape[1] // parts
-    copies = []
-    for k in range(parts):
-        at = pl.ds(k * size, size)
-        copies.append(pltpu.make_async_copy(carried.at[:, at, :], buf.at[:, at, :], sems.at[k]))
-        copies[-1].start()
-    load_own = pltpu.make_async_copy(features, own, own_sem)
-    load_own.start()
-    small = [
-        pltpu.make_async_copy(a, b, small_sems.at[k])
-        for k, (a, b) in enumerate(((partner, partner_s), (pattern, pattern_s), (valid, valid_s)))
-    ]
-    for c in small:
-        c.start()
+def edges_kernel(carried, even, odd):
     last = R - 1
     even_row = jnp.where(parity() == 0, last, 0)
     both = jnp.concatenate([edge_pick(even_row), edge_pick(last - even_row)], axis=0)
     for q in range(carried.shape[1] // 16):
-        if q % (size // 16) == 0:
-            copies[q // (size // 16)].wait()
-        v = dot(both, buf[:, q * 16 : q * 16 + 16, :].reshape(256, W)).astype(BF)
+        v = dot(both, carried[:, q * 16 : q * 16 + 16, :].reshape(256, W)).astype(BF)
         even[4 * q : 4 * q + 4] = v[:64].reshape(4, A, W)
         odd[4 * q : 4 * q + 4] = v[64:].reshape(4, A, W)
-    for c in small:
-        c.wait()
-    cam = lax.axis_index("cam")
-    flag = jnp.where(partner_s[cam] < cam, 1.0, 0.0)
-    right[...] = jnp.full((8, W), flag, F32)
-    line = lanes((DTILE, W)) // BLOCK_COLS
-    for r in range(R):
-        pixels = jnp.zeros((DTILE, W), F32)
-        for k in range(W // BLOCK_COLS):
-            pixels = jnp.where(line == k, valid_s[0, r, k].astype(F32), pixels)
-        for t in range(masks.shape[1] // DTILE):
-            masks[r, t * DTILE : (t + 1) * DTILE, :] = pixels * pattern_s[r, t].astype(F32)
-    load_own.wait()
 
 
 def ordered(w):
@@ -221,8 +188,10 @@
     return jnp.concatenate([w3[:, (3 * a + b) * A : (3 * a + b + 1) * A] for a in range(3)], axis=1)
 
 
-def corr_kernel(own, mate, masks, right_ref, even_c, odd_c, corr, even, odd, even_out, odd_out):
-    right = right_ref[0:1, :] > 0.5
+def corr_kernel(own, mate, partner, pattern, valid, even_c, odd_c, corr, even, odd, even_out, odd_out):
+    cam = lax.axis_index("cam")
+    right = partner[cam] < cam
+    line = lanes((1, W)) // BLOCK_COLS
     disp = corr.shape[1]
     channels = own.shape[0] // R
     x, y = own[...], mate[...]
@@ -240,9 +209,15 @@
     for r in range(R):
         v = pltpu.roll(s[:, r * W : (r + 1) * W], 1, 1, stride=1, stride_axis=0)
         v = jnp.where(lane <= sub, v, 0.0).T[:disp] * scale
+        v = jnp.concatenate(
+            [v[t * DTILE : (t + 1) * DTILE] * pattern[r, t].astype(F32) for t in range(disp // DTILE)], axis=0
+        )
         v = dot(v.astype(BF), flip)
         v = jnp.where(right, v, pltpu.roll(v, 0, 1, stride=1, stride_axis=0))
-        corr[r] = (v * masks[r]).astype(BF)
+        pixels = jnp.zeros((1, W), F32)
+        for k in range(W // BLOCK_COLS):
+            pixels = jnp.where(line == k, valid[r, k].astype(F32), pixels)
+        corr[r] = (v * pixels).astype(BF)
     side = 1 - parity()
     even[...] = corr[pl.ds(side, 3)]
     odd[...] = corr[pl.ds(1 - side, 3)]
@@ -250,23 +225,16 @@
     odd_out[...] = odd_c[...]
 
 
+def gate_kernel(a, token, out):
+    out[...] = a[...]
+
+
 def volume_kernel(
-    corr, even, odd, carried_hbm, pick_hbm,
-    w1_hbm, w2_hbm, w3_hbm, w4_hbm, p1_hbm, p2_hbm, p3_hbm, ph_hbm, im_hbm, ie_hbm,
+    corr, even, odd, carried, pick, w1, w2, w3, w4, p1, p2, p3, ph, im, ie,
     pre2, pre3, main, ah, ae,
     ext, cs, h1, h2, h3, acc, comb, a1, a2, a3, am,
-    carried, pick, w1, w2, w3, w4, p1, p2, p3, ph, im, ie, sems,
 ):
-    far = (w1_hbm, w2_hbm, w3_hbm, w4_hbm, p1_hbm, p2_hbm, p3_hbm, ph_hbm, im_hbm, ie_hbm, pick_hbm, carried_hbm)
-    near = (w1, w2, w3, w4, p1, p2, p3, ph, im, ie, pick, carried)
-    copies = [pltpu.make_async_copy(a, b, sems.at[k]) for k, (a, b) in enumerate(zip(far, near))]
-    for c in copies:
-        c.start()
-    for c in copies[:10]:
-        c.wait()
     place_weights(w1, w2, w3, w4, p1, p2, p3, ph, im, ie, a1, a2, a3, ah, am, ae)
-    for c in copies[10:]:
-        c.wait()
     disp = corr.shape[1]
     bands = lax.axis_size("rows")
     me = lax.axis_index("rows")
@@ -403,34 +371,32 @@
     disp = carried.shape[0]
     side = parity()
     edge_rows(side, carried, pre2.at[side], pre3.at[side], ah, ae, acc, h2, h3, comb)
-    main[...] = main_in[...]
-    for k in range(2):
-        main[2 * side + k] += comb[pl.ds(2 * side + 1 + k, disp, stride=8), :]
-    part[...] = comb[pl.ds(5 * side, disp, stride=8), :]
+    part[...] = comb[pl.ds(5 * side, disp, stride=8), :].astype(BF)
+    for r in range(R):
+        v = main_in[r] + jnp.where(side == r // 2, comb[pl.ds(r + 1, disp, stride=8), :], 0.0)
+        main[pl.ds(r, disp, stride=R), :] = v
     pre2_rest[...] = pre2[1 - side]
     pre3_rest[...] = pre3[1 - side]
 
 
-def last_kernel(carried, main_in, received, pre2, pre3, ah, ae, main, part, acc, h2, h3, comb):
+def last_kernel(carried, main_in, pre2, pre3, ah, ae, main, part, acc, h2, h3, comb):
     disp = carried.shape[0]
     side = 1 - parity()
+    main[...] = main_in[...]
     edge_rows(side, carried, pre2, pre3, ah, ae, acc, h2, h3, comb)
-    for r in range(R):
-        v = main_in[r] + jnp.where(side == r // 2, comb[pl.ds(r + 1, disp, stride=8), :], 0.0)
-        if r in (0, R - 1):
-            v += jnp.where(side == r // 2, 0.0, received[...])
-        main[pl.ds(r, disp, stride=R), :] = v
-    part[...] = comb[pl.ds(5 * side, disp, stride=8), :]
-
-
-def add_kernel(main, part, out):
-    disp = part.shape[0]
+    part[...] = comb[pl.ds(5 * side, disp, stride=8), :].astype(BF)
+    for k in range(2):
+        r = 2 * side + k
+        main[pl.ds(r, disp, stride=R), :] += comb[pl.ds(r + 1, disp, stride=8), :]
+
+
+def add_kernel(main, odd, even, out):
+    disp = odd.shape[0]
     out[...] = main[...]
-    odd_band = parity() == 1
-    for r in (0, R - 1):
-        at = pl.ds(r, disp, stride=R)
-        mine = odd_band if r == 0 else jnp.logical_not(odd_band)
-        out[at, :] += jnp.where(mine, part[...], 0.0)
+    side = parity()
+    for k, part in enumerate((odd, even)):
+        edge = side if k == 0 else 1 - side
+        out[pl.ds((R - 1) * edge, disp, stride=R), :] += part[...].astype(F32)
 
 
 def call(kernel, outs, args, specs=None, scratch=(), sems=0, us=2.0):
@@ -460,38 +426,18 @@
     mate = lax.ppermute(own, "cam", [(i, i ^ 1) for i in range(cams)])
     flat = carried.reshape(A, disp * R, W)
     edge = ((disp, A, W), BF)
-    parts = 4
-    even_c, odd_c, own, masks, right = pl.pallas_call(
-        edges_kernel,
-        out_shape=tuple(
-            jax.ShapeDtypeStruct(s, d)
-            for s, d in (edge, edge, (own.shape, BF), ((R, disp, W), F32), ((8, W), F32))
-        ),
-        in_specs=[HB] * 5,
-        out_specs=(VM,) * 5,
-        scratch_shapes=[
-            pltpu.VMEM(flat.shape, BF),
-            pltpu.SemaphoreType.DMA((parts,)),
-            pltpu.SMEM(partner.shape, jnp.int32),
-            pltpu.SMEM(pattern.shape, jnp.int32),
-            pltpu.SMEM(valid.shape, jnp.int32),
-            pltpu.SemaphoreType.DMA,
-            pltpu.SemaphoreType.DMA((3,)),
-        ],
-        compiler_params=pltpu.CompilerParams(vmem_limit_bytes=24 * MIB),
-        cost_estimate=pl.CostEstimate(flops=2 * 10**9, bytes_accessed=1000, transcendentals=0),
-    )(flat, own, partner, pattern, valid)
-
+    even_c, odd_c = call(edges_kernel, [edge, edge], [flat], us=EDGES)
     rows3 = ((3, disp, W), BF)
     corr, even_r, odd_r, even_c, odd_c = call(
         corr_kernel,
         [((R, disp, W), BF), rows3, rows3, edge, edge],
-        [own, mate, masks, right, even_c, odd_c],
-        us=2.0,
+        [own, mate, partner, pattern, valid[0], even_c, odd_c],
+        specs=[VM, VM, SM, SM, SM, VM, VM],
+        us=CORR,
     )
     odd_r = swap(odd_r, odd_pairs)
+    odd_c = swap(odd_c, odd_pairs)
     even_r = swap(even_r, even_pairs)
-    odd_c = swap(odd_c, odd_pairs)
     even_c = swap(even_c, even_pairs)
 
     by_tap = lambda w: w.transpose(1, 2, 0).reshape(A * A, 27)
@@ -501,12 +447,11 @@
     far += [bf(c) for c in consts]
     pre = ((2, disp, A, W), F32)
     rows = ((R, disp, W), F32)
-    line = ((disp, W), F32)
+    line = ((disp, W), BF)
     pre2, pre3, main, ah, ae = call(
         volume_kernel,
         [pre, pre, rows, ((2, T1 * 48, 256), BF), ((2, 432, 256), BF)],
         [corr, even_r, odd_r] + far,
-        specs=[VM] * 3 + [HB] * len(far),
         scratch=[
             ((10, disp + 16, W), F32),
             ((len(window_starts(disp)), 512, W), BF),
@@ -520,9 +465,7 @@
             ((384, 256), BF),
             ((240, 256), BF),
         ]
-        + [(x.shape, BF) for x in far],
-        sems=len(far),
-        us=8.0,
+        ,us=VOL,
     )
     scratch = [
         ((disp + 2, 24, W), F32),
@@ -531,16 +474,16 @@
         ((disp * 8, W), F32),
     ]
     half = ((disp, A, W), F32)
-    main, part, pre2, pre3 = call(
-        first_kernel, [rows, line, half, half], [odd_c, main, pre2, pre3, ah, ae], scratch=scratch, us=2.0
+    flat_rows = ((disp * R, W), F32)
+    main, odd_part, pre2, pre3 = call(
+        first_kernel, [flat_rows, line, half, half], [odd_c, main, pre2, pre3, ah, ae], scratch=scratch, us=EDGE
     )
-    part = swap(part, odd_pairs)
-    flat_rows = ((disp * R, W), F32)
-    main, part = call(
-        last_kernel, [flat_rows, line], [even_c, main, part, pre2, pre3, ah, ae], scratch=scratch, us=2.0
+    odd_part = swap(odd_part, odd_pairs)
+    main, even_part = call(
+        last_kernel, [flat_rows, line], [even_c, main, pre2, pre3, ah, ae], scratch=scratch, us=EDGE
     )
-    part = swap(part, even_pairs)
-    (out,) = call(add_kernel, [flat_rows], [main, part], us=0.3)
+    even_part = swap(even_part, even_pairs)
+    (out,) = call(add_kernel, [flat_rows], [main, odd_part, even_part], us=0.1)
     return out.reshape(1, disp, R, W)
 
 

time: 44.1 us -> 39.4 us (0.89)
  the two profiles are of different devices: /device:TPU:0 before, /device:TPU:16 now
where the time goes in v3:
time: 39.4 us; the launch traced here: 39.2 us
  Pallas kernels  14.9 us (38%)
  starting transfers between devices  12.3 us (31%)
  waiting for transfers between devices  9.96 us (25%)
  local copies, waits for them, and re-layouts  1.82 us (5%)
    pallas_call x6, Pallas kernels, call(): pl.pallas_call(kernel, out_shape=tuple((jax.ShapeDtypeStruct(s, d) for s,...  14.9 us
    ppermute x6, starting transfers between devices, swap(): return lax.ppermute(x, 'rows', pairs)  12.3 us
    ppermute x6, waiting for transfers between devices, swap(): return lax.ppermute(x, 'rows', pairs)  9.96 us
    unnamed x34, local copies, waits for them, and re-layouts  1.82 us
  transfers between devices with their start and end apart: 7, of which 4 were waited for; matrix products, arithmetic and copies ran while one was open for 0% of the time, Pallas kernels for 28%

profile of v3, /device:TPU:16, one launch (start us, length us, event | category | flops | bytes accessed | tf_op | source)
XLA Modules:
  0.0 39.2 jit_solution(8976637403916814619)
XLA Ops:
  0.0 0.0 collective-permute-start
  0.0 0.0 copy-start
  0.0 1.4 %copy-done = bf16[1,16,96,4,128]{4,3,2,1,0:T(4,128)(2,1)S(1)} copy-done((bf16[1,16,96,4,128]{4,3,2,1,0:T(4,128)(2,1)S(1)}, bf16[1,16,96,4,128]{4,3,2,1,0:T(4,128)(2,1)}, u32[]{:S(2)}) %copy-start) | copy-done | bytes 1572888
  1.4 0.0 copy-start.2
  1.4 0.0 copy-start.7
  1.4 0.0 copy-start.8
  1.4 0.0 copy-start.9
  1.4 0.6 %shard_map.154 = (bf16[96,16,128]{2,1,0:T(8,128)(2,1)S(1)}, bf16[96,16,128]{2,1,0:T(8,128)(2,1)S(1)}) custom-call(bf16[16,384,128]{2,1,0:T(8,128)(2,1)S(1)} %bitcast.12), custom_call_target="tpu_custom_call" | custom-call | flops 1650000000 | bytes 1000 | tf_op jit(solution)/shard_map/pallas_call | solution.py:403
  2.0 0.0 collective-permute-done.mate
  2.0 0.3 copy-done.2
  2.3 0.0 copy-done.7
  2.3 0.0 copy-done.8
  2.3 0.0 copy-done.9
  2.3 0.0 copy-start.1
  2.3 0.0 copy-start.3
  2.3 0.0 copy-start.4
  2.4 0.0 copy-start.5
  2.4 0.0 copy-start.6
  2.4 0.0 copy-start.10
  2.4 0.0 copy-start.11
  2.4 0.0 copy-start.12
  2.4 0.0 copy-start.13
  2.4 0.0 copy-start.14
  2.4 0.0 copy-start.15
  2.5 0.0 copy-start.16
  2.5 1.5 %shard_map.155 = (bf16[4,96,128]{2,1,0:T(8,128)(2,1)S(1)}, bf16[3,96,128]{2,1,0:T(8,128)(2,1)S(1)}, bf16[3,96,128]{2,1,0:T(8,128)(2,1)S(1)}, bf16[96,16,128]{2,1,0:T(8,128)(2,1)S(1)}, bf16[96,16,128]{2,1,0:T(8,128)(2,1)S(1)}) custom-call(bf16[512,128]{1,0:T(8,128)(2,1)S(1)} %bitcast.15, bf16[512,128]{1,0:T(8,128)(2,1)S(1)} %collective-permute-done.mate, ...), custom_call_target="tpu_custom_call" | custom-call | flops 1650000000 | bytes 1000 | tf_op jit(solution)/shard_map/pallas_call | solution.py:403
  4.0 1.6 %collective-permute-start.3 = (bf16[3,96,128]{2,1,0:T(8,128)(2,1)S(1)}, bf16[3,96,128]{2,1,0:T(8,128)(2,1)S(1)}, u32[]{:S(2)}, u32[]{:S(2)}) collective-permute-start(bf16[3,96,128]{2,1,0:T(8,128)(2,1)S(1)} %get-tuple-element.28), channel_id=1, source_target_pairs={{0,2},{2,0},{4,6},{6,4},{8,10},{10,8},{12,14},{14,12},{1,3},{3,1},... | collective-permute-start | bytes 221192 | tf_op jit(solution)/shard_map/ppermute | solution.py:423
  5.5 2.3 %collective-permute-start.4 = (bf16[3,96,128]{2,1,0:T(8,128)(2,1)S(1)}, bf16[3,96,128]{2,1,0:T(8,128)(2,1)S(1)}, u32[]{:S(2)}, u32[]{:S(2)}) collective-permute-start(bf16[3,96,128]{2,1,0:T(8,128)(2,1)S(1)} %get-tuple-element.29), channel_id=1, source_target_pairs={{2,4},{4,2},{6,8},{8,6},{10,12},{12,10},{3,5},{5,3},{7,9},{9,7},{1... | collective-permute-start | bytes 221192 | tf_op jit(solution)/shard_map/ppermute | solution.py:423
  7.8 2.7 %collective-permute-start.1 = (bf16[96,16,128]{2,1,0:T(8,128)(2,1)S(1)}, bf16[96,16,128]{2,1,0:T(8,128)(2,1)S(1)}, u32[]{:S(2)}, u32[]{:S(2)}) collective-permute-start(bf16[96,16,128]{2,1,0:T(8,128)(2,1)S(1)} %get-tuple-element.25), channel_id=1, source_target_pairs={{0,2},{2,0},{4,6},{6,4},{8,10},{10,8},{12,14},{14,12},{1,3},{3,1},... | collective-permute-start | bytes 1179656 | tf_op jit(solution)/shard_map/ppermute | solution.py:423
  10.5 1.9 %collective-permute-start.2 = (bf16[96,16,128]{2,1,0:T(8,128)(2,1)S(1)}, bf16[96,16,128]{2,1,0:T(8,128)(2,1)S(1)}, u32[]{:S(2)}, u32[]{:S(2)}) collective-permute-start(bf16[96,16,128]{2,1,0:T(8,128)(2,1)S(1)} %get-tuple-element.26), channel_id=1, source_target_pairs={{2,4},{4,2},{6,8},{8,6},{10,12},{12,10},{3,5},{5,3},{7,9},{9,7},{1... | collective-permute-start | bytes 1179656 | tf_op jit(solution)/shard_map/ppermute | solution.py:423
  12.4 0.0 collective-permute-done.3.even
  12.4 0.4 collective-permute-done.4.odd
  12.8 0.0 copy-done.1
  12.8 0.0 copy-done.3
  12.8 0.0 copy-done.4
  12.8 0.0 copy-done.5
  12.8 0.0 copy-done.6
  12.8 0.0 copy-done.10
  12.8 0.0 copy-done.11
  12.8 0.0 copy-done.12
  12.9 0.0 copy-done.13
  12.9 0.0 copy-done.14
  12.9 0.0 copy-done.15
  12.9 0.0 copy-done.16
  12.9 8.6 %shard_map.156 = (f32[2,96,16,128]{3,2,1,0:T(8,128)S(1)}, f32[2,96,16,128]{3,2,1,0:T(8,128)S(1)}, f32[4,96,128]{2,1,0:T(8,128)S(1)}, bf16[2,672,256]{2,1,0:T(8,128)(2,1)S(1)}, bf16[2,432,256]{2,1,0:T(8,128)(2,1)S(1)}) custom-call(bf16[4,96,128]{2,1,0:T(8,128)(2,1)S(1)} %get-tuple-element.27.corr, bf16[3,96,128]{2,1,0:T(8,128)(2,1)S(1)} %collective-permute-done.3.even, ...), custom_call_target="tpu_custom_call" | custom-call | flops 8800000000 | bytes 1000 | tf_op jit(solution)/shard_map/pallas_call | solution.py:403
  21.5 2.6 %collective-permute-done.2.carried = bf16[96,16,128]{2,1,0:T(8,128)(2,1)S(1)} collective-permute-done((bf16[96,16,128]{2,1,0:T(8,128)(2,1)S(1)}, bf16[96,16,128]{2,1,0:T(8,128)(2,1)S(1)}, u32[]{:S(2)}, u32[]{:S(2)}) %collective-permute-start.2) | collective-permute-done | bytes 393248 | tf_op jit(solution)/shard_map/ppermute | solution.py:423
  24.1 1.8 %shard_map.157 = (f32[384,128]{1,0:T(8,128)S(1)}, bf16[96,128]{1,0:T(8,128)(2,1)S(1)}, f32[96,16,128]{2,1,0:T(8,128)S(1)}, f32[96,16,128]{2,1,0:T(8,128)S(1)}) custom-call(bf16[96,16,128]{2,1,0:T(8,128)(2,1)S(1)} %collective-permute-done.2.carried, f32[4,96,128]{2,1,0:T(8,128)S(1)} %get-tuple-element.30.main_in, ...), custom_call_target="tpu_custom_call" | custom-call | flops 2200000000 | bytes 1000 | tf_op jit(solution)/shard_map/pallas_call | solution.py:403
  25.9 3.6 %collective-permute-done.1.carried = bf16[96,16,128]{2,1,0:T(8,128)(2,1)S(1)} collective-permute-done((bf16[96,16,128]{2,1,0:T(8,128)(2,1)S(1)}, bf16[96,16,128]{2,1,0:T(8,128)(2,1)S(1)}, u32[]{:S(2)}, u32[]{:S(2)}) %collective-permute-start.1) | collective-permute-done | bytes 393248 | tf_op jit(solution)/shard_map/ppermute | solution.py:423
  29.5 1.7 %shard_map.158 = (f32[384,128]{1,0:T(8,128)S(1)}, bf16[96,128]{1,0:T(8,128)(2,1)S(1)}) custom-call(bf16[96,16,128]{2,1,0:T(8,128)(2,1)S(1)} %collective-permute-done.1.carried, f32[384,128]{1,0:T(8,128)S(1)} %get-tuple-element.35.main_in, f32[96,16,128]{2,1,0:T(8,128)S(1)} %get-tuple-element.36.pre2, f32[96,16,128]{2,1,0:T(8,128)S(1)} %get-tuple-element.37.pre3, ...), custom_call_target="tpu_custom_call" | custom-call | flops 2200000000 | bytes 1000 | tf_op jit(solution)/shard_map/pallas_call | solution.py:403
  31.3 0.6 %collective-permute-start.6 = (bf16[96,128]{1,0:T(8,128)(2,1)S(1)}, bf16[96,128]{1,0:T(8,128)(2,1)S(1)}, u32[]{:S(2)}, u32[]{:S(2)}) collective-permute-start(bf16[96,128]{1,0:T(8,128)(2,1)S(1)} %get-tuple-element.40), channel_id=1, source_target_pairs={{0,2},{2,0},{4,6},{6,4},{8,10},{10,8},{12,14},{14,12},{1,3},{3,1},... | collective-permute-start | bytes 73736 | tf_op jit(solution)/shard_map/ppermute | solution.py:423
  31.9 3.2 %collective-permute-start.5 = (bf16[96,128]{1,0:T(8,128)(2,1)S(1)}, bf16[96,128]{1,0:T(8,128)(2,1)S(1)}, u32[]{:S(2)}, u32[]{:S(2)}) collective-permute-start(bf16[96,128]{1,0:T(8,128)(2,1)S(1)} %get-tuple-element.39), channel_id=1, source_target_pairs={{2,4},{4,2},{6,8},{8,6},{10,12},{12,10},{3,5},{5,3},{7,9},{9,7},{1... | collective-permute-start | bytes 73736 | tf_op jit(solution)/shard_map/ppermute | solution.py:423
  35.1 0.0 collective-permute-done.6.even
  35.2 3.3 %collective-permute-done.5.odd = bf16[96,128]{1,0:T(8,128)(2,1)S(1)} collective-permute-done((bf16[96,128]{1,0:T(8,128)(2,1)S(1)}, bf16[96,128]{1,0:T(8,128)(2,1)S(1)}, u32[]{:S(2)}, u32[]{:S(2)}) %collective-permute-start.5) | collective-permute-done | bytes 24608 | tf_op jit(solution)/shard_map/ppermute | solution.py:423
  38.5 0.7 %shard_map.159 = f32[384,128]{1,0:T(8,128)} custom-call(f32[384,128]{1,0:T(8,128)S(1)} %get-tuple-element.38.main, bf16[96,128]{1,0:T(8,128)(2,1)S(1)} %collective-permute-done.5.odd, bf16[96,128]{1,0:T(8,128)(2,1)S(1)} %collective-permute-done.6.even), custom_call_target="tpu_custom_call" | custom-call | flops 110000000 | bytes 1000 | tf_op jit(solution)/shard_map/pallas_call | solution.py:403
Async XLA Ops:
  0.0 2.0 %collective-permute-start = (bf16[512,128]{1,0:T(8,128)(2,1)}, bf16[512,128]{1,0:T(8,128)(2,1)S(1)}, u32[]{:S(2)}, u32[]{:S(2)}) collective-permute-start(bf16[512,128]{1,0:T(8,128)(2,1)} %bitcast.14), channel_id=1, source_target_pairs={{0,1},{1,0},{2,3},{3,2},{4,5},{5,4},{6,7},{7,6},{8,9},{9,8},{10,11... | collective-permute-start | bytes 393224 | tf_op jit(solution)/shard_map/ppermute | solution.py:426
  0.0 1.4 %copy-start = (bf16[1,16,96,4,128]{4,3,2,1,0:T(4,128)(2,1)S(1)}, bf16[1,16,96,4,128]{4,3,2,1,0:T(4,128)(2,1)}, u32[]{:S(2)}) copy-start(bf16[1,16,96,4,128]{4,3,2,1,0:T(4,128)(2,1)} %param.20) | copy-start | bytes 4718596
  1.4 0.9 %copy-start.2 = (bf16[1,128,4,128]{3,2,1,0:T(4,128)(2,1)S(1)}, bf16[1,128,4,128]{3,2,1,0:T(4,128)(2,1)}, u32[]{:S(2)}) copy-start(bf16[1,128,4,128]{3,2,1,0:T(4,128)(2,1)} %param.16) | copy-start | bytes 393220
  1.4 0.9 %copy-start.7 = (s32[4,6]{1,0:T(4,128)S(1)}, s32[4,6]{1,0:T(4,128)}, u32[]{:S(2)}) copy-start(s32[4,6]{1,0:T(4,128)} %pattern.1) | copy-start | bytes 292
  1.4 0.9 %copy-start.8 = (s32[1,4,4]{2,1,0:T(4,128)S(1)}, s32[1,4,4]{2,1,0:T(4,128)}, u32[]{:S(2)}) copy-start(s32[1,4,4]{2,1,0:T(4,128)} %param.19) | copy-start | bytes 196
  1.4 0.9 %copy-start.9 = (s32[2]{0:T(128)S(1)}, s32[2]{0:T(128)}, u32[]{:S(2)}) copy-start(s32[2]{0:T(128)} %partner.1) | copy-start | bytes 28
  2.3 10.5 %copy-start.1 = (bf16[1,16,96,4,128]{4,3,2,1,0:T(4,128)(2,1)S(1)}, bf16[1,16,96,4,128]{4,3,2,1,0:T(4,128)(2,1)}, u32[]{:S(2)}) copy-start(bf16[1,16,96,4,128]{4,3,2,1,0:T(4,128)(2,1)} %param.20) | copy-start | bytes 4718596
  2.3 10.5 %copy-start.3 = (bf16[27,16,16]{0,2,1:T(8,128)(2,1)S(1)}, bf16[27,16,16]{0,2,1:T(8,128)(2,1)}, u32[]{:S(2)}) copy-start(bf16[27,16,16]{0,2,1:T(8,128)(2,1)} %param.22) | copy-start | bytes 41476
  2.3 10.5 %copy-start.4 = (bf16[27,16,16]{0,2,1:T(8,128)(2,1)S(1)}, bf16[27,16,16]{0,2,1:T(8,128)(2,1)}, u32[]{:S(2)}) copy-start(bf16[27,16,16]{0,2,1:T(8,128)(2,1)} %param.23) | copy-start | bytes 41476
  2.4 10.5 %copy-start.5 = (bf16[27,16]{0,1:T(8,128)(2,1)S(1)}, bf16[27,16]{0,1:T(8,128)(2,1)}, u32[]{:S(2)}) copy-start(bf16[27,16]{0,1:T(8,128)(2,1)} %param.21) | copy-start | bytes 2596
  2.4 10.5 %copy-start.6 = (bf16[27,16]{0,1:T(8,128)(2,1)S(1)}, bf16[27,16]{0,1:T(8,128)(2,1)}, u32[]{:S(2)}) copy-start(bf16[27,16]{0,1:T(8,128)(2,1)} %param.24) | copy-start | bytes 2596
  2.4 10.4 %copy-start.10 = (bf16[2,432,432]{2,1,0:T(8,128)(2,1)S(1)}, bf16[2,432,432]{2,1,0:T(8,128)(2,1)}, u32[]{:S(2)}) copy-start(bf16[2,432,432]{2,1,0:T(8,128)(2,1)} %constant.20.clone.ie) | copy-start | bytes 2239492
  2.4 10.4 %copy-start.11 = (bf16[27,10752]{1,0:T(8,128)(2,1)S(1)}, bf16[27,10752]{1,0:T(8,128)(2,1)}, u32[]{:S(2)}) copy-start(bf16[27,10752]{1,0:T(8,128)(2,1)} %constant.15.clone.p1) | copy-start | bytes 1741828
  2.4 10.4 %copy-start.12 = (bf16[144,2048]{1,0:T(8,128)(2,1)S(1)}, bf16[144,2048]{1,0:T(8,128)(2,1)}, u32[]{:S(2)}) copy-start(bf16[144,2048]{1,0:T(8,128)(2,1)} %constant.17.clone.p3) | copy-start | bytes 1769476
  2.4 10.4 %copy-start.13 = (bf16[48,3584]{1,0:T(8,128)(2,1)S(1)}, bf16[48,3584]{1,0:T(8,128)(2,1)}, u32[]{:S(2)}) copy-start(bf16[48,3584]{1,0:T(8,128)(2,1)} %constant.18.clone.ph) | copy-start | bytes 1032196
  2.4 10.4 %copy-start.14 = (bf16[144,1024]{1,0:T(8,128)(2,1)S(1)}, bf16[144,1024]{1,0:T(8,128)(2,1)}, u32[]{:S(2)}) copy-start(bf16[144,1024]{1,0:T(8,128)(2,1)} %constant.16.clone.p2) | copy-start | bytes 884740
  2.4 10.4 %copy-start.15 = (bf16[240,432]{1,0:T(8,128)(2,1)S(1)}, bf16[240,432]{1,0:T(8,128)(2,1)}, u32[]{:S(2)}) copy-start(bf16[240,432]{1,0:T(8,128)(2,1)} %constant.19.clone.im) | copy-start | bytes 622084
  2.5 10.4 %copy-start.16 = (bf16[256,256]{1,0:T(8,128)(2,1)S(1)}, bf16[256,256]{1,0:T(8,128)(2,1)}, u32[]{:S(2)}) copy-start(bf16[256,256]{1,0:T(8,128)(2,1)} %constant.14.clone.pick) | copy-start | bytes 393220
  4.0 8.5 %collective-permute-start.3 = (bf16[3,96,128]{2,1,0:T(8,128)(2,1)S(1)}, bf16[3,96,128]{2,1,0:T(8,128)(2,1)S(1)}, u32[]{:S(2)}, u32[]{:S(2)}) collective-permute-start(bf16[3,96,128]{2,1,0:T(8,128)(2,1)S(1)} %get-tuple-element.28), channel_id=1, source_target_pairs={{0,2},{2,0},{4,6},{6,4},{8,10},{10,8},{12,14},{14,12},{1,3},{3,1},... | collective-permute-start | bytes 221192 | tf_op jit(solution)/shard_map/ppermute | solution.py:423
  5.5 7.3 %collective-permute-start.4 = (bf16[3,96,128]{2,1,0:T(8,128)(2,1)S(1)}, bf16[3,96,128]{2,1,0:T(8,128)(2,1)S(1)}, u32[]{:S(2)}, u32[]{:S(2)}) collective-permute-start(bf16[3,96,128]{2,1,0:T(8,128)(2,1)S(1)} %get-tuple-element.29), channel_id=1, source_target_pairs={{2,4},{4,2},{6,8},{8,6},{10,12},{12,10},{3,5},{5,3},{7,9},{9,7},{1... | collective-permute-start | bytes 221192 | tf_op jit(solution)/shard_map/ppermute | solution.py:423
  7.8 21.7 %collective-permute-start.1 = (bf16[96,16,128]{2,1,0:T(8,128)(2,1)S(1)}, bf16[96,16,128]{2,1,0:T(8,128)(2,1)S(1)}, u32[]{:S(2)}, u32[]{:S(2)}) collective-permute-start(bf16[96,16,128]{2,1,0:T(8,128)(2,1)S(1)} %get-tuple-element.25), channel_id=1, source_target_pairs={{0,2},{2,0},{4,6},{6,4},{8,10},{10,8},{12,14},{14,12},{1,3},{3,1},... | collective-permute-start | bytes 1179656 | tf_op jit(solution)/shard_map/ppermute | solution.py:423
  10.5 13.6 %collective-permute-start.2 = (bf16[96,16,128]{2,1,0:T(8,128)(2,1)S(1)}, bf16[96,16,128]{2,1,0:T(8,128)(2,1)S(1)}, u32[]{:S(2)}, u32[]{:S(2)}) collective-permute-start(bf16[96,16,128]{2,1,0:T(8,128)(2,1)S(1)} %get-tuple-element.26), channel_id=1, source_target_pairs={{2,4},{4,2},{6,8},{8,6},{10,12},{12,10},{3,5},{5,3},{7,9},{9,7},{1... | collective-permute-start | bytes 1179656 | tf_op jit(solution)/shard_map/ppermute | solution.py:423
  31.3 3.9 %collective-permute-start.6 = (bf16[96,128]{1,0:T(8,128)(2,1)S(1)}, bf16[96,128]{1,0:T(8,128)(2,1)S(1)}, u32[]{:S(2)}, u32[]{:S(2)}) collective-permute-start(bf16[96,128]{1,0:T(8,128)(2,1)S(1)} %get-tuple-element.40), channel_id=1, source_target_pairs={{0,2},{2,0},{4,6},{6,4},{8,10},{10,8},{12,14},{14,12},{1,3},{3,1},... | collective-permute-start | bytes 73736 | tf_op jit(solution)/shard_map/ppermute | solution.py:423
  31.9 6.6 %collective-permute-start.5 = (bf16[96,128]{1,0:T(8,128)(2,1)S(1)}, bf16[96,128]{1,0:T(8,128)(2,1)S(1)}, u32[]{:S(2)}, u32[]{:S(2)}) collective-permute-start(bf16[96,128]{1,0:T(8,128)(2,1)S(1)} %get-tuple-element.39), channel_id=1, source_target_pairs={{2,4},{4,2},{6,8},{8,6},{10,12},{12,10},{3,5},{5,3},{7,9},{9,7},{1... | collective-permute-start | bytes 73736 | tf_op jit(solution)/shard_map/ppermute | solution.py:423

commit v4 on v3

--- a/solution.py
+++ b/solution.py
@@ -371,7 +371,8 @@
     disp = carried.shape[0]
     side = parity()
     edge_rows(side, carried, pre2.at[side], pre3.at[side], ah, ae, acc, h2, h3, comb)
-    part[...] = comb[pl.ds(5 * side, disp, stride=8), :].astype(BF)
+    part[:disp] = comb[pl.ds(5 * side, disp, stride=8), :]
+    part[disp:] = jnp.zeros((part.shape[0] - disp, W), F32)
     for r in range(R):
         v = main_in[r] + jnp.where(side == r // 2, comb[pl.ds(r + 1, disp, stride=8), :], 0.0)
         main[pl.ds(r, disp, stride=R), :] = v
@@ -384,19 +385,19 @@
     side = 1 - parity()
     main[...] = main_in[...]
     edge_rows(side, carried, pre2, pre3, ah, ae, acc, h2, h3, comb)
-    part[...] = comb[pl.ds(5 * side, disp, stride=8), :].astype(BF)
+    part[...] = comb[pl.ds(5 * side, disp, stride=8), :]
     for k in range(2):
         r = 2 * side + k
         main[pl.ds(r, disp, stride=R), :] += comb[pl.ds(r + 1, disp, stride=8), :]
 
 
 def add_kernel(main, odd, even, out):
-    disp = odd.shape[0]
+    disp = even.shape[0]
     out[...] = main[...]
     side = parity()
     for k, part in enumerate((odd, even)):
         edge = side if k == 0 else 1 - side
-        out[pl.ds((R - 1) * edge, disp, stride=R), :] += part[...].astype(F32)
+        out[pl.ds((R - 1) * edge, disp, stride=R), :] += part[:disp]
 
 
 def call(kernel, outs, args, specs=None, scratch=(), sems=0, us=2.0):
@@ -447,7 +448,7 @@
     far += [bf(c) for c in consts]
     pre = ((2, disp, A, W), F32)
     rows = ((R, disp, W), F32)
-    line = ((disp, W), BF)
+    line = ((disp, W), F32)
     pre2, pre3, main, ah, ae = call(
         volume_kernel,
         [pre, pre, rows, ((2, T1 * 48, 256), BF), ((2, 432, 256), BF)],
@@ -476,7 +477,7 @@
     half = ((disp, A, W), F32)
     flat_rows = ((disp * R, W), F32)
     main, odd_part, pre2, pre3 = call(
-        first_kernel, [flat_rows, line, half, half], [odd_c, main, pre2, pre3, ah, ae], scratch=scratch, us=EDGE
+        first_kernel, [flat_rows, ((disp + 8, W), F32), half, half], [odd_c, main, pre2, pre3, ah, ae], scratch=scratch, us=EDGE
     )
     odd_part = swap(odd_part, odd_pairs)
     main, even_part = call(

time: 39.4 us -> 37.1 us (0.942)
  the two profiles are of different devices: /device:TPU:16 before, /device:TPU:0 now
where the time goes in v4:
time: 37.1 us; the launch traced here: 36.9 us
  Pallas kernels  14.9 us (40%)
  starting transfers between devices  12.9 us (35%)
  waiting for transfers between devices  7.11 us (19%)
  local copies, waits for them, and re-layouts  1.82 us (5%)
    pallas_call x6, Pallas kernels, call(): pl.pallas_call(kernel, out_shape=tuple((jax.ShapeDtypeStruct(s, d) for s,...  14.9 us
    ppermute x6, starting transfers between devices, swap(): return lax.ppermute(x, 'rows', pairs)  12.4 us
    ppermute x6, waiting for transfers between devices, swap(): return lax.ppermute(x, 'rows', pairs)  7.11 us
    unnamed x34, local copies, waits for them, and re-layouts  1.82 us
  transfers between devices with their start and end apart: 7, of which 2 were waited for; matrix products, arithmetic and copies ran while one was open for 0% of the time, Pallas kernels for 34%

profile of v4, /device:TPU:0, one launch (start us, length us, event | category | flops | bytes accessed | tf_op | source)
XLA Modules:
  0.0 36.9 jit_solution(3616889975958624747)
XLA Ops:
  0.0 0.5 %collective-permute-start = (bf16[512,128]{1,0:T(8,128)(2,1)}, bf16[512,128]{1,0:T(8,128)(2,1)S(1)}, u32[]{:S(2)}, u32[]{:S(2)}) collective-permute-start(bf16[512,128]{1,0:T(8,128)(2,1)} %bitcast.14), channel_id=1, source_target_pairs={{0,1},{1,0},{2,3},{3,2},{4,5},{5,4},{6,7},{7,6},{8,9},{9,8},{10,11... | collective-permute-start | bytes 393224 | tf_op jit(solution)/shard_map/ppermute | solution.py:427
  0.5 0.0 copy-start
  0.5 1.4 %copy-done = bf16[1,16,96,4,128]{4,3,2,1,0:T(4,128)(2,1)S(1)} copy-done((bf16[1,16,96,4,128]{4,3,2,1,0:T(4,128)(2,1)S(1)}, bf16[1,16,96,4,128]{4,3,2,1,0:T(4,128)(2,1)}, u32[]{:S(2)}) %copy-start) | copy-done | bytes 1572888
  1.9 0.0 copy-start.2
  1.9 0.0 copy-start.7
  1.9 0.0 copy-start.8
  1.9 0.0 copy-start.9
  1.9 0.6 %shard_map.154 = (bf16[96,16,128]{2,1,0:T(8,128)(2,1)S(1)}, bf16[96,16,128]{2,1,0:T(8,128)(2,1)S(1)}) custom-call(bf16[16,384,128]{2,1,0:T(8,128)(2,1)S(1)} %bitcast.12), custom_call_target="tpu_custom_call" | custom-call | flops 1650000000 | bytes 1000 | tf_op jit(solution)/shard_map/pallas_call | solution.py:404
  2.4 0.0 collective-permute-done.mate
  2.4 0.3 copy-done.2
  2.8 0.0 copy-done.7
  2.8 0.0 copy-done.8
  2.8 0.0 copy-done.9
  2.8 0.0 copy-start.1
  2.8 0.0 copy-start.3
  2.8 0.0 copy-start.4
  2.8 0.0 copy-start.5
  2.8 0.0 copy-start.6
  2.8 0.0 copy-start.10
  2.8 0.0 copy-start.11
  2.9 0.0 copy-start.12
  2.9 0.0 copy-start.13
  2.9 0.0 copy-start.14
  2.9 0.0 copy-start.15
  2.9 0.0 copy-start.16
  2.9 1.5 %shard_map.155 = (bf16[4,96,128]{2,1,0:T(8,128)(2,1)S(1)}, bf16[3,96,128]{2,1,0:T(8,128)(2,1)S(1)}, bf16[3,96,128]{2,1,0:T(8,128)(2,1)S(1)}, bf16[96,16,128]{2,1,0:T(8,128)(2,1)S(1)}, bf16[96,16,128]{2,1,0:T(8,128)(2,1)S(1)}) custom-call(bf16[512,128]{1,0:T(8,128)(2,1)S(1)} %bitcast.15, bf16[512,128]{1,0:T(8,128)(2,1)S(1)} %collective-permute-done.mate, ...), custom_call_target="tpu_custom_call" | custom-call | flops 1650000000 | bytes 1000 | tf_op jit(solution)/shard_map/pallas_call | solution.py:404
  4.4 2.6 %collective-permute-start.3 = (bf16[3,96,128]{2,1,0:T(8,128)(2,1)S(1)}, bf16[3,96,128]{2,1,0:T(8,128)(2,1)S(1)}, u32[]{:S(2)}, u32[]{:S(2)}) collective-permute-start(bf16[3,96,128]{2,1,0:T(8,128)(2,1)S(1)} %get-tuple-element.28), channel_id=1, source_target_pairs={{0,2},{2,0},{4,6},{6,4},{8,10},{10,8},{12,14},{14,12},{1,3},{3,1},... | collective-permute-start | bytes 221192 | tf_op jit(solution)/shard_map/ppermute | solution.py:424
  7.0 0.7 %collective-permute-start.4 = (bf16[3,96,128]{2,1,0:T(8,128)(2,1)S(1)}, bf16[3,96,128]{2,1,0:T(8,128)(2,1)S(1)}, u32[]{:S(2)}, u32[]{:S(2)}) collective-permute-start(bf16[3,96,128]{2,1,0:T(8,128)(2,1)S(1)} %get-tuple-element.29), channel_id=1, source_target_pairs={{2,4},{4,2},{6,8},{8,6},{10,12},{12,10},{3,5},{5,3},{7,9},{9,7},{1... | collective-permute-start | bytes 221192 | tf_op jit(solution)/shard_map/ppermute | solution.py:424
  7.6 4.3 %collective-permute-start.1 = (bf16[96,16,128]{2,1,0:T(8,128)(2,1)S(1)}, bf16[96,16,128]{2,1,0:T(8,128)(2,1)S(1)}, u32[]{:S(2)}, u32[]{:S(2)}) collective-permute-start(bf16[96,16,128]{2,1,0:T(8,128)(2,1)S(1)} %get-tuple-element.25), channel_id=1, source_target_pairs={{0,2},{2,0},{4,6},{6,4},{8,10},{10,8},{12,14},{14,12},{1,3},{3,1},... | collective-permute-start | bytes 1179656 | tf_op jit(solution)/shard_map/ppermute | solution.py:424
  12.0 0.7 %collective-permute-start.2 = (bf16[96,16,128]{2,1,0:T(8,128)(2,1)S(1)}, bf16[96,16,128]{2,1,0:T(8,128)(2,1)S(1)}, u32[]{:S(2)}, u32[]{:S(2)}) collective-permute-start(bf16[96,16,128]{2,1,0:T(8,128)(2,1)S(1)} %get-tuple-element.26), channel_id=1, source_target_pairs={{2,4},{4,2},{6,8},{8,6},{10,12},{12,10},{3,5},{5,3},{7,9},{9,7},{1... | collective-permute-start | bytes 1179656 | tf_op jit(solution)/shard_map/ppermute | solution.py:424
  12.7 0.0 collective-permute-done.3.even
  12.7 0.0 collective-permute-done.4.odd
  12.7 0.0 copy-done.1
  12.7 0.0 copy-done.3
  12.7 0.0 copy-done.4
  12.7 0.0 copy-done.5
  12.7 0.0 copy-done.6
  12.7 0.0 copy-done.10
  12.7 0.0 copy-done.11
  12.7 0.0 copy-done.12
  12.8 0.0 copy-done.13
  12.8 0.0 copy-done.14
  12.8 0.0 copy-done.15
  12.8 0.0 copy-done.16
  12.8 8.6 %shard_map.156 = (f32[2,96,16,128]{3,2,1,0:T(8,128)S(1)}, f32[2,96,16,128]{3,2,1,0:T(8,128)S(1)}, f32[4,96,128]{2,1,0:T(8,128)S(1)}, bf16[2,672,256]{2,1,0:T(8,128)(2,1)S(1)}, bf16[2,432,256]{2,1,0:T(8,128)(2,1)S(1)}) custom-call(bf16[4,96,128]{2,1,0:T(8,128)(2,1)S(1)} %get-tuple-element.27.corr, bf16[3,96,128]{2,1,0:T(8,128)(2,1)S(1)} %collective-permute-done.3.even, ...), custom_call_target="tpu_custom_call" | custom-call | flops 8800000000 | bytes 1000 | tf_op jit(solution)/shard_map/pallas_call | solution.py:404
  21.4 0.0 collective-permute-done.2.carried
  21.4 1.8 %shard_map.157 = (f32[384,128]{1,0:T(8,128)S(1)}, f32[104,128]{1,0:T(8,128)S(1)}, f32[96,16,128]{2,1,0:T(8,128)S(1)}, f32[96,16,128]{2,1,0:T(8,128)S(1)}) custom-call(bf16[96,16,128]{2,1,0:T(8,128)(2,1)S(1)} %collective-permute-done.2.carried, f32[4,96,128]{2,1,0:T(8,128)S(1)} %get-tuple-element.30.main_in, f32[2,96,16,128]{3,2,1,0:T(8,128)S(1)} %get-tuple-element.31.pre2, ...), custom_call_target="tpu_custom_call" | custom-call | flops 2200000000 | bytes 1000 | tf_op jit(solution)/shard_map/pallas_call | solution.py:404
  23.2 0.7 %collective-permute-start.5 = (f32[104,128]{1,0:T(8,128)S(1)}, f32[104,128]{1,0:T(8,128)S(1)}, u32[]{:S(2)}, u32[]{:S(2)}) collective-permute-start(f32[104,128]{1,0:T(8,128)S(1)} %get-tuple-element.39), channel_id=1, source_target_pairs={{2,4},{4,2},{6,8},{8,6},{10,12},{12,10},{3,5},{5,3},{7,9},{9,7},{1... | collective-permute-start | bytes 159752 | tf_op jit(solution)/shard_map/ppermute | solution.py:424
  23.9 5.0 %collective-permute-done.1.carried = bf16[96,16,128]{2,1,0:T(8,128)(2,1)S(1)} collective-permute-done((bf16[96,16,128]{2,1,0:T(8,128)(2,1)S(1)}, bf16[96,16,128]{2,1,0:T(8,128)(2,1)S(1)}, u32[]{:S(2)}, u32[]{:S(2)}) %collective-permute-start.1) | collective-permute-done | bytes 393248 | tf_op jit(solution)/shard_map/ppermute | solution.py:424
  28.9 1.7 %shard_map.158 = (f32[384,128]{1,0:T(8,128)S(1)}, f32[96,128]{1,0:T(8,128)S(1)}) custom-call(bf16[96,16,128]{2,1,0:T(8,128)(2,1)S(1)} %collective-permute-done.1.carried, f32[384,128]{1,0:T(8,128)S(1)} %get-tuple-element.35.main_in, f32[96,16,128]{2,1,0:T(8,128)S(1)} %get-tuple-element.36.pre2, f32[96,16,128]{2,1,0:T(8,128)S(1)} %get-tuple-element.37.pre3, ...), custom_call_target="tpu_custom_call" | custom-call | flops 2200000000 | bytes 1000 | tf_op jit(solution)/shard_map/pallas_call | solution.py:404
  30.6 3.5 %collective-permute-start.6 = (f32[96,128]{1,0:T(8,128)S(1)}, f32[96,128]{1,0:T(8,128)S(1)}, u32[]{:S(2)}, u32[]{:S(2)}) collective-permute-start(f32[96,128]{1,0:T(8,128)S(1)} %get-tuple-element.40), channel_id=1, source_target_pairs={{0,2},{2,0},{4,6},{6,4},{8,10},{10,8},{12,14},{14,12},{1,3},{3,1},... | collective-permute-start | bytes 147464 | tf_op jit(solution)/shard_map/ppermute | solution.py:424
  34.2 2.1 %collective-permute-done.6.even = f32[96,128]{1,0:T(8,128)S(1)} collective-permute-done((f32[96,128]{1,0:T(8,128)S(1)}, f32[96,128]{1,0:T(8,128)S(1)}, u32[]{:S(2)}, u32[]{:S(2)}) %collective-permute-start.6) | collective-permute-done | bytes 49184 | tf_op jit(solution)/shard_map/ppermute | solution.py:424
  36.2 0.0 collective-permute-done.5.odd
  36.2 0.7 %shard_map.159 = f32[384,128]{1,0:T(8,128)} custom-call(f32[384,128]{1,0:T(8,128)S(1)} %get-tuple-element.38.main, f32[104,128]{1,0:T(8,128)S(1)} %collective-permute-done.5.odd, f32[96,128]{1,0:T(8,128)S(1)} %collective-permute-done.6.even), custom_call_target="tpu_custom_call" | custom-call | flops 110000000 | bytes 1000 | tf_op jit(solution)/shard_map/pallas_call | solution.py:404
Async XLA Ops:
  0.0 2.4 %collective-permute-start = (bf16[512,128]{1,0:T(8,128)(2,1)}, bf16[512,128]{1,0:T(8,128)(2,1)S(1)}, u32[]{:S(2)}, u32[]{:S(2)}) collective-permute-start(bf16[512,128]{1,0:T(8,128)(2,1)} %bitcast.14), channel_id=1, source_target_pairs={{0,1},{1,0},{2,3},{3,2},{4,5},{5,4},{6,7},{7,6},{8,9},{9,8},{10,11... | collective-permute-start | bytes 393224 | tf_op jit(solution)/shard_map/ppermute | solution.py:427
  0.5 1.4 %copy-start = (bf16[1,16,96,4,128]{4,3,2,1,0:T(4,128)(2,1)S(1)}, bf16[1,16,96,4,128]{4,3,2,1,0:T(4,128)(2,1)}, u32[]{:S(2)}) copy-start(bf16[1,16,96,4,128]{4,3,2,1,0:T(4,128)(2,1)} %param.20) | copy-start | bytes 4718596
  1.9 0.9 %copy-start.2 = (bf16[1,128,4,128]{3,2,1,0:T(4,128)(2,1)S(1)}, bf16[1,128,4,128]{3,2,1,0:T(4,128)(2,1)}, u32[]{:S(2)}) copy-start(bf16[1,128,4,128]{3,2,1,0:T(4,128)(2,1)} %param.16) | copy-start | bytes 393220
  1.9 0.9 %copy-start.7 = (s32[4,6]{1,0:T(4,128)S(1)}, s32[4,6]{1,0:T(4,128)}, u32[]{:S(2)}) copy-start(s32[4,6]{1,0:T(4,128)} %pattern.1) | copy-start | bytes 292
  1.9 0.9 %copy-start.8 = (s32[1,4,4]{2,1,0:T(4,128)S(1)}, s32[1,4,4]{2,1,0:T(4,128)}, u32[]{:S(2)}) copy-start(s32[1,4,4]{2,1,0:T(4,128)} %param.19) | copy-start | bytes 196
  1.9 0.9 %copy-start.9 = (s32[2]{0:T(128)S(1)}, s32[2]{0:T(128)}, u32[]{:S(2)}) copy-start(s32[2]{0:T(128)} %partner.1) | copy-start | bytes 28
  2.8 9.9 %copy-start.1 = (bf16[1,16,96,4,128]{4,3,2,1,0:T(4,128)(2,1)S(1)}, bf16[1,16,96,4,128]{4,3,2,1,0:T(4,128)(2,1)}, u32[]{:S(2)}) copy-start(bf16[1,16,96,4,128]{4,3,2,1,0:T(4,128)(2,1)} %param.20) | copy-start | bytes 4718596
  2.8 9.9 %copy-start.3 = (bf16[27,16,16]{0,2,1:T(8,128)(2,1)S(1)}, bf16[27,16,16]{0,2,1:T(8,128)(2,1)}, u32[]{:S(2)}) copy-start(bf16[27,16,16]{0,2,1:T(8,128)(2,1)} %param.22) | copy-start | bytes 41476
  2.8 9.9 %copy-start.4 = (bf16[27,16,16]{0,2,1:T(8,128)(2,1)S(1)}, bf16[27,16,16]{0,2,1:T(8,128)(2,1)}, u32[]{:S(2)}) copy-start(bf16[27,16,16]{0,2,1:T(8,128)(2,1)} %param.23) | copy-start | bytes 41476
  2.8 9.9 %copy-start.5 = (bf16[27,16]{0,1:T(8,128)(2,1)S(1)}, bf16[27,16]{0,1:T(8,128)(2,1)}, u32[]{:S(2)}) copy-start(bf16[27,16]{0,1:T(8,128)(2,1)} %param.21) | copy-start | bytes 2596
  2.8 9.9 %copy-start.6 = (bf16[27,16]{0,1:T(8,128)(2,1)S(1)}, bf16[27,16]{0,1:T(8,128)(2,1)}, u32[]{:S(2)}) copy-start(bf16[27,16]{0,1:T(8,128)(2,1)} %param.24) | copy-start | bytes 2596
  2.8 9.9 %copy-start.10 = (bf16[2,432,432]{2,1,0:T(8,128)(2,1)S(1)}, bf16[2,432,432]{2,1,0:T(8,128)(2,1)}, u32[]{:S(2)}) copy-start(bf16[2,432,432]{2,1,0:T(8,128)(2,1)} %constant.20.clone.ie) | copy-start | bytes 2239492
  2.8 9.9 %copy-start.11 = (bf16[27,10752]{1,0:T(8,128)(2,1)S(1)}, bf16[27,10752]{1,0:T(8,128)(2,1)}, u32[]{:S(2)}) copy-start(bf16[27,10752]{1,0:T(8,128)(2,1)} %constant.15.clone.p1) | copy-start | bytes 1741828
  2.9 9.9 %copy-start.12 = (bf16[144,2048]{1,0:T(8,128)(2,1)S(1)}, bf16[144,2048]{1,0:T(8,128)(2,1)}, u32[]{:S(2)}) copy-start(bf16[144,2048]{1,0:T(8,128)(2,1)} %constant.17.clone.p3) | copy-start | bytes 1769476
  2.9 9.9 %copy-start.13 = (bf16[48,3584]{1,0:T(8,128)(2,1)S(1)}, bf16[48,3584]{1,0:T(8,128)(2,1)}, u32[]{:S(2)}) copy-start(bf16[48,3584]{1,0:T(8,128)(2,1)} %constant.18.clone.ph) | copy-start | bytes 1032196
  2.9 9.9 %copy-start.14 = (bf16[144,1024]{1,0:T(8,128)(2,1)S(1)}, bf16[144,1024]{1,0:T(8,128)(2,1)}, u32[]{:S(2)}) copy-start(bf16[144,1024]{1,0:T(8,128)(2,1)} %constant.16.clone.p2) | copy-start | bytes 884740
  2.9 9.9 %copy-start.15 = (bf16[240,432]{1,0:T(8,128)(2,1)S(1)}, bf16[240,432]{1,0:T(8,128)(2,1)}, u32[]{:S(2)}) copy-start(bf16[240,432]{1,0:T(8,128)(2,1)} %constant.19.clone.im) | copy-start | bytes 622084
  2.9 9.9 %copy-start.16 = (bf16[256,256]{1,0:T(8,128)(2,1)S(1)}, bf16[256,256]{1,0:T(8,128)(2,1)}, u32[]{:S(2)}) copy-start(bf16[256,256]{1,0:T(8,128)(2,1)} %constant.14.clone.pick) | copy-start | bytes 393220
  4.4 8.3 %collective-permute-start.3 = (bf16[3,96,128]{2,1,0:T(8,128)(2,1)S(1)}, bf16[3,96,128]{2,1,0:T(8,128)(2,1)S(1)}, u32[]{:S(2)}, u32[]{:S(2)}) collective-permute-start(bf16[3,96,128]{2,1,0:T(8,128)(2,1)S(1)} %get-tuple-element.28), channel_id=1, source_target_pairs={{0,2},{2,0},{4,6},{6,4},{8,10},{10,8},{12,14},{14,12},{1,3},{3,1},... | collective-permute-start | bytes 221192 | tf_op jit(solution)/shard_map/ppermute | solution.py:424
  7.0 5.7 %collective-permute-start.4 = (bf16[3,96,128]{2,1,0:T(8,128)(2,1)S(1)}, bf16[3,96,128]{2,1,0:T(8,128)(2,1)S(1)}, u32[]{:S(2)}, u32[]{:S(2)}) collective-permute-start(bf16[3,96,128]{2,1,0:T(8,128)(2,1)S(1)} %get-tuple-element.29), channel_id=1, source_target_pairs={{2,4},{4,2},{6,8},{8,6},{10,12},{12,10},{3,5},{5,3},{7,9},{9,7},{1... | collective-permute-start | bytes 221192 | tf_op jit(solution)/shard_map/ppermute | solution.py:424
  7.6 21.3 %collective-permute-start.1 = (bf16[96,16,128]{2,1,0:T(8,128)(2,1)S(1)}, bf16[96,16,128]{2,1,0:T(8,128)(2,1)S(1)}, u32[]{:S(2)}, u32[]{:S(2)}) collective-permute-start(bf16[96,16,128]{2,1,0:T(8,128)(2,1)S(1)} %get-tuple-element.25), channel_id=1, source_target_pairs={{0,2},{2,0},{4,6},{6,4},{8,10},{10,8},{12,14},{14,12},{1,3},{3,1},... | collective-permute-start | bytes 1179656 | tf_op jit(solution)/shard_map/ppermute | solution.py:424
  12.0 9.4 %collective-permute-start.2 = (bf16[96,16,128]{2,1,0:T(8,128)(2,1)S(1)}, bf16[96,16,128]{2,1,0:T(8,128)(2,1)S(1)}, u32[]{:S(2)}, u32[]{:S(2)}) collective-permute-start(bf16[96,16,128]{2,1,0:T(8,128)(2,1)S(1)} %get-tuple-element.26), channel_id=1, source_target_pairs={{2,4},{4,2},{6,8},{8,6},{10,12},{12,10},{3,5},{5,3},{7,9},{9,7},{1... | collective-permute-start | bytes 1179656 | tf_op jit(solution)/shard_map/ppermute | solution.py:424
  23.2 13.0 %collective-permute-start.5 = (f32[104,128]{1,0:T(8,128)S(1)}, f32[104,128]{1,0:T(8,128)S(1)}, u32[]{:S(2)}, u32[]{:S(2)}) collective-permute-start(f32[104,128]{1,0:T(8,128)S(1)} %get-tuple-element.39), channel_id=1, source_target_pairs={{2,4},{4,2},{6,8},{8,6},{10,12},{12,10},{3,5},{5,3},{7,9},{9,7},{1... | collective-permute-start | bytes 159752 | tf_op jit(solution)/shard_map/ppermute | solution.py:424
  30.6 5.6 %collective-permute-start.6 = (f32[96,128]{1,0:T(8,128)S(1)}, f32[96,128]{1,0:T(8,128)S(1)}, u32[]{:S(2)}, u32[]{:S(2)}) collective-permute-start(f32[96,128]{1,0:T(8,128)S(1)} %get-tuple-element.40), channel_id=1, source_target_pairs={{0,2},{2,0},{4,6},{6,4},{8,10},{10,8},{12,14},{14,12},{1,3},{3,1},... | collective-permute-start | bytes 147464 | tf_op jit(solution)/shard_map/ppermute | solution.py:424

commit v5 on v4

--- a/solution.py
+++ b/solution.py
@@ -353,17 +353,23 @@
     v = jnp.maximum(pre2[...] + carried[...].astype(F32), 0.0) * live
     h2[1 : disp + 1] = v.astype(BF)
     w3 = ah[side]
-    for d0 in window_starts(disp):
-        p = dot(w3, h2[d0 : d0 + 16].reshape(256, W))
-        for d in range(T1):
-            v = combine(p[d * 48 : d * 48 + 48]) + pre3[d0 + d]
-            h3[d0 + d] = jnp.maximum(v, 0.0).astype(BF)
+    starts = window_starts(disp)
+    for n in range(0, len(starts), 2):
+        pair = starts[n : n + 2]
+        p = dot(w3, jnp.concatenate([h2[d0 : d0 + 16].reshape(256, W) for d0 in pair], axis=1))
+        for k, d0 in enumerate(pair):
+            for d in range(T1):
+                v = combine(p[d * 48 : d * 48 + 48, k * W : (k + 1) * W]) + pre3[d0 + d]
+                h3[d0 + d] = jnp.maximum(v, 0.0).astype(BF)
     w4 = ae[side]
     acc[0:2] = jnp.zeros((2, 24, W), F32)
-    for k in range(disp // 16):
-        p = dot(w4, h3[16 * k : 16 * k + 16].reshape(256, W)).reshape(18, 24, W)
-        acc[16 * k : 16 * k + 2] += p[:2]
-        acc[16 * k + 2 : 16 * k + 18] = p[2:]
+    for n in range(0, disp // 16, 2):
+        x = jnp.concatenate([h3[16 * k : 16 * k + 16].reshape(256, W) for k in (n, n + 1)], axis=1)
+        both = dot(w4, x)
+        for k in (n, n + 1):
+            p = both[:, (k - n) * W : (k - n + 1) * W].reshape(18, 24, W)
+            acc[16 * k : 16 * k + 2] += p[:2]
+            acc[16 * k + 2 : 16 * k + 18] = p[2:]
     sum_columns(acc, comb, disp)
 
 

time: 37.1 us -> 35.9 us (0.968)
  Pallas kernels: 14.9 us -> 13.7 us
  starting transfers between devices: 12.9 us -> 12.3 us
  waiting for transfers between devices: 7.11 us -> 7.69 us
    pallas_call x6, Pallas kernels: 14.9 us -> 13.7 us  [call(): pl.pallas_call(kernel, out_shape=tuple((jax.ShapeDtypeStruct(s, d) for s,...]
    ppermute x6, starting transfers between devices: 12.4 us -> 11.8 us  [swap(): return lax.ppermute(x, 'rows', pairs)]
    ppermute x6, waiting for transfers between devices: 7.11 us -> 7.69 us  [swap(): return lax.ppermute(x, 'rows', pairs)]
  transfers between devices with their start and end apart: 7 -> 7, of which waited for: 2 -> 2; matrix products, arithmetic and copies ran while one was open for 0% -> 0% of each run, Pallas kernels for 34% -> 32%
where the time goes in v5:
time: 35.9 us; the launch traced here: 35.7 us
  Pallas kernels  13.7 us (38%)
  starting transfers between devices  12.3 us (34%)
  waiting for transfers between devices  7.69 us (21%)
  local copies, waits for them, and re-layouts  1.82 us (5%)
    pallas_call x6, Pallas kernels, call(): pl.pallas_call(kernel, out_shape=tuple((jax.ShapeDtypeStruct(s, d) for s,...  13.7 us
    ppermute x6, starting transfers between devices, swap(): return lax.ppermute(x, 'rows', pairs)  11.8 us
    ppermute x6, waiting for transfers between devices, swap(): return lax.ppermute(x, 'rows', pairs)  7.69 us
    unnamed x34, local copies, waits for them, and re-layouts  1.82 us
  transfers between devices with their start and end apart: 7, of which 2 were waited for; matrix products, arithmetic and copies ran while one was open for 0% of the time, Pallas kernels for 32%

profile of v5, /device:TPU:0, one launch (start us, length us, event | category | flops | bytes accessed | tf_op | source)
XLA Modules:
  0.0 35.7 jit_solution(4394538224424999810)
XLA Ops:
  0.0 0.5 %collective-permute-start = (bf16[512,128]{1,0:T(8,128)(2,1)}, bf16[512,128]{1,0:T(8,128)(2,1)S(1)}, u32[]{:S(2)}, u32[]{:S(2)}) collective-permute-start(bf16[512,128]{1,0:T(8,128)(2,1)} %bitcast.14), channel_id=1, source_target_pairs={{0,1},{1,0},{2,3},{3,2},{4,5},{5,4},{6,7},{7,6},{8,9},{9,8},{10,11... | collective-permute-start | bytes 393224 | tf_op jit(solution)/shard_map/ppermute | solution.py:433
  0.5 0.0 copy-start
  0.5 1.4 %copy-done = bf16[1,16,96,4,128]{4,3,2,1,0:T(4,128)(2,1)S(1)} copy-done((bf16[1,16,96,4,128]{4,3,2,1,0:T(4,128)(2,1)S(1)}, bf16[1,16,96,4,128]{4,3,2,1,0:T(4,128)(2,1)}, u32[]{:S(2)}) %copy-start) | copy-done | bytes 1572888
  1.9 0.0 copy-start.2
  1.9 0.0 copy-start.7
  1.9 0.0 copy-start.8
  1.9 0.0 copy-start.9
  1.9 0.6 %shard_map.154 = (bf16[96,16,128]{2,1,0:T(8,128)(2,1)S(1)}, bf16[96,16,128]{2,1,0:T(8,128)(2,1)S(1)}) custom-call(bf16[16,384,128]{2,1,0:T(8,128)(2,1)S(1)} %bitcast.12), custom_call_target="tpu_custom_call" | custom-call | flops 1650000000 | bytes 1000 | tf_op jit(solution)/shard_map/pallas_call | solution.py:410
  2.4 0.0 collective-permute-done.mate
  2.4 0.3 copy-done.2
  2.8 0.0 copy-done.7
  2.8 0.0 copy-done.8
  2.8 0.0 copy-done.9
  2.8 0.0 copy-start.1
  2.8 0.0 copy-start.3
  2.8 0.0 copy-start.4
  2.8 0.0 copy-start.5
  2.8 0.0 copy-start.6
  2.8 0.0 copy-start.10
  2.8 0.0 copy-start.11
  2.9 0.0 copy-start.12
  2.9 0.0 copy-start.13
  2.9 0.0 copy-start.14
  2.9 0.0 copy-start.15
  2.9 0.0 copy-start.16
  2.9 1.5 %shard_map.155 = (bf16[4,96,128]{2,1,0:T(8,128)(2,1)S(1)}, bf16[3,96,128]{2,1,0:T(8,128)(2,1)S(1)}, bf16[3,96,128]{2,1,0:T(8,128)(2,1)S(1)}, bf16[96,16,128]{2,1,0:T(8,128)(2,1)S(1)}, bf16[96,16,128]{2,1,0:T(8,128)(2,1)S(1)}) custom-call(bf16[512,128]{1,0:T(8,128)(2,1)S(1)} %bitcast.15, bf16[512,128]{1,0:T(8,128)(2,1)S(1)} %collective-permute-done.mate, ...), custom_call_target="tpu_custom_call" | custom-call | flops 1650000000 | bytes 1000 | tf_op jit(solution)/shard_map/pallas_call | solution.py:410
  4.4 2.6 %collective-permute-start.3 = (bf16[3,96,128]{2,1,0:T(8,128)(2,1)S(1)}, bf16[3,96,128]{2,1,0:T(8,128)(2,1)S(1)}, u32[]{:S(2)}, u32[]{:S(2)}) collective-permute-start(bf16[3,96,128]{2,1,0:T(8,128)(2,1)S(1)} %get-tuple-element.28), channel_id=1, source_target_pairs={{0,2},{2,0},{4,6},{6,4},{8,10},{10,8},{12,14},{14,12},{1,3},{3,1},... | collective-permute-start | bytes 221192 | tf_op jit(solution)/shard_map/ppermute | solution.py:430
  7.0 0.7 %collective-permute-start.4 = (bf16[3,96,128]{2,1,0:T(8,128)(2,1)S(1)}, bf16[3,96,128]{2,1,0:T(8,128)(2,1)S(1)}, u32[]{:S(2)}, u32[]{:S(2)}) collective-permute-start(bf16[3,96,128]{2,1,0:T(8,128)(2,1)S(1)} %get-tuple-element.29), channel_id=1, source_target_pairs={{2,4},{4,2},{6,8},{8,6},{10,12},{12,10},{3,5},{5,3},{7,9},{9,7},{1... | collective-permute-start | bytes 221192 | tf_op jit(solution)/shard_map/ppermute | solution.py:430
  7.6 4.3 %collective-permute-start.1 = (bf16[96,16,128]{2,1,0:T(8,128)(2,1)S(1)}, bf16[96,16,128]{2,1,0:T(8,128)(2,1)S(1)}, u32[]{:S(2)}, u32[]{:S(2)}) collective-permute-start(bf16[96,16,128]{2,1,0:T(8,128)(2,1)S(1)} %get-tuple-element.25), channel_id=1, source_target_pairs={{0,2},{2,0},{4,6},{6,4},{8,10},{10,8},{12,14},{14,12},{1,3},{3,1},... | collective-permute-start | bytes 1179656 | tf_op jit(solution)/shard_map/ppermute | solution.py:430
  12.0 0.7 %collective-permute-start.2 = (bf16[96,16,128]{2,1,0:T(8,128)(2,1)S(1)}, bf16[96,16,128]{2,1,0:T(8,128)(2,1)S(1)}, u32[]{:S(2)}, u32[]{:S(2)}) collective-permute-start(bf16[96,16,128]{2,1,0:T(8,128)(2,1)S(1)} %get-tuple-element.26), channel_id=1, source_target_pairs={{2,4},{4,2},{6,8},{8,6},{10,12},{12,10},{3,5},{5,3},{7,9},{9,7},{1... | collective-permute-start | bytes 1179656 | tf_op jit(solution)/shard_map/ppermute | solution.py:430
  12.7 0.0 collective-permute-done.3.even
  12.7 0.0 collective-permute-done.4.odd
  12.7 0.0 copy-done.1
  12.7 0.0 copy-done.3
  12.7 0.0 copy-done.4
  12.7 0.0 copy-done.5
  12.7 0.0 copy-done.6
  12.7 0.0 copy-done.10
  12.7 0.0 copy-done.11
  12.7 0.0 copy-done.12
  12.8 0.0 copy-done.13
  12.8 0.0 copy-done.14
  12.8 0.0 copy-done.15
  12.8 0.0 copy-done.16
  12.8 8.6 %shard_map.156 = (f32[2,96,16,128]{3,2,1,0:T(8,128)S(1)}, f32[2,96,16,128]{3,2,1,0:T(8,128)S(1)}, f32[4,96,128]{2,1,0:T(8,128)S(1)}, bf16[2,672,256]{2,1,0:T(8,128)(2,1)S(1)}, bf16[2,432,256]{2,1,0:T(8,128)(2,1)S(1)}) custom-call(bf16[4,96,128]{2,1,0:T(8,128)(2,1)S(1)} %get-tuple-element.27.corr, bf16[3,96,128]{2,1,0:T(8,128)(2,1)S(1)} %collective-permute-done.3.even, ...), custom_call_target="tpu_custom_call" | custom-call | flops 8800000000 | bytes 1000 | tf_op jit(solution)/shard_map/pallas_call | solution.py:410
  21.4 0.0 collective-permute-done.2.carried
  21.4 1.3 %shard_map.157 = (f32[384,128]{1,0:T(8,128)S(1)}, f32[104,128]{1,0:T(8,128)S(1)}, f32[96,16,128]{2,1,0:T(8,128)S(1)}, f32[96,16,128]{2,1,0:T(8,128)S(1)}) custom-call(bf16[96,16,128]{2,1,0:T(8,128)(2,1)S(1)} %collective-permute-done.2.carried, f32[4,96,128]{2,1,0:T(8,128)S(1)} %get-tuple-element.30.main_in, f32[2,96,16,128]{3,2,1,0:T(8,128)S(1)} %get-tuple-element.31.pre2, ...), custom_call_target="tpu_custom_call" | custom-call | flops 2200000000 | bytes 1000 | tf_op jit(solution)/shard_map/pallas_call | solution.py:410
  22.6 0.7 %collective-permute-start.5 = (f32[104,128]{1,0:T(8,128)S(1)}, f32[104,128]{1,0:T(8,128)S(1)}, u32[]{:S(2)}, u32[]{:S(2)}) collective-permute-start(f32[104,128]{1,0:T(8,128)S(1)} %get-tuple-element.39), channel_id=1, source_target_pairs={{2,4},{4,2},{6,8},{8,6},{10,12},{12,10},{3,5},{5,3},{7,9},{9,7},{1... | collective-permute-start | bytes 159752 | tf_op jit(solution)/shard_map/ppermute | solution.py:430
  23.3 5.6 %collective-permute-done.1.carried = bf16[96,16,128]{2,1,0:T(8,128)(2,1)S(1)} collective-permute-done((bf16[96,16,128]{2,1,0:T(8,128)(2,1)S(1)}, bf16[96,16,128]{2,1,0:T(8,128)(2,1)S(1)}, u32[]{:S(2)}, u32[]{:S(2)}) %collective-permute-start.1) | collective-permute-done | bytes 393248 | tf_op jit(solution)/shard_map/ppermute | solution.py:430
  28.9 1.1 %shard_map.158 = (f32[384,128]{1,0:T(8,128)S(1)}, f32[96,128]{1,0:T(8,128)S(1)}) custom-call(bf16[96,16,128]{2,1,0:T(8,128)(2,1)S(1)} %collective-permute-done.1.carried, f32[384,128]{1,0:T(8,128)S(1)} %get-tuple-element.35.main_in, f32[96,16,128]{2,1,0:T(8,128)S(1)} %get-tuple-element.36.pre2, f32[96,16,128]{2,1,0:T(8,128)S(1)} %get-tuple-element.37.pre3, ...), custom_call_target="tpu_custom_call" | custom-call | flops 2200000000 | bytes 1000 | tf_op jit(solution)/shard_map/pallas_call | solution.py:410
  30.0 2.9 %collective-permute-start.6 = (f32[96,128]{1,0:T(8,128)S(1)}, f32[96,128]{1,0:T(8,128)S(1)}, u32[]{:S(2)}, u32[]{:S(2)}) collective-permute-start(f32[96,128]{1,0:T(8,128)S(1)} %get-tuple-element.40), channel_id=1, source_target_pairs={{0,2},{2,0},{4,6},{6,4},{8,10},{10,8},{12,14},{14,12},{1,3},{3,1},... | collective-permute-start | bytes 147464 | tf_op jit(solution)/shard_map/ppermute | solution.py:430
  33.0 2.1 %collective-permute-done.6.even = f32[96,128]{1,0:T(8,128)S(1)} collective-permute-done((f32[96,128]{1,0:T(8,128)S(1)}, f32[96,128]{1,0:T(8,128)S(1)}, u32[]{:S(2)}, u32[]{:S(2)}) %collective-permute-start.6) | collective-permute-done | bytes 49184 | tf_op jit(solution)/shard_map/ppermute | solution.py:430
  35.0 0.0 collective-permute-done.5.odd
  35.0 0.7 %shard_map.159 = f32[384,128]{1,0:T(8,128)} custom-call(f32[384,128]{1,0:T(8,128)S(1)} %get-tuple-element.38.main, f32[104,128]{1,0:T(8,128)S(1)} %collective-permute-done.5.odd, f32[96,128]{1,0:T(8,128)S(1)} %collective-permute-done.6.even), custom_call_target="tpu_custom_call" | custom-call | flops 110000000 | bytes 1000 | tf_op jit(solution)/shard_map/pallas_call | solution.py:410
Async XLA Ops:
  0.0 2.4 %collective-permute-start = (bf16[512,128]{1,0:T(8,128)(2,1)}, bf16[512,128]{1,0:T(8,128)(2,1)S(1)}, u32[]{:S(2)}, u32[]{:S(2)}) collective-permute-start(bf16[512,128]{1,0:T(8,128)(2,1)} %bitcast.14), channel_id=1, source_target_pairs={{0,1},{1,0},{2,3},{3,2},{4,5},{5,4},{6,7},{7,6},{8,9},{9,8},{10,11... | collective-permute-start | bytes 393224 | tf_op jit(solution)/shard_map/ppermute | solution.py:433
  0.5 1.4 %copy-start = (bf16[1,16,96,4,128]{4,3,2,1,0:T(4,128)(2,1)S(1)}, bf16[1,16,96,4,128]{4,3,2,1,0:T(4,128)(2,1)}, u32[]{:S(2)}) copy-start(bf16[1,16,96,4,128]{4,3,2,1,0:T(4,128)(2,1)} %param.20) | copy-start | bytes 4718596
  1.9 0.9 %copy-start.2 = (bf16[1,128,4,128]{3,2,1,0:T(4,128)(2,1)S(1)}, bf16[1,128,4,128]{3,2,1,0:T(4,128)(2,1)}, u32[]{:S(2)}) copy-start(bf16[1,128,4,128]{3,2,1,0:T(4,128)(2,1)} %param.16) | copy-start | bytes 393220
  1.9 0.9 %copy-start.7 = (s32[4,6]{1,0:T(4,128)S(1)}, s32[4,6]{1,0:T(4,128)}, u32[]{:S(2)}) copy-start(s32[4,6]{1,0:T(4,128)} %pattern.1) | copy-start | bytes 292
  1.9 0.9 %copy-start.8 = (s32[1,4,4]{2,1,0:T(4,128)S(1)}, s32[1,4,4]{2,1,0:T(4,128)}, u32[]{:S(2)}) copy-start(s32[1,4,4]{2,1,0:T(4,128)} %param.19) | copy-start | bytes 196
  1.9 0.9 %copy-start.9 = (s32[2]{0:T(128)S(1)}, s32[2]{0:T(128)}, u32[]{:S(2)}) copy-start(s32[2]{0:T(128)} %partner.1) | copy-start | bytes 28
  2.8 9.9 %copy-start.1 = (bf16[1,16,96,4,128]{4,3,2,1,0:T(4,128)(2,1)S(1)}, bf16[1,16,96,4,128]{4,3,2,1,0:T(4,128)(2,1)}, u32[]{:S(2)}) copy-start(bf16[1,16,96,4,128]{4,3,2,1,0:T(4,128)(2,1)} %param.20) | copy-start | bytes 4718596
  2.8 9.9 %copy-start.3 = (bf16[27,16,16]{0,2,1:T(8,128)(2,1)S(1)}, bf16[27,16,16]{0,2,1:T(8,128)(2,1)}, u32[]{:S(2)}) copy-start(bf16[27,16,16]{0,2,1:T(8,128)(2,1)} %param.22) | copy-start | bytes 41476
  2.8 9.9 %copy-start.4 = (bf16[27,16,16]{0,2,1:T(8,128)(2,1)S(1)}, bf16[27,16,16]{0,2,1:T(8,128)(2,1)}, u32[]{:S(2)}) copy-start(bf16[27,16,16]{0,2,1:T(8,128)(2,1)} %param.23) | copy-start | bytes 41476
  2.8 9.9 %copy-start.5 = (bf16[27,16]{0,1:T(8,128)(2,1)S(1)}, bf16[27,16]{0,1:T(8,128)(2,1)}, u32[]{:S(2)}) copy-start(bf16[27,16]{0,1:T(8,128)(2,1)} %param.21) | copy-start | bytes 2596
  2.8 9.9 %copy-start.6 = (bf16[27,16]{0,1:T(8,128)(2,1)S(1)}, bf16[27,16]{0,1:T(8,128)(2,1)}, u32[]{:S(2)}) copy-start(bf16[27,16]{0,1:T(8,128)(2,1)} %param.24) | copy-start | bytes 2596
  2.8 9.9 %copy-start.10 = (bf16[2,432,432]{2,1,0:T(8,128)(2,1)S(1)}, bf16[2,432,432]{2,1,0:T(8,128)(2,1)}, u32[]{:S(2)}) copy-start(bf16[2,432,432]{2,1,0:T(8,128)(2,1)} %constant.20.clone.ie) | copy-start | bytes 2239492
  2.8 9.9 %copy-start.11 = (bf16[27,10752]{1,0:T(8,128)(2,1)S(1)}, bf16[27,10752]{1,0:T(8,128)(2,1)}, u32[]{:S(2)}) copy-start(bf16[27,10752]{1,0:T(8,128)(2,1)} %constant.15.clone.p1) | copy-start | bytes 1741828
  2.9 9.9 %copy-start.12 = (bf16[144,2048]{1,0:T(8,128)(2,1)S(1)}, bf16[144,2048]{1,0:T(8,128)(2,1)}, u32[]{:S(2)}) copy-start(bf16[144,2048]{1,0:T(8,128)(2,1)} %constant.17.clone.p3) | copy-start | bytes 1769476
  2.9 9.9 %copy-start.13 = (bf16[48,3584]{1,0:T(8,128)(2,1)S(1)}, bf16[48,3584]{1,0:T(8,128)(2,1)}, u32[]{:S(2)}) copy-start(bf16[48,3584]{1,0:T(8,128)(2,1)} %constant.18.clone.ph) | copy-start | bytes 1032196
  2.9 9.9 %copy-start.14 = (bf16[144,1024]{1,0:T(8,128)(2,1)S(1)}, bf16[144,1024]{1,0:T(8,128)(2,1)}, u32[]{:S(2)}) copy-start(bf16[144,1024]{1,0:T(8,128)(2,1)} %constant.16.clone.p2) | copy-start | bytes 884740
  2.9 9.9 %copy-start.15 = (bf16[240,432]{1,0:T(8,128)(2,1)S(1)}, bf16[240,432]{1,0:T(8,128)(2,1)}, u32[]{:S(2)}) copy-start(bf16[240,432]{1,0:T(8,128)(2,1)} %constant.19.clone.im) | copy-start | bytes 622084
  2.9 9.9 %copy-start.16 = (bf16[256,256]{1,0:T(8,128)(2,1)S(1)}, bf16[256,256]{1,0:T(8,128)(2,1)}, u32[]{:S(2)}) copy-start(bf16[256,256]{1,0:T(8,128)(2,1)} %constant.14.clone.pick) | copy-start | bytes 393220
  4.4 8.3 %collective-permute-start.3 = (bf16[3,96,128]{2,1,0:T(8,128)(2,1)S(1)}, bf16[3,96,128]{2,1,0:T(8,128)(2,1)S(1)}, u32[]{:S(2)}, u32[]{:S(2)}) collective-permute-start(bf16[3,96,128]{2,1,0:T(8,128)(2,1)S(1)} %get-tuple-element.28), channel_id=1, source_target_pairs={{0,2},{2,0},{4,6},{6,4},{8,10},{10,8},{12,14},{14,12},{1,3},{3,1},... | collective-permute-start | bytes 221192 | tf_op jit(solution)/shard_map/ppermute | solution.py:430
  7.0 5.7 %collective-permute-start.4 = (bf16[3,96,128]{2,1,0:T(8,128)(2,1)S(1)}, bf16[3,96,128]{2,1,0:T(8,128)(2,1)S(1)}, u32[]{:S(2)}, u32[]{:S(2)}) collective-permute-start(bf16[3,96,128]{2,1,0:T(8,128)(2,1)S(1)} %get-tuple-element.29), channel_id=1, source_target_pairs={{2,4},{4,2},{6,8},{8,6},{10,12},{12,10},{3,5},{5,3},{7,9},{9,7},{1... | collective-permute-start | bytes 221192 | tf_op jit(solution)/shard_map/ppermute | solution.py:430
  7.6 21.3 %collective-permute-start.1 = (bf16[96,16,128]{2,1,0:T(8,128)(2,1)S(1)}, bf16[96,16,128]{2,1,0:T(8,128)(2,1)S(1)}, u32[]{:S(2)}, u32[]{:S(2)}) collective-permute-start(bf16[96,16,128]{2,1,0:T(8,128)(2,1)S(1)} %get-tuple-element.25), channel_id=1, source_target_pairs={{0,2},{2,0},{4,6},{6,4},{8,10},{10,8},{12,14},{14,12},{1,3},{3,1},... | collective-permute-start | bytes 1179656 | tf_op jit(solution)/shard_map/ppermute | solution.py:430
  12.0 9.4 %collective-permute-start.2 = (bf16[96,16,128]{2,1,0:T(8,128)(2,1)S(1)}, bf16[96,16,128]{2,1,0:T(8,128)(2,1)S(1)}, u32[]{:S(2)}, u32[]{:S(2)}) collective-permute-start(bf16[96,16,128]{2,1,0:T(8,128)(2,1)S(1)} %get-tuple-element.26), channel_id=1, source_target_pairs={{2,4},{4,2},{6,8},{8,6},{10,12},{12,10},{3,5},{5,3},{7,9},{9,7},{1... | collective-permute-start | bytes 1179656 | tf_op jit(solution)/shard_map/ppermute | solution.py:430
  22.6 12.4 %collective-permute-start.5 = (f32[104,128]{1,0:T(8,128)S(1)}, f32[104,128]{1,0:T(8,128)S(1)}, u32[]{:S(2)}, u32[]{:S(2)}) collective-permute-start(f32[104,128]{1,0:T(8,128)S(1)} %get-tuple-element.39), channel_id=1, source_target_pairs={{2,4},{4,2},{6,8},{8,6},{10,12},{12,10},{3,5},{5,3},{7,9},{9,7},{1... | collective-permute-start | bytes 159752 | tf_op jit(solution)/shard_map/ppermute | solution.py:430
  30.0 5.0 %collective-permute-start.6 = (f32[96,128]{1,0:T(8,128)S(1)}, f32[96,128]{1,0:T(8,128)S(1)}, u32[]{:S(2)}, u32[]{:S(2)}) collective-permute-start(f32[96,128]{1,0:T(8,128)S(1)} %get-tuple-element.40), channel_id=1, source_target_pairs={{0,2},{2,0},{4,6},{6,4},{8,10},{10,8},{12,14},{14,12},{1,3},{3,1},... | collective-permute-start | bytes 147464 | tf_op jit(solution)/shard_map/ppermute | solution.py:430

commit v6 on v5

--- a/solution.py
+++ b/solution.py
@@ -128,10 +128,13 @@
     last = R - 1
     even_row = jnp.where(parity() == 0, last, 0)
     both = jnp.concatenate([edge_pick(even_row), edge_pick(last - even_row)], axis=0)
-    for q in range(carried.shape[1] // 16):
-        v = dot(both, carried[:, q * 16 : q * 16 + 16, :].reshape(256, W)).astype(BF)
-        even[4 * q : 4 * q + 4] = v[:64].reshape(4, A, W)
-        odd[4 * q : 4 * q + 4] = v[64:].reshape(4, A, W)
+    for n in range(0, carried.shape[1] // 16, 2):
+        x = jnp.concatenate([carried[:, q * 16 : q * 16 + 16, :].reshape(256, W) for q in (n, n + 1)], axis=1)
+        p = dot(both, x).astype(BF)
+        for q in (n, n + 1):
+            v = p[:, (q - n) * W : (q - n + 1) * W]
+            even[4 * q : 4 * q + 4] = v[:64].reshape(4, A, W)
+            odd[4 * q : 4 * q + 4] = v[64:].reshape(4, A, W)
 
 
 def ordered(w):
@@ -190,7 +193,12 @@
 
 def corr_kernel(own, mate, partner, pattern, valid, even_c, odd_c, corr, even, odd, even_out, odd_out):
     cam = lax.axis_index("cam")
-    right = partner[cam] < cam
+    mates = jnp.broadcast_to(partner[...].astype(F32), (1, partner.shape[1]))
+    flag = jnp.zeros((1, W), F32)
+    for k in range(partner.shape[1]):
+        one = jnp.broadcast_to(mates[:, k : k + 1], (1, W))
+        flag = jnp.where(cam == k, one, flag)
+    right = flag < cam.astype(F32)
     line = lanes((1, W)) // BLOCK_COLS
     disp = corr.shape[1]
     channels = own.shape[0] // R
@@ -206,17 +214,21 @@
     rs = jnp.concatenate([jnp.where(row == r, right_side, zero) for r in range(R)], axis=1)
     s = dot(lt, rs)
     scale = 1.0 / np.sqrt(channels).astype(np.float32)
+    rows = []
     for r in range(R):
         v = pltpu.roll(s[:, r * W : (r + 1) * W], 1, 1, stride=1, stride_axis=0)
         v = jnp.where(lane <= sub, v, 0.0).T[:disp] * scale
         v = jnp.concatenate(
-            [v[t * DTILE : (t + 1) * DTILE] * pattern[r, t].astype(F32) for t in range(disp // DTILE)], axis=0
+            [v[t * DTILE : (t + 1) * DTILE] * pattern[r : r + 1, t : t + 1].astype(F32) for t in range(disp // DTILE)], axis=0
         )
-        v = dot(v.astype(BF), flip)
+        rows.append(v.astype(BF))
+    flipped = dot(jnp.concatenate(rows, axis=0), flip)
+    for r in range(R):
+        v = flipped[r * disp : (r + 1) * disp]
         v = jnp.where(right, v, pltpu.roll(v, 0, 1, stride=1, stride_axis=0))
         pixels = jnp.zeros((1, W), F32)
         for k in range(W // BLOCK_COLS):
-            pixels = jnp.where(line == k, valid[r, k].astype(F32), pixels)
+            pixels = jnp.where(line == k, valid[r : r + 1, k : k + 1].astype(F32), pixels)
         corr[r] = (v * pixels).astype(BF)
     side = 1 - parity()
     even[...] = corr[pl.ds(side, 3)]
@@ -438,8 +450,8 @@
     corr, even_r, odd_r, even_c, odd_c = call(
         corr_kernel,
         [((R, disp, W), BF), rows3, rows3, edge, edge],
-        [own, mate, partner, pattern, valid[0], even_c, odd_c],
-        specs=[VM, VM, SM, SM, SM, VM, VM],
+        [own, mate, partner[None], pattern, valid[0], even_c, odd_c],
+        specs=[VM] * 7,
         us=CORR,
     )
     odd_r = swap(odd_r, odd_pairs)

time: 35.9 us -> 35.5 us (0.989)
  Pallas kernels: 13.7 us -> 13.1 us
    pallas_call x6, Pallas kernels: 13.7 us -> 13.1 us  [call(): pl.pallas_call(kernel, out_shape=tuple((jax.ShapeDtypeStruct(s, d) for s,...]
where the time goes in v6:
time: 35.5 us; the launch traced here: 35.3 us
  Pallas kernels  13.1 us (37%)
  starting transfers between devices  12.2 us (34%)
  waiting for transfers between devices  7.73 us (22%)
  local copies, waits for them, and re-layouts  2 us (6%)
    pallas_call x6, Pallas kernels, call(): pl.pallas_call(kernel, out_shape=tuple((jax.ShapeDtypeStruct(s, d) for s,...  13.1 us
    ppermute x6, starting transfers between devices, swap(): return lax.ppermute(x, 'rows', pairs)  11.8 us
    ppermute x6, waiting for transfers between devices, swap(): return lax.ppermute(x, 'rows', pairs)  7.73 us
    unnamed x34, local copies, waits for them, and re-layouts  2 us
  transfers between devices with their start and end apart: 7, of which 2 were waited for; matrix products, arithmetic and copies ran while one was open for 0% of the time, Pallas kernels for 32%

profile of v6, /device:TPU:0, one launch (start us, length us, event | category | flops | bytes accessed | tf_op | source)
XLA Modules:
  0.0 35.3 jit_solution(7865529272761055071)
XLA Ops:
  0.0 0.5 %collective-permute-start = (bf16[512,128]{1,0:T(8,128)(2,1)}, bf16[512,128]{1,0:T(8,128)(2,1)S(1)}, u32[]{:S(2)}, u32[]{:S(2)}) collective-permute-start(bf16[512,128]{1,0:T(8,128)(2,1)} %bitcast.15), channel_id=1, source_target_pairs={{0,1},{1,0},{2,3},{3,2},{4,5},{5,4},{6,7},{7,6},{8,9},{9,8},{10,11... | collective-permute-start | bytes 393224 | tf_op jit(solution)/shard_map/ppermute | solution.py:445
  0.5 0.0 copy-start
  0.5 1.4 %copy-done = bf16[1,16,96,4,128]{4,3,2,1,0:T(4,128)(2,1)S(1)} copy-done((bf16[1,16,96,4,128]{4,3,2,1,0:T(4,128)(2,1)S(1)}, bf16[1,16,96,4,128]{4,3,2,1,0:T(4,128)(2,1)}, u32[]{:S(2)}) %copy-start) | copy-done | bytes 1572888
  1.9 0.0 copy-start.2
  1.9 0.0 copy-start.7
  1.9 0.0 copy-start.8
  1.9 0.0 copy-start.9
  1.9 0.4 %shard_map.154 = (bf16[96,16,128]{2,1,0:T(8,128)(2,1)S(1)}, bf16[96,16,128]{2,1,0:T(8,128)(2,1)S(1)}) custom-call(bf16[16,384,128]{2,1,0:T(8,128)(2,1)S(1)} %bitcast.13), custom_call_target="tpu_custom_call" | custom-call | flops 1650000000 | bytes 1000 | tf_op jit(solution)/shard_map/pallas_call | solution.py:422
  2.3 0.0 collective-permute-done.mate
  2.3 0.5 %copy-done.2 = bf16[1,128,4,128]{3,2,1,0:T(4,128)(2,1)S(1)} copy-done((bf16[1,128,4,128]{3,2,1,0:T(4,128)(2,1)S(1)}, bf16[1,128,4,128]{3,2,1,0:T(4,128)(2,1)}, u32[]{:S(2)}) %copy-start.2) | copy-done | bytes 131096
  2.8 0.0 copy-done.7
  2.8 0.0 copy-done.8
  2.8 0.0 copy-done.9
  2.8 0.0 copy-start.1
  2.8 0.0 copy-start.3
  2.8 0.0 copy-start.4
  2.8 0.0 copy-start.5
  2.8 0.0 copy-start.6
  2.8 0.0 copy-start.10
  2.8 0.0 copy-start.11
  2.9 0.0 copy-start.12
  2.9 0.0 copy-start.13
  2.9 0.0 copy-start.14
  2.9 0.0 copy-start.15
  2.9 0.0 copy-start.16
  2.9 1.0 %shard_map.155 = (bf16[4,96,128]{2,1,0:T(8,128)(2,1)S(1)}, bf16[3,96,128]{2,1,0:T(8,128)(2,1)S(1)}, bf16[3,96,128]{2,1,0:T(8,128)(2,1)S(1)}, bf16[96,16,128]{2,1,0:T(8,128)(2,1)S(1)}, bf16[96,16,128]{2,1,0:T(8,128)(2,1)S(1)}) custom-call(bf16[512,128]{1,0:T(8,128)(2,1)S(1)} %bitcast.16, bf16[512,128]{1,0:T(8,128)(2,1)S(1)} %collective-permute-done.mate, ...), custom_call_target="tpu_custom_call" | custom-call | flops 1650000000 | bytes 1000 | tf_op jit(solution)/shard_map/pallas_call | solution.py:422
  4.0 2.6 %collective-permute-start.3 = (bf16[3,96,128]{2,1,0:T(8,128)(2,1)S(1)}, bf16[3,96,128]{2,1,0:T(8,128)(2,1)S(1)}, u32[]{:S(2)}, u32[]{:S(2)}) collective-permute-start(bf16[3,96,128]{2,1,0:T(8,128)(2,1)S(1)} %get-tuple-element.28), channel_id=1, source_target_pairs={{0,2},{2,0},{4,6},{6,4},{8,10},{10,8},{12,14},{14,12},{1,3},{3,1},... | collective-permute-start | bytes 221192 | tf_op jit(solution)/shard_map/ppermute | solution.py:442
  6.5 0.7 %collective-permute-start.4 = (bf16[3,96,128]{2,1,0:T(8,128)(2,1)S(1)}, bf16[3,96,128]{2,1,0:T(8,128)(2,1)S(1)}, u32[]{:S(2)}, u32[]{:S(2)}) collective-permute-start(bf16[3,96,128]{2,1,0:T(8,128)(2,1)S(1)} %get-tuple-element.29), channel_id=1, source_target_pairs={{2,4},{4,2},{6,8},{8,6},{10,12},{12,10},{3,5},{5,3},{7,9},{9,7},{1... | collective-permute-start | bytes 221192 | tf_op jit(solution)/shard_map/ppermute | solution.py:442
  7.2 4.3 %collective-permute-start.1 = (bf16[96,16,128]{2,1,0:T(8,128)(2,1)S(1)}, bf16[96,16,128]{2,1,0:T(8,128)(2,1)S(1)}, u32[]{:S(2)}, u32[]{:S(2)}) collective-permute-start(bf16[96,16,128]{2,1,0:T(8,128)(2,1)S(1)} %get-tuple-element.25), channel_id=1, source_target_pairs={{0,2},{2,0},{4,6},{6,4},{8,10},{10,8},{12,14},{14,12},{1,3},{3,1},... | collective-permute-start | bytes 1179656 | tf_op jit(solution)/shard_map/ppermute | solution.py:442
  11.5 0.7 %collective-permute-start.2 = (bf16[96,16,128]{2,1,0:T(8,128)(2,1)S(1)}, bf16[96,16,128]{2,1,0:T(8,128)(2,1)S(1)}, u32[]{:S(2)}, u32[]{:S(2)}) collective-permute-start(bf16[96,16,128]{2,1,0:T(8,128)(2,1)S(1)} %get-tuple-element.26), channel_id=1, source_target_pairs={{2,4},{4,2},{6,8},{8,6},{10,12},{12,10},{3,5},{5,3},{7,9},{9,7},{1... | collective-permute-start | bytes 1179656 | tf_op jit(solution)/shard_map/ppermute | solution.py:442
  12.2 0.0 collective-permute-done.3.even
  12.2 0.0 collective-permute-done.4.odd
  12.2 0.0 copy-done.1
  12.2 0.0 copy-done.3
  12.2 0.0 copy-done.4
  12.3 0.0 copy-done.5
  12.3 0.0 copy-done.6
  12.3 0.0 copy-done.10
  12.3 0.0 copy-done.11
  12.3 0.0 copy-done.12
  12.3 0.0 copy-done.13
  12.3 0.0 copy-done.14
  12.3 0.0 copy-done.15
  12.3 0.0 copy-done.16
  12.3 8.6 %shard_map.156 = (f32[2,96,16,128]{3,2,1,0:T(8,128)S(1)}, f32[2,96,16,128]{3,2,1,0:T(8,128)S(1)}, f32[4,96,128]{2,1,0:T(8,128)S(1)}, bf16[2,672,256]{2,1,0:T(8,128)(2,1)S(1)}, bf16[2,432,256]{2,1,0:T(8,128)(2,1)S(1)}) custom-call(bf16[4,96,128]{2,1,0:T(8,128)(2,1)S(1)} %get-tuple-element.27.corr, bf16[3,96,128]{2,1,0:T(8,128)(2,1)S(1)} %collective-permute-done.3.even, ...), custom_call_target="tpu_custom_call" | custom-call | flops 8800000000 | bytes 1000 | tf_op jit(solution)/shard_map/pallas_call | solution.py:422
  20.9 0.0 collective-permute-done.2.carried
  20.9 1.3 %shard_map.157 = (f32[384,128]{1,0:T(8,128)S(1)}, f32[104,128]{1,0:T(8,128)S(1)}, f32[96,16,128]{2,1,0:T(8,128)S(1)}, f32[96,16,128]{2,1,0:T(8,128)S(1)}) custom-call(bf16[96,16,128]{2,1,0:T(8,128)(2,1)S(1)} %collective-permute-done.2.carried, f32[4,96,128]{2,1,0:T(8,128)S(1)} %get-tuple-element.30.main_in, f32[2,96,16,128]{3,2,1,0:T(8,128)S(1)} %get-tuple-element.31.pre2, ...), custom_call_target="tpu_custom_call" | custom-call | flops 2200000000 | bytes 1000 | tf_op jit(solution)/shard_map/pallas_call | solution.py:422
  22.2 0.7 %collective-permute-start.5 = (f32[104,128]{1,0:T(8,128)S(1)}, f32[104,128]{1,0:T(8,128)S(1)}, u32[]{:S(2)}, u32[]{:S(2)}) collective-permute-start(f32[104,128]{1,0:T(8,128)S(1)} %get-tuple-element.39), channel_id=1, source_target_pairs={{2,4},{4,2},{6,8},{8,6},{10,12},{12,10},{3,5},{5,3},{7,9},{9,7},{1... | collective-permute-start | bytes 159752 | tf_op jit(solution)/shard_map/ppermute | solution.py:442
  22.9 5.6 %collective-permute-done.1.carried = bf16[96,16,128]{2,1,0:T(8,128)(2,1)S(1)} collective-permute-done((bf16[96,16,128]{2,1,0:T(8,128)(2,1)S(1)}, bf16[96,16,128]{2,1,0:T(8,128)(2,1)S(1)}, u32[]{:S(2)}, u32[]{:S(2)}) %collective-permute-start.1) | collective-permute-done | bytes 393248 | tf_op jit(solution)/shard_map/ppermute | solution.py:442
  28.5 1.1 %shard_map.158 = (f32[384,128]{1,0:T(8,128)S(1)}, f32[96,128]{1,0:T(8,128)S(1)}) custom-call(bf16[96,16,128]{2,1,0:T(8,128)(2,1)S(1)} %collective-permute-done.1.carried, f32[384,128]{1,0:T(8,128)S(1)} %get-tuple-element.35.main_in, f32[96,16,128]{2,1,0:T(8,128)S(1)} %get-tuple-element.36.pre2, f32[96,16,128]{2,1,0:T(8,128)S(1)} %get-tuple-element.37.pre3, ...), custom_call_target="tpu_custom_call" | custom-call | flops 2200000000 | bytes 1000 | tf_op jit(solution)/shard_map/pallas_call | solution.py:422
  29.6 2.9 %collective-permute-start.6 = (f32[96,128]{1,0:T(8,128)S(1)}, f32[96,128]{1,0:T(8,128)S(1)}, u32[]{:S(2)}, u32[]{:S(2)}) collective-permute-start(f32[96,128]{1,0:T(8,128)S(1)} %get-tuple-element.40), channel_id=1, source_target_pairs={{0,2},{2,0},{4,6},{6,4},{8,10},{10,8},{12,14},{14,12},{1,3},{3,1},... | collective-permute-start | bytes 147464 | tf_op jit(solution)/shard_map/ppermute | solution.py:442
  32.5 2.1 %collective-permute-done.6.even = f32[96,128]{1,0:T(8,128)S(1)} collective-permute-done((f32[96,128]{1,0:T(8,128)S(1)}, f32[96,128]{1,0:T(8,128)S(1)}, u32[]{:S(2)}, u32[]{:S(2)}) %collective-permute-start.6) | collective-permute-done | bytes 49184 | tf_op jit(solution)/shard_map/ppermute | solution.py:442
  34.6 0.0 collective-permute-done.5.odd
  34.6 0.7 %shard_map.159 = f32[384,128]{1,0:T(8,128)} custom-call(f32[384,128]{1,0:T(8,128)S(1)} %get-tuple-element.38.main, f32[104,128]{1,0:T(8,128)S(1)} %collective-permute-done.5.odd, f32[96,128]{1,0:T(8,128)S(1)} %collective-permute-done.6.even), custom_call_target="tpu_custom_call" | custom-call | flops 110000000 | bytes 1000 | tf_op jit(solution)/shard_map/pallas_call | solution.py:422
Async XLA Ops:
  0.0 2.3 %collective-permute-start = (bf16[512,128]{1,0:T(8,128)(2,1)}, bf16[512,128]{1,0:T(8,128)(2,1)S(1)}, u32[]{:S(2)}, u32[]{:S(2)}) collective-permute-start(bf16[512,128]{1,0:T(8,128)(2,1)} %bitcast.15), channel_id=1, source_target_pairs={{0,1},{1,0},{2,3},{3,2},{4,5},{5,4},{6,7},{7,6},{8,9},{9,8},{10,11... | collective-permute-start | bytes 393224 | tf_op jit(solution)/shard_map/ppermute | solution.py:445
  0.5 1.4 %copy-start = (bf16[1,16,96,4,128]{4,3,2,1,0:T(4,128)(2,1)S(1)}, bf16[1,16,96,4,128]{4,3,2,1,0:T(4,128)(2,1)}, u32[]{:S(2)}) copy-start(bf16[1,16,96,4,128]{4,3,2,1,0:T(4,128)(2,1)} %param.20) | copy-start | bytes 4718596
  1.9 0.9 %copy-start.2 = (bf16[1,128,4,128]{3,2,1,0:T(4,128)(2,1)S(1)}, bf16[1,128,4,128]{3,2,1,0:T(4,128)(2,1)}, u32[]{:S(2)}) copy-start(bf16[1,128,4,128]{3,2,1,0:T(4,128)(2,1)} %param.16) | copy-start | bytes 393220
  1.9 0.9 %copy-start.7 = (s32[4,6]{1,0:T(4,128)S(1)}, s32[4,6]{1,0:T(4,128)}, u32[]{:S(2)}) copy-start(s32[4,6]{1,0:T(4,128)} %pattern.1) | copy-start | bytes 292
  1.9 0.9 %copy-start.8 = (s32[1,4,4]{2,1,0:T(4,128)S(1)}, s32[1,4,4]{2,1,0:T(4,128)}, u32[]{:S(2)}) copy-start(s32[1,4,4]{2,1,0:T(4,128)} %param.19) | copy-start | bytes 196
  1.9 0.9 %copy-start.9 = (s32[2]{0:T(128)S(1)}, s32[2]{0:T(128)}, u32[]{:S(2)}) copy-start(s32[2]{0:T(128)} %param.17) | copy-start | bytes 28
  2.8 9.4 %copy-start.1 = (bf16[1,16,96,4,128]{4,3,2,1,0:T(4,128)(2,1)S(1)}, bf16[1,16,96,4,128]{4,3,2,1,0:T(4,128)(2,1)}, u32[]{:S(2)}) copy-start(bf16[1,16,96,4,128]{4,3,2,1,0:T(4,128)(2,1)} %param.20) | copy-start | bytes 4718596
  2.8 9.5 %copy-start.3 = (bf16[27,16,16]{0,2,1:T(8,128)(2,1)S(1)}, bf16[27,16,16]{0,2,1:T(8,128)(2,1)}, u32[]{:S(2)}) copy-start(bf16[27,16,16]{0,2,1:T(8,128)(2,1)} %param.22) | copy-start | bytes 41476
  2.8 9.4 %copy-start.4 = (bf16[27,16,16]{0,2,1:T(8,128)(2,1)S(1)}, bf16[27,16,16]{0,2,1:T(8,128)(2,1)}, u32[]{:S(2)}) copy-start(bf16[27,16,16]{0,2,1:T(8,128)(2,1)} %param.23) | copy-start | bytes 41476
  2.8 9.4 %copy-start.5 = (bf16[27,16]{0,1:T(8,128)(2,1)S(1)}, bf16[27,16]{0,1:T(8,128)(2,1)}, u32[]{:S(2)}) copy-start(bf16[27,16]{0,1:T(8,128)(2,1)} %param.21) | copy-start | bytes 2596
  2.8 9.4 %copy-start.6 = (bf16[27,16]{0,1:T(8,128)(2,1)S(1)}, bf16[27,16]{0,1:T(8,128)(2,1)}, u32[]{:S(2)}) copy-start(bf16[27,16]{0,1:T(8,128)(2,1)} %param.24) | copy-start | bytes 2596
  2.8 9.4 %copy-start.10 = (bf16[2,432,432]{2,1,0:T(8,128)(2,1)S(1)}, bf16[2,432,432]{2,1,0:T(8,128)(2,1)}, u32[]{:S(2)}) copy-start(bf16[2,432,432]{2,1,0:T(8,128)(2,1)} %constant.20.clone.ie) | copy-start | bytes 2239492
  2.8 9.4 %copy-start.11 = (bf16[27,10752]{1,0:T(8,128)(2,1)S(1)}, bf16[27,10752]{1,0:T(8,128)(2,1)}, u32[]{:S(2)}) copy-start(bf16[27,10752]{1,0:T(8,128)(2,1)} %constant.15.clone.p1) | copy-start | bytes 1741828
  2.9 9.4 %copy-start.12 = (bf16[144,2048]{1,0:T(8,128)(2,1)S(1)}, bf16[144,2048]{1,0:T(8,128)(2,1)}, u32[]{:S(2)}) copy-start(bf16[144,2048]{1,0:T(8,128)(2,1)} %constant.17.clone.p3) | copy-start | bytes 1769476
  2.9 9.4 %copy-start.13 = (bf16[48,3584]{1,0:T(8,128)(2,1)S(1)}, bf16[48,3584]{1,0:T(8,128)(2,1)}, u32[]{:S(2)}) copy-start(bf16[48,3584]{1,0:T(8,128)(2,1)} %constant.18.clone.ph) | copy-start | bytes 1032196
  2.9 9.4 %copy-start.14 = (bf16[144,1024]{1,0:T(8,128)(2,1)S(1)}, bf16[144,1024]{1,0:T(8,128)(2,1)}, u32[]{:S(2)}) copy-start(bf16[144,1024]{1,0:T(8,128)(2,1)} %constant.16.clone.p2) | copy-start | bytes 884740
  2.9 9.4 %copy-start.15 = (bf16[240,432]{1,0:T(8,128)(2,1)S(1)}, bf16[240,432]{1,0:T(8,128)(2,1)}, u32[]{:S(2)}) copy-start(bf16[240,432]{1,0:T(8,128)(2,1)} %constant.19.clone.im) | copy-start | bytes 622084
  2.9 9.4 %copy-start.16 = (bf16[256,256]{1,0:T(8,128)(2,1)S(1)}, bf16[256,256]{1,0:T(8,128)(2,1)}, u32[]{:S(2)}) copy-start(bf16[256,256]{1,0:T(8,128)(2,1)} %constant.14.clone.pick) | copy-start | bytes 393220
  4.0 8.3 %collective-permute-start.3 = (bf16[3,96,128]{2,1,0:T(8,128)(2,1)S(1)}, bf16[3,96,128]{2,1,0:T(8,128)(2,1)S(1)}, u32[]{:S(2)}, u32[]{:S(2)}) collective-permute-start(bf16[3,96,128]{2,1,0:T(8,128)(2,1)S(1)} %get-tuple-element.28), channel_id=1, source_target_pairs={{0,2},{2,0},{4,6},{6,4},{8,10},{10,8},{12,14},{14,12},{1,3},{3,1},... | collective-permute-start | bytes 221192 | tf_op jit(solution)/shard_map/ppermute | solution.py:442
  6.5 5.7 %collective-permute-start.4 = (bf16[3,96,128]{2,1,0:T(8,128)(2,1)S(1)}, bf16[3,96,128]{2,1,0:T(8,128)(2,1)S(1)}, u32[]{:S(2)}, u32[]{:S(2)}) collective-permute-start(bf16[3,96,128]{2,1,0:T(8,128)(2,1)S(1)} %get-tuple-element.29), channel_id=1, source_target_pairs={{2,4},{4,2},{6,8},{8,6},{10,12},{12,10},{3,5},{5,3},{7,9},{9,7},{1... | collective-permute-start | bytes 221192 | tf_op jit(solution)/shard_map/ppermute | solution.py:442
  7.2 21.3 %collective-permute-start.1 = (bf16[96,16,128]{2,1,0:T(8,128)(2,1)S(1)}, bf16[96,16,128]{2,1,0:T(8,128)(2,1)S(1)}, u32[]{:S(2)}, u32[]{:S(2)}) collective-permute-start(bf16[96,16,128]{2,1,0:T(8,128)(2,1)S(1)} %get-tuple-element.25), channel_id=1, source_target_pairs={{0,2},{2,0},{4,6},{6,4},{8,10},{10,8},{12,14},{14,12},{1,3},{3,1},... | collective-permute-start | bytes 1179656 | tf_op jit(solution)/shard_map/ppermute | solution.py:442
  11.5 9.4 %collective-permute-start.2 = (bf16[96,16,128]{2,1,0:T(8,128)(2,1)S(1)}, bf16[96,16,128]{2,1,0:T(8,128)(2,1)S(1)}, u32[]{:S(2)}, u32[]{:S(2)}) collective-permute-start(bf16[96,16,128]{2,1,0:T(8,128)(2,1)S(1)} %get-tuple-element.26), channel_id=1, source_target_pairs={{2,4},{4,2},{6,8},{8,6},{10,12},{12,10},{3,5},{5,3},{7,9},{9,7},{1... | collective-permute-start | bytes 1179656 | tf_op jit(solution)/shard_map/ppermute | solution.py:442
  22.2 12.4 %collective-permute-start.5 = (f32[104,128]{1,0:T(8,128)S(1)}, f32[104,128]{1,0:T(8,128)S(1)}, u32[]{:S(2)}, u32[]{:S(2)}) collective-permute-start(f32[104,128]{1,0:T(8,128)S(1)} %get-tuple-element.39), channel_id=1, source_target_pairs={{2,4},{4,2},{6,8},{8,6},{10,12},{12,10},{3,5},{5,3},{7,9},{9,7},{1... | collective-permute-start | bytes 159752 | tf_op jit(solution)/shard_map/ppermute | solution.py:442
  29.6 5.0 %collective-permute-start.6 = (f32[96,128]{1,0:T(8,128)S(1)}, f32[96,128]{1,0:T(8,128)S(1)}, u32[]{:S(2)}, u32[]{:S(2)}) collective-permute-start(f32[96,128]{1,0:T(8,128)S(1)} %get-tuple-element.40), channel_id=1, source_target_pairs={{0,2},{2,0},{4,6},{6,4},{8,10},{10,8},{12,14},{14,12},{1,3},{3,1},... | collective-permute-start | bytes 147464 | tf_op jit(solution)/shard_map/ppermute | solution.py:442
